TPU v7x, 32 devices: a whole 2x2x4 slice. The times are simulated.
32 devices in a mesh: group: 2 (over core), seq: 16 (over z, y, x).
Axes of the slice: x: 2, y: 2, z: 4, core: 2. Of those that a mesh axis runs over, the one named last changes fastest.
Arguments:
- x_rows: float32 [8192, 512], P(('group', 'seq')), may hold values from -300 to 300
- seg_ids: int32 [8192], P(('group', 'seq')), may hold values from 0 to 5, as said below
- row_kind: int32 [8192], P(('group', 'seq')), may hold values from 0 to 2, as said below
- prompt: bfloat16 [128, 512], P(('group', 'seq')), may hold values from -5 to 5
- w_qkv: bfloat16 [2, 512, 1536], replicated, may hold values from -0.375 to 0.375
- w_out: bfloat16 [2, 512, 512], replicated, may hold values from -0.875 to 0.875
- w_up: bfloat16 [2, 512, 1024], replicated, may hold values from -0.25 to 0.25
- w_down: bfloat16 [2, 1024, 512], replicated, may hold values from -0.1875 to 0.1875
- ln_gain: float32 [2, 2, 512], replicated, may hold values from 0.25 to 1.75
- ln_bias: float32 [2, 2, 512], replicated, may hold values from -1.5 to 1.5
- d_out: float32 [8192, 512], P(('group', 'seq')), may hold values from -20 to 20
Outputs:
- out_rows: float32 [8192, 512], P(('group', 'seq'))
- grad_rows: float32 [8192, 512], P(('group', 'seq'))
- grad_prompt: float32 [128, 512], P(('group', 'seq'))
Inputs may be any that keep to these rules, and one draw needn't show every extreme that they name: `seg_ids`: each block of 4096 rows (one index of group, number g) holds three datasets in consecutive rows, numbered 3 g, 3 g + 1 and 3 g + 2; the middle one begins within the block's first 256 rows and ends within its last 256 rows. `row_kind`: padding rows are the last rows of each block of 4096 rows, inside its third dataset, one or more in every block. In the middle dataset of a block the context rows are exactly those whose position in the block is congruent modulo 8 to a residue of that block, the others are test rows; in the first and third datasets context and test rows are mixed.
All inputs are finite; a program needn't handle non-finite values.
Results may differ from a plain program's by a relative error of at most 0.03.
The roundings to bfloat16 on the way count: a program that leaves them out, or rounds other values in their place, can miss the bound.
Values may be sent and summed in bfloat16 or wider, within the bound.
A program may use at most 192 MiB of HBM per device.

v0:
```python
import math

import jax
import jax.numpy as jnp
from jax import lax
from jax.sharding import PartitionSpec as P

HEADS = 4
LAYERS = 2


epsilon = 1e-05
masked_score = -1e30
inverse_root_two = 0.7071067811865476
inverse_root_two_pi = 0.3989422804014327


def split_heads(array):
    return array.reshape(array.shape[0], HEADS, array.shape[1] // HEADS)


def merge_heads(array):
    return array.reshape(array.shape[0], array.shape[1] * array.shape[2])


def blocks_of(array, size):
    return array.reshape((array.shape[0] // size, size) + array.shape[1:])


def times_transpose(left, right):
    return lax.dot_general(
        left, right, (((1,), (1,)), ((), ())), preferred_element_type=jnp.float32
    )


def norm_forward(inputs, gain, shift):
    center = inputs - jnp.mean(inputs, axis=-1, keepdims=True)
    scale = lax.rsqrt(jnp.mean(center * center, axis=-1, keepdims=True) + epsilon)
    return center * scale * gain + shift


def norm_backward(inputs, gain, grad):
    center = inputs - jnp.mean(inputs, axis=-1, keepdims=True)
    scale = lax.rsqrt(jnp.mean(center * center, axis=-1, keepdims=True) + epsilon)
    normal = center * scale
    upstream = grad * gain
    return scale * (
        upstream
        - jnp.mean(upstream, axis=-1, keepdims=True)
        - normal * jnp.mean(upstream * normal, axis=-1, keepdims=True)
    )


def gelu_slope(inputs):
    return (
        0.5 * (1.0 + lax.erf(inputs * inverse_root_two))
        + inputs * jnp.exp(-0.5 * inputs * inputs) * inverse_root_two_pi
    )


def scores_of(queries, keys, allowed):
    raw = jnp.einsum(
        "rhe,khe->hrk", queries, keys, preferred_element_type=jnp.float32
    ) * queries.shape[2] ** (-0.5)
    return jnp.where(allowed[None], raw, masked_score)


def permits(query_label, key_label):
    return query_label[:, None] == key_label[None, :]


def key_block(count):
    return math.gcd(count, 2048)


def attention_forward(
    queries, query_label, prompt_keys, prompt_values, group_keys, group_values, key_label
):
    open_prompt = jnp.ones((queries.shape[0], prompt_keys.shape[0]), dtype=bool)
    first = scores_of(queries, prompt_keys, open_prompt)
    highest = jnp.max(first, axis=-1)
    totals = jnp.sum(jnp.exp(first - highest[..., None]), axis=-1)
    if group_keys.shape[0] > 0:
        size = key_block(group_keys.shape[0])
        key_blocks = blocks_of(group_keys, size)
        value_blocks = blocks_of(group_values, size)
        label_blocks = blocks_of(key_label, size)

        def gather_stats(carry, pieces):
            high_now, total_now = carry
            scores = scores_of(queries, pieces[0], permits(query_label, pieces[1]))
            high_next = jnp.maximum(high_now, jnp.max(scores, axis=-1))
            total_next = total_now * jnp.exp(high_now - high_next) + jnp.sum(
                jnp.exp(scores - high_next[..., None]), axis=-1
            )
            return ((high_next, total_next), None)

        (highest, totals), unused = lax.scan(
            gather_stats, (highest, totals), (key_blocks, label_blocks)
        )
    log_total = highest + jnp.log(totals)

    def weigh(scores):
        return jnp.exp(scores - log_total[..., None]).astype(jnp.bfloat16)

    mixed = jnp.einsum(
        "hrk,khe->rhe", weigh(first), prompt_values, preferred_element_type=jnp.float32
    )
    if group_keys.shape[0] > 0:

        def add_values(accum, pieces):
            scores = scores_of(queries, pieces[0], permits(query_label, pieces[2]))
            return (
                accum
                + jnp.einsum(
                    "hrk,khe->rhe", weigh(scores), pieces[1], preferred_element_type=jnp.float32
                ),
                None,
            )

        mixed, unused = lax.scan(add_values, mixed, (key_blocks, value_blocks, label_blocks))
    return (mixed, log_total)


def attention_backward(
    queries,
    query_label,
    prompt_keys,
    prompt_values,
    group_keys,
    group_values,
    key_label,
    log_total,
    grad_mixed,
    delta,
):
    scale = queries.shape[2] ** (-0.5)

    def one_block(keys, values, allowed):
        weights = jnp.exp(scores_of(queries, keys, allowed) - log_total[..., None])
        grad_weights = jnp.einsum(
            "rhe,khe->hrk", grad_mixed, values, preferred_element_type=jnp.float32
        )
        grad_scores = (weights * (grad_weights - delta[..., None])).astype(jnp.bfloat16)
        grad_queries = (
            jnp.einsum("hrk,khe->rhe", grad_scores, keys, preferred_element_type=jnp.float32)
            * scale
        )
        grad_values = jnp.einsum(
            "hrk,rhe->khe",
            weights.astype(jnp.bfloat16),
            grad_mixed,
            preferred_element_type=jnp.float32,
        )
        grad_keys = (
            jnp.einsum("hrk,rhe->khe", grad_scores, queries, preferred_element_type=jnp.float32)
            * scale
        )
        return (grad_queries, grad_keys, grad_values)

    open_prompt = jnp.ones((queries.shape[0], prompt_keys.shape[0]), dtype=bool)
    grad_queries, prompt_grad_keys, prompt_grad_values = one_block(
        prompt_keys, prompt_values, open_prompt
    )
    group_grads = None
    if group_keys.shape[0] > 0:
        size = key_block(group_keys.shape[0])

        def step(carry, pieces):
            block_queries, block_keys, block_values = one_block(
                pieces[0], pieces[1], permits(query_label, pieces[2])
            )
            return (carry + block_queries, (block_keys, block_values))

        grad_queries, stacked = lax.scan(
            step,
            grad_queries,
            (
                blocks_of(group_keys, size),
                blocks_of(group_values, size),
                blocks_of(key_label, size),
            ),
        )
        group_grads = (stacked[0].reshape(group_keys.shape), stacked[1].reshape(group_keys.shape))
    return (grad_queries, prompt_grad_keys, prompt_grad_values, group_grads)


def block_tail(inputs, mixed, out_weight, up_weight, down_weight, gain, shift):
    attended = jnp.dot(
        merge_heads(mixed).astype(jnp.bfloat16), out_weight, preferred_element_type=jnp.float32
    )
    first_sum = inputs + attended
    hidden = norm_forward(first_sum, gain[0], shift[0])
    expanded = jnp.dot(hidden.astype(jnp.bfloat16), up_weight, preferred_element_type=jnp.float32)
    activated = jax.nn.gelu(expanded, approximate=False).astype(jnp.bfloat16)
    second_sum = hidden + jnp.dot(activated, down_weight, preferred_element_type=jnp.float32)
    return (norm_forward(second_sum, gain[1], shift[1]), (first_sum, expanded, second_sum))


def tail_backward(grad_out, kept, out_weight, up_weight, down_weight, gain):
    first_sum, expanded, second_sum = kept
    grad_second = norm_backward(second_sum, gain[1], grad_out)
    grad_activated = times_transpose(grad_second.astype(jnp.bfloat16), down_weight)
    grad_expanded = (grad_activated * gelu_slope(expanded)).astype(jnp.bfloat16)
    grad_hidden = grad_second + times_transpose(grad_expanded, up_weight)
    grad_first = norm_backward(first_sum, gain[0], grad_hidden)
    grad_mixed = times_transpose(grad_first.astype(jnp.bfloat16), out_weight).astype(jnp.bfloat16)
    return (grad_first, split_heads(grad_mixed))


def head_delta(grad_mixed, mixed):
    return jnp.sum(grad_mixed.astype(jnp.float32) * mixed, axis=2).T


def per_device(
    x_rows, seg_ids, row_kind, prompt, w_qkv, w_out, w_up, w_down, ln_gain, ln_bias, d_out
):
    width = x_rows.shape[1]
    labels = lax.all_gather(jnp.stack([seg_ids, row_kind]), "seq", axis=1, tiled=True)
    key_label = jnp.where(labels[1] == 0, labels[0], -1)
    query_label = jnp.where(row_kind == 2, -2, seg_ids)
    prompt_label = jnp.zeros((prompt.shape[0],), jnp.int32)
    empty_keys = jnp.zeros((0, HEADS, width // HEADS), jnp.bfloat16)
    empty_label = jnp.zeros((0,), jnp.int32)
    usable = (row_kind != 2).astype(jnp.float32)[:, None]
    totals, squares, count = lax.psum(
        (
            jnp.sum(usable * x_rows, axis=0),
            jnp.sum(usable * x_rows * x_rows, axis=0),
            jnp.sum(usable),
        ),
        ("group", "seq"),
    )
    mean = totals / count
    second = squares / count
    spread = lax.rsqrt(second - mean * mean + epsilon)
    normed = (x_rows - mean) * spread
    rows = normed
    prompt_rows = prompt.astype(jnp.float32)
    saved = []
    for layer in range(LAYERS):
        full = layer + 1 < LAYERS
        weight = w_qkv[layer]
        projected = jnp.dot(
            rows.astype(jnp.bfloat16), weight, preferred_element_type=jnp.float32
        ).astype(jnp.bfloat16)
        if full:
            prompt_projected = jnp.dot(
                prompt_rows.astype(jnp.bfloat16), weight, preferred_element_type=jnp.float32
            ).astype(jnp.bfloat16)
            prompt_pair = prompt_projected[:, width:]
        else:
            prompt_pair = jnp.dot(
                prompt_rows.astype(jnp.bfloat16),
                weight[:, width:],
                preferred_element_type=jnp.float32,
            ).astype(jnp.bfloat16)
        prompt_keys, prompt_values = (
            lax.all_gather(prompt_pair[:, :width], ("group", "seq"), axis=0, tiled=True),
            lax.all_gather(prompt_pair[:, width:], ("group", "seq"), axis=0, tiled=True),
        )
        group_keys, group_values = (
            lax.all_gather(projected[:, width : 2 * width], "seq", axis=0, tiled=True),
            lax.all_gather(projected[:, 2 * width :], "seq", axis=0, tiled=True),
        )
        queries = split_heads(projected[:, :width])
        prompt_keys = split_heads(prompt_keys)
        prompt_values = split_heads(prompt_values)
        group_keys = split_heads(group_keys)
        group_values = split_heads(group_values)
        mixed, log_total = attention_forward(
            queries, query_label, prompt_keys, prompt_values, group_keys, group_values, key_label
        )
        rows_next, tail_kept = block_tail(
            rows, mixed, w_out[layer], w_up[layer], w_down[layer], ln_gain[layer], ln_bias[layer]
        )
        prompt_kept = None
        if full:
            prompt_queries = split_heads(prompt_projected[:, :width])
            prompt_mixed, prompt_total = attention_forward(
                prompt_queries,
                prompt_label,
                prompt_keys,
                prompt_values,
                empty_keys,
                empty_keys,
                empty_label,
            )
            prompt_next, prompt_tail = block_tail(
                prompt_rows,
                prompt_mixed,
                w_out[layer],
                w_up[layer],
                w_down[layer],
                ln_gain[layer],
                ln_bias[layer],
            )
            prompt_kept = (prompt_queries, prompt_mixed, prompt_total, prompt_tail)
            prompt_rows = prompt_next
        saved.append(
            (
                queries,
                mixed,
                log_total,
                prompt_keys,
                prompt_values,
                group_keys,
                group_values,
                tail_kept,
                projected,
                prompt_kept,
            )
        )
        rows = rows_next
    grad_rows = d_out
    grad_prompt_rows = jnp.zeros(prompt_rows.shape, jnp.float32)
    for layer in range(LAYERS - 1, -1, -1):
        (
            queries,
            mixed,
            log_total,
            prompt_keys,
            prompt_values,
            group_keys,
            group_values,
            tail_kept,
            projected,
            prompt_kept,
        ) = saved[layer]
        weight = w_qkv[layer]
        grad_first, grad_mixed = tail_backward(
            grad_rows, tail_kept, w_out[layer], w_up[layer], w_down[layer], ln_gain[layer]
        )
        delta = head_delta(grad_mixed, mixed)
        grad_queries, prompt_grad_keys, prompt_grad_values, group_grads = attention_backward(
            queries,
            query_label,
            prompt_keys,
            prompt_values,
            group_keys,
            group_values,
            key_label,
            log_total,
            grad_mixed,
            delta,
        )
        own_grad_keys, own_grad_values = (
            lax.psum_scatter(
                merge_heads(group_grads[0]).astype(jnp.bfloat16),
                "seq",
                scatter_dimension=0,
                tiled=True,
            ).astype(jnp.float32),
            lax.psum_scatter(
                merge_heads(group_grads[1]).astype(jnp.bfloat16),
                "seq",
                scatter_dimension=0,
                tiled=True,
            ).astype(jnp.float32),
        )
        if prompt_kept is not None:
            prompt_queries, prompt_mixed, prompt_total, prompt_tail = prompt_kept
            prompt_first, prompt_grad_mixed = tail_backward(
                grad_prompt_rows,
                prompt_tail,
                w_out[layer],
                w_up[layer],
                w_down[layer],
                ln_gain[layer],
            )
            prompt_delta = head_delta(prompt_grad_mixed, prompt_mixed)
            prompt_grad_queries, extra_keys, extra_values, nothing = attention_backward(
                prompt_queries,
                prompt_label,
                prompt_keys,
                prompt_values,
                empty_keys,
                empty_keys,
                empty_label,
                prompt_total,
                prompt_grad_mixed,
                prompt_delta,
            )
            prompt_grad_keys = prompt_grad_keys + extra_keys
            prompt_grad_values = prompt_grad_values + extra_values
        summed_keys, summed_values = (
            lax.psum_scatter(
                merge_heads(prompt_grad_keys), ("group", "seq"), scatter_dimension=0, tiled=True
            ),
            lax.psum_scatter(
                merge_heads(prompt_grad_values), ("group", "seq"), scatter_dimension=0, tiled=True
            ),
        )
        pair_grad = jnp.concatenate(
            [summed_keys.astype(jnp.bfloat16), summed_values.astype(jnp.bfloat16)], axis=1
        )
        grad_projected = jnp.concatenate(
            [
                merge_heads(grad_queries).astype(jnp.bfloat16),
                own_grad_keys.astype(jnp.bfloat16),
                own_grad_values.astype(jnp.bfloat16),
            ],
            axis=1,
        )
        grad_rows = grad_first + times_transpose(grad_projected, weight)
        if prompt_kept is not None:
            prompt_projected_grad = jnp.concatenate(
                [merge_heads(prompt_grad_queries).astype(jnp.bfloat16), pair_grad], axis=1
            )
            grad_prompt_rows = prompt_first + times_transpose(prompt_projected_grad, weight)
        else:
            grad_prompt_rows = times_transpose(pair_grad, weight[:, width:])
    grad_sum, grad_dot = lax.psum(
        (jnp.sum(grad_rows, axis=0), jnp.sum(grad_rows * normed, axis=0)), ("group", "seq")
    )
    grad_inputs = spread * (grad_rows - usable / count * (grad_sum + normed * grad_dot))
    return (rows, grad_inputs, grad_prompt_rows)


def solution(mesh):
    return jax.shard_map(
        per_device,
        mesh=mesh,
        in_specs=(
            P(("group", "seq"), None),
            P(("group", "seq")),
            P(("group", "seq")),
            P(("group", "seq"), None),
            P(),
            P(),
            P(),
            P(),
            P(),
            P(),
            P(("group", "seq"), None),
        ),
        out_specs=(P(("group", "seq"), None), P(("group", "seq"), None), P(("group", "seq"), None)),
        check_vma=False,
    )
```

profile of v0, /device:TPU:0, one launch (start us, length us, event | category | flops | bytes accessed | tf_op | source)
XLA Modules:
  0.0 1060.8 jit_solution(16519996613919139321)
XLA Ops:
  10.4 42.3 %all-reduce.6 = (f32[512]{0:T(512)S(1)}, f32[]{:T(128)}, f32[512]{0:T(512)S(1)}) all-reduce(f32[512]{0:T(512)S(1)} %get-tuple-element.576, f32[]{:T(128)} %convert_reduce_fusion, f32[512]{0:T(512)S(1)} %get-tuple-element.575), channel_id=1, replica_groups=mesh['group'=2,'seq'=16] {'group','seq'}, use_global_device_ids=true, to_apply=%region_5.6 | all-reduce | flops 1025 | bytes 8200 | tf_op jit(solution)/shard_map/psum | solution.py:226
  59.6 68.1 %all-gather.1 = bf16[32,4,512]{2,1,0:T(4,128)(2,1)S(1)} all-gather(bf16[1,4,512]{2,1,0:T(4,128)(2,1)S(1)} %get-tuple-element.717), channel_id=1, replica_groups=mesh['group'=2,'seq'=16] {'group','seq'}, dimensions={0}, use_global_device_ids=true | all-gather | bytes 135168 | tf_op jit(solution)/shard_map/all_gather | solution.py:259
  127.8 36.9 %all_gather.29 = s32[2,4096]{1,0:T(2,128)S(1)} all-gather(s32[2,256]{1,0:T(2,128)S(1)} %pad_add_fusion), channel_id=1, replica_groups=mesh['group'=2,'seq'=16] {'seq'}, dimensions={1}, use_global_device_ids=true | all-gather | bytes 34816 | tf_op jit(solution)/shard_map/all_gather | solution.py:219
  164.8 66.2 %all-gather = bf16[32,4,512]{2,1,0:T(4,128)(2,1)S(1)} all-gather(bf16[1,4,512]{2,1,0:T(4,128)(2,1)S(1)} %get-tuple-element.718), channel_id=1, replica_groups=mesh['group'=2,'seq'=16] {'group','seq'}, dimensions={0}, use_global_device_ids=true | all-gather | bytes 135168 | tf_op jit(solution)/shard_map/all_gather | solution.py:260
  232.8 6.9 reshape_reshape.8
  244.4 10.8 %while.72 = (s32[]{:T(128)}, f32[4,256]{1,0:T(4,128)S(1)}, f32[4,256]{1,0:T(4,128)S(1)}, s32[256]{0:T(256)S(1)}, s32[2,2048]{1,0:T(2,128)S(1)}, /*index=5*/bf16[...) while((s32[]{:T(128)}, f32[4,256]{1,0:T(4,128)S(1)}, f32[4,256]{1,0:T(4,128)S(1)}, ...), condition=%wide.region_11.12_spmd, body=%wide.region_8.11_spmd.sunk | while | flops 552077312 | bytes 20788824 | solution.py:98
  257.6 6.9 reshape_reshape.9
  264.5 22.2 %while.73 = (s32[]{:T(128)}, f32[256,4,128]{0,2,1:T(8,128)}, bf16[2,2048,4,128]{3,2,1,0:T(4,128)(2,1)}, s32[256]{0:T(256)S(1)}, s32[2,2048]{1,0:T(2,128)S(1)}, /...) while((s32[]{:T(128)}, f32[256,4,128]{0,2,1:T(8,128)}, ...), condition=%wide.region_13.14_spmd, body=%wide.region_12.13_spmd.sunk | while | flops 1082785792 | bytes 14980765 | solution.py:121
  303.2 67.0 %all-gather.3 = bf16[32,4,512]{2,1,0:T(4,128)(2,1)S(1)} all-gather(bf16[1,4,512]{2,1,0:T(4,128)(2,1)S(1)} %get-tuple-element.727), channel_id=1, replica_groups=mesh['group'=2,'seq'=16] {'group','seq'}, dimensions={0}, use_global_device_ids=true | all-gather | bytes 135168 | tf_op jit(solution)/shard_map/all_gather | solution.py:259
  370.4 65.2 %all-gather.2 = bf16[32,4,512]{2,1,0:T(4,128)(2,1)S(1)} all-gather(bf16[1,4,512]{2,1,0:T(4,128)(2,1)S(1)} %get-tuple-element.728), channel_id=1, replica_groups=mesh['group'=2,'seq'=16] {'group','seq'}, dimensions={0}, use_global_device_ids=true | all-gather | bytes 135168 | tf_op jit(solution)/shard_map/all_gather | solution.py:260
  436.3 7.0 reshape_reshape.10
  448.0 10.8 %while.74 = (s32[]{:T(128)}, f32[4,256]{1,0:T(4,128)S(1)}, f32[4,256]{1,0:T(4,128)S(1)}, s32[256]{0:T(256)S(1)}, s32[2,2048]{1,0:T(2,128)S(1)}, /*index=5*/bf16[...) while((s32[]{:T(128)}, f32[4,256]{1,0:T(4,128)S(1)}, f32[4,256]{1,0:T(4,128)S(1)}, ...), condition=%wide.region_29.30_spmd, body=%wide.region_26.29_spmd.sunk | while | flops 552077312 | bytes 20788824 | solution.py:98
  461.2 6.9 reshape_reshape.11
  468.1 22.2 %while.75 = (s32[]{:T(128)}, f32[256,4,128]{0,2,1:T(8,128)}, bf16[2,2048,4,128]{3,2,1,0:T(4,128)(2,1)}, s32[256]{0:T(256)S(1)}, s32[2,2048]{1,0:T(2,128)S(1)}, /...) while((s32[]{:T(128)}, f32[256,4,128]{0,2,1:T(8,128)}, ...), condition=%wide.region_31.32_spmd, body=%wide.region_30.31_spmd.sunk | while | flops 1082785792 | bytes 14980765 | solution.py:121
  473.3 5.9 fusion.698
  516.2 32.0 %while.76 = (s32[]{:T(128)}, f32[256,4,128]{0,2,1:T(8,128)S(1)}, bf16[2,2048,4,128]{3,1,2,0:T(8,128)(2,1)}, bf16[2,2048,4,128]{3,1,2,0:T(8,128)(2,1)}, bf16[2,20...) while((s32[]{:T(128)}, f32[256,4,128]{0,2,1:T(8,128)S(1)}, ...), condition=%wide.region_42.43_spmd, body=%wide.region_41.42_spmd.sunk | while | flops 2707161088 | bytes 127441144 | solution.py:175
  565.9 84.0 %reduce-scatter.7.cloned.1.call-done = bf16[256,512]{1,0:T(8,128)(2,1)} async-done(((bf16[4096,512]{1,0:T(8,128)(2,1)}), bf16[256,512]{1,0:T(8,128)(2,1)}) %reduce-scatter.7.cloned.1.call-update) | async-done | bytes 262160 | tf_op jit(solution)/shard_map/reduce_scatter | solution.py:348
  649.8 96.9 %reduce-scatter.9.cloned.1.call-done = bf16[256,512]{1,0:T(8,128)(2,1)} async-done(((bf16[4096,512]{1,0:T(8,128)(2,1)}), bf16[256,512]{1,0:T(8,128)(2,1)}) %reduce-scatter.9.cloned.1.call-update) | async-done | bytes 262160 | tf_op jit(solution)/shard_map/reduce_scatter | solution.py:354
  763.0 31.7 %while.77 = (s32[]{:T(128)}, f32[256,4,128]{0,2,1:T(8,128)S(1)}, bf16[2,2048,4,128]{3,1,2,0:T(8,128)(2,1)}, bf16[2,2048,4,128]{3,1,2,0:T(8,128)(2,1)}, bf16[2,20...) while((s32[]{:T(128)}, f32[256,4,128]{0,2,1:T(8,128)S(1)}, ...), condition=%wide.region_51.52_spmd, body=%wide.region_50.51_spmd.sunk | while | flops 2707161088 | bytes 128489752 | solution.py:175
  803.3 6.0 copy.310
  817.3 56.4 %all-reduce.9 = (bf16[128,512]{0,1:T(8,128)(2,1)S(1)}, bf16[128,512]{0,1:T(8,128)(2,1)S(1)}) all-reduce(f32[128,512]{0,1:T(8,128)} %bitcast.559, f32[128,512]{0,1:T(8,128)S(1)} %bitcast.555), channel_id=7, replica_groups=mesh['group'=2,'seq'=16] {'group','seq'}, use_global_device_ids=true, to_apply=%region_59.60.clone | all-reduce | flops 131072 | bytes 786432
  889.8 14.1 %reduce-scatter.11.cloned.1.call-done = bf16[256,512]{1,0:T(8,128)(2,1)} async-done(((bf16[4096,512]{1,0:T(8,128)(2,1)}), bf16[256,512]{1,0:T(8,128)(2,1)}) %reduce-scatter.11.cloned.1.call-update) | async-done | bytes 262160 | tf_op jit(solution)/shard_map/reduce_scatter | solution.py:348
  904.0 96.9 %reduce-scatter.13.cloned.1.call-done = bf16[256,512]{1,0:T(8,128)(2,1)} async-done(((bf16[4096,512]{1,0:T(8,128)(2,1)}), bf16[256,512]{1,0:T(8,128)(2,1)}) %reduce-scatter.13.cloned.1.call-update) | async-done | bytes 262160 | tf_op jit(solution)/shard_map/reduce_scatter | solution.py:354
  1003.2 46.7 %all-reduce.10 = (f32[512]{0:T(512)S(1)}, f32[512]{0:T(512)S(1)}, bf16[128,512]{1,0:T(8,128)(2,1)S(1)}, bf16[128,512]{1,0:T(8,128)(2,1)S(1)}) all-reduce(f32[512]{0:T(512)S(1)} %get-tuple-element.578, f32[512]{0:T(512)S(1)} %get-tuple-element.577, f32[128,512]{1,0:T(8,128)S(1)} %copy.325, ...), channel_id=1, replica_groups=mesh['group'=2,'seq'=16] {'group','seq'}, use_global_device_ids=true, to_apply=%region_57.58 | all-reduce | flops 132096 | bytes 794624 | tf_op jit(solution)/shard_map/psum | solution.py:413
  (523 shorter events, 262.4 us)
Async XLA Ops:
  7.2 225.6 %all-gather.9.cloned.1.call-start = ((), (), s32[]{:S(2)}) async-start(), calls=%async_computation.4 | async-start | bytes 4456448 | tf_op jit(solution)/shard_map/all_gather | solution.py:263
  53.4 178.1 %copy-start.100 = (f32[2,2,512]{2,1,0:T(2,128)S(1)}, f32[2,2,512]{2,1,0:T(2,128)}, u32[]{:S(2)}) copy-start(f32[2,2,512]{2,1,0:T(2,128)} %param.31) | copy-start | bytes 24580
  53.4 178.8 %copy-start.101 = (f32[2,2,512]{2,1,0:T(2,128)S(1)}, f32[2,2,512]{2,1,0:T(2,128)}, u32[]{:S(2)}) copy-start(f32[2,2,512]{2,1,0:T(2,128)} %param.32) | copy-start | bytes 24580
  56.4 183.3 %copy-start.26 = (bf16[32,4,8,128]{3,2,1,0:T(8,128)(2,1)}, bf16[32,4,8,128]{3,2,1,0:T(8,128)(2,1)S(1)}, u32[]{:S(2)}) copy-start(bf16[32,4,8,128]{3,2,1,0:T(8,128)(2,1)S(1)} %get-tuple-element.715) | copy-start | bytes 786436
  56.5 201.1 %all-gather.11.cloned.1.call-start = ((), (), s32[]{:S(2)}) async-start(), calls=%async_computation.5 | async-start | bytes 4456448 | tf_op jit(solution)/shard_map/all_gather | solution.py:264
  57.2 379.1 %all-gather.13.cloned.1.call-start = ((), (), s32[]{:S(2)}) async-start(), calls=%async_computation.6 | async-start | bytes 4456448 | tf_op jit(solution)/shard_map/all_gather | solution.py:263
  296.9 164.4 %all-gather.15.cloned.1.call-start = ((), (), s32[]{:S(2)}) async-start(), calls=%async_computation.7 | async-start | bytes 4456448 | tf_op jit(solution)/shard_map/all_gather | solution.py:264
  298.8 351.1 %reduce-scatter.7.cloned.1.call-start = ((), (), s32[]{:S(2)}) async-start(), calls=%async_computation.8 | async-start | bytes 4456448 | tf_op jit(solution)/shard_map/reduce_scatter | solution.py:348
  556.8 190.0 %reduce-scatter.9.cloned.1.call-start = ((), (), s32[]{:S(2)}) async-start(), calls=%async_computation.9 | async-start | bytes 4456448 | tf_op jit(solution)/shard_map/reduce_scatter | solution.py:354
  565.3 181.5 %copy-start.53 = (f32[256,512]{1,0:T(8,128)S(1)}, f32[256,512]{1,0:T(8,128)}, u32[]{:S(2)}) copy-start(f32[256,512]{1,0:T(8,128)} %get-tuple-element.749) | copy-start | bytes 1572868
  565.3 181.5 %copy-start.55 = (f32[256,512]{1,0:T(8,128)S(1)}, f32[256,512]{1,0:T(8,128)}, u32[]{:S(2)}) copy-start(f32[256,512]{1,0:T(8,128)} %copy-done.54) | copy-start | bytes 1572868
  565.3 181.5 %copy-start.77 = (f32[256]{0:T(256)S(1)}, f32[256]{0:T(256)}, u32[]{:S(2)}) copy-start(f32[256]{0:T(256)} %copy-done.76) | copy-start | bytes 3076
  565.3 181.5 %copy-start.89 = (f32[256]{0:T(256)S(1)}, f32[256]{0:T(256)}, u32[]{:S(2)}) copy-start(f32[256]{0:T(256)} %copy-done.88) | copy-start | bytes 3076
  565.3 181.5 %copy-start.95 = (f32[1,1,512]{2,1,0:T(1,128)S(1)}, f32[1,1,512]{2,1,0:T(1,128)}, u32[]{:S(2)}) copy-start(f32[1,1,512]{2,1,0:T(1,128)} %get-tuple-element.720) | copy-start | bytes 6148
  565.3 181.5 %copy-start.109 = (f32[256]{0:T(256)S(1)}, f32[256]{0:T(256)}, u32[]{:S(2)}) copy-start(f32[256]{0:T(256)} %copy-done.108) | copy-start | bytes 3076
  565.3 181.5 %copy-start.111 = (f32[256]{0:T(256)S(1)}, f32[256]{0:T(256)}, u32[]{:S(2)}) copy-start(f32[256]{0:T(256)} %copy-done.110) | copy-start | bytes 3076
  565.4 181.5 %copy-start.113 = (f32[256]{0:T(256)S(1)}, f32[256]{0:T(256)}, u32[]{:S(2)}) copy-start(f32[256]{0:T(256)} %copy-done.112) | copy-start | bytes 3076
  565.4 181.5 %copy-start.121 = (f32[256]{0:T(256)S(1)}, f32[256]{0:T(256)}, u32[]{:S(2)}) copy-start(f32[256]{0:T(256)} %copy-done.120) | copy-start | bytes 3076
  565.4 183.8 %copy-start.15 = (f32[256,512]{1,0:T(8,128)S(1)}, f32[256,512]{1,0:T(8,128)}, u32[]{:S(2)}) copy-start(f32[256,512]{1,0:T(8,128)} %copy-done.14) | copy-start | bytes 1572868
  565.4 183.8 %copy-start.69 = (f32[1,1,512]{2,1,0:T(1,128)S(1)}, f32[1,1,512]{2,1,0:T(1,128)}, u32[]{:S(2)}) copy-start(f32[1,1,512]{2,1,0:T(1,128)} %get-tuple-element.721) | copy-start | bytes 6148
  565.4 183.8 %copy-start.73 = (f32[256]{0:T(256)S(1)}, f32[256]{0:T(256)}, u32[]{:S(2)}) copy-start(f32[256]{0:T(256)} %copy-done.72) | copy-start | bytes 3076
  565.4 183.8 %copy-start.85 = (f32[256]{0:T(256)S(1)}, f32[256]{0:T(256)}, u32[]{:S(2)}) copy-start(f32[256]{0:T(256)} %copy-done.84) | copy-start | bytes 3076
  565.4 338.5 %reduce-scatter.11.cloned.1.call-start = ((), (), s32[]{:S(2)}) async-start(), calls=%async_computation.10 | async-start | bytes 4456448 | tf_op jit(solution)/shard_map/reduce_scatter | solution.py:348
  803.2 197.6 %reduce-scatter.13.cloned.1.call-start = ((), (), s32[]{:S(2)}) async-start(), calls=%async_computation.11 | async-start | bytes 4456448 | tf_op jit(solution)/shard_map/reduce_scatter | solution.py:354
  (129 other events, 4122.6 us)
Sparse Core Ops, SparseCore 0:
  56.6 76.6 all-gather.8
  136.6 75.7 all-gather.10
  297.0 74.4 all-gather.12
  374.7 74.8 all-gather.14
  556.9 92.8 reduce-scatter.6
  652.0 94.7 reduce-scatter.8
  803.4 100.5 reduce-scatter.10
  906.2 94.5 reduce-scatter.12
where the time goes:
time: 1070 us; the launch traced here: 1060 us
  blocking collectives  449 us (42%)
  waiting for transfers between devices  293 us (27%)
  matrix products  152 us (14%)
  local copies, waits for them, and re-layouts  118 us (11%)
  other arithmetic  30.8 us (3%)
  between operations  17.1 us (2%)
    reduce_scatter x2, waiting for transfers between devices, per_device(): lax.psum_scatter(merge_heads(group_grads[1]).astype(jnp.bfloat16), 'seq',...  194 us
    all_gather x2, blocking collectives, per_device(): lax.all_gather(prompt_pair[:, :width], ('group', 'seq'), axis=0, tiled=True)  135 us
    all_gather x2, blocking collectives, per_device(): lax.all_gather(prompt_pair[:, width:], ('group', 'seq'), axis=0, tiled=True)  131 us
    reduce_scatter x2, waiting for transfers between devices, per_device(): lax.psum_scatter(merge_heads(group_grads[0]).astype(jnp.bfloat16), 'seq',...  98.1 us
    unnamed x1, blocking collectives  56.4 us
    psum x1, blocking collectives, per_device(): lax.psum((jnp.sum(grad_rows, axis=0), jnp.sum(grad_rows * normed, axis=0)...  46.7 us
    psum x1, blocking collectives, per_device(): lax.psum((jnp.sum(usable * x_rows, axis=0), jnp.sum(usable * x_rows * x_r...  42.3 us
    all_gather x1, blocking collectives, per_device(): lax.all_gather(jnp.stack([seg_ids, row_kind]), 'seq', axis=1, tiled=True)  36.9 us
  transfers between devices with their start and end apart: 8, of which 4 were waited for; matrix products, arithmetic and copies ran while one was open for 9% of the time, Pallas kernels for 0%

commit v1 on v0

v1 whole, which is shorter than its diff:
```python
import functools

import jax
import jax.numpy as jnp
from jax import lax
from jax.experimental import pallas as pl
from jax.experimental.pallas import tpu as pltpu
from jax.sharding import PartitionSpec as P

MESH = pl.DeviceIdType.MESH
def seq_dims(n):
    return {16:(4,2,2),32:(2,4,4)}.get(n,(n,1,1))

class Net:
    def __init__(self, groups, seq):
        self.G=groups; self.dims=seq_dims(seq)
        Z,Y,X=self.dims
        self.g=lax.axis_index("group"); s=lax.axis_index("seq")
        self.z=s//(Y*X); self.y=(s//X)%Y; self.x=s%X
    def dev(self,z=None,y=None,x=None,g=None):
        Z,Y,X=self.dims
        z=self.z if z is None else z; y=self.y if y is None else y; x=self.x if x is None else x; g=self.g if g is None else g
        return (g,(z*Y+y)*X+x)


def prepare(group, x, segs, kinds, prompt_rows, ctx_in, small_in, prompt_in):
    own,width=x.shape; lanes=width//128
    middle=3*group+1
    eye=lax.broadcasted_iota(jnp.int32,(own,own),0)==lax.broadcasted_iota(jnp.int32,(own,own),1)
    kind=kinds[...]
    def column(flag): return jnp.max(jnp.where(eye&flag,1.0,0.0),axis=1,keepdims=True)
    usable=column(kind!=2)
    chosen=column((kind==0)&(segs[...]==middle))
    rows=x[...]
    picked=jnp.sum((rows*chosen).reshape(own//8,8,width),axis=1)
    held=jnp.sum(jnp.broadcast_to(chosen,(own,width)).reshape(own//8,8,width),axis=1)
    ctx_in[...]=jnp.where(held>0.5,picked,absent)
    weighed=rows*usable
    total=jnp.sum(weighed,axis=0,keepdims=True); square=jnp.sum(weighed*rows,axis=0,keepdims=True)
    small_in[0:lanes]=narrow(total); small_in[lanes:2*lanes]=narrow(square)
    small_in[2*lanes:4*lanes]=jnp.broadcast_to(jnp.sum(usable),(2*lanes,128))
    prompt_in[...]=narrow(prompt_rows[...].astype(f32)).astype(bf16)

def narrow(rows):
    return jnp.concatenate([rows[:,i:i+128] for i in range(0,rows.shape[1],128)],axis=0)

def gather_kernel(groups, seq, x, segs, kinds, prompt_rows, ctx, small, prompt, ctx_in, small_in, prompt_in, zsmall, zs, zr, ps, pr, cs, cr, ls):
    net=Net(groups,seq); Z,Y,X=net.dims; G=groups
    half=ctx.shape[-1]//2
    C=ctx_in.shape[0]
    bar=pltpu.get_barrier_semaphore()
    zpeers=[(lambda d=d: (net.z+d)%Z)() for d in range(1,Z)]
    zback=[(net.z+Z-d)%Z for d in range(1,Z)]
    for zp in zpeers: pl.semaphore_signal(bar,inc=1,device_id=net.dev(z=zp),device_id_type=MESH)
    plane=[]
    N=G*Y*X
    p=(net.g*Y+net.y)*X+net.x
    for d in range(1,N):
        def who(q):
            return dict(g=q//(Y*X),y=(q//X)%Y,x=q%X)
        plane.append((who((p+d)%N),who((p+N-d)%N)))
    for to,fr in plane: pl.semaphore_signal(bar,inc=1,device_id=net.dev(**to),device_id_type=MESH)
    pl.semaphore_wait(bar,Z-1+N-1)
    prepare(net.g,x,segs,kinds,prompt_rows,ctx_in,small_in,prompt_in)
    pending=[]
    def remote(src,dst,s,r,dev):
        c=pltpu.make_async_remote_copy(src_ref=src,dst_ref=dst,send_sem=s,recv_sem=r,device_id=dev,device_id_type=MESH)
        c.start(); pending.append(c); return c
    def arrived(dst,s,r,dev):
        pltpu.make_async_remote_copy(src_ref=dst,dst_ref=dst,send_sem=s,recv_sem=r,device_id=dev,device_id_type=MESH).wait_recv()
    own=ctx.at[net.z,net.y,net.x]
    l0=pltpu.make_async_copy(ctx_in,own,ls.at[0]); l0.start()
    l1=pltpu.make_async_copy(small_in,zsmall.at[net.z],ls.at[1]); l1.start()
    l2=pltpu.make_async_copy(prompt_in,prompt.at[net.g,net.y,net.x,net.z],ls.at[2]); l2.start()
    for i,zp in enumerate(zpeers):
        dev=net.dev(z=zp)
        remote(small_in,zsmall.at[net.z],zs.at[0,i],zr.at[0,i],dev)
        remote(prompt_in,prompt.at[net.g,net.y,net.x,net.z],zs.at[1,i],zr.at[1,i],dev)
    for h in range(2):
        for i,zp in enumerate(zpeers):
            remote(ctx_in.at[:,pl.ds(h*half,half)],ctx.at[net.z,net.y,net.x,:,pl.ds(h*half,half)],zs.at[2+h,i],zr.at[2+h,i],net.dev(z=zp))
    l0.wait(); l1.wait(); l2.wait()
    for i,zp in enumerate(zback):
        arrived(zsmall.at[zp],zs.at[0,i],zr.at[0,i],net.dev(z=zp))
    tot=zsmall[0]
    for z in range(1,Z): tot=tot+zsmall[z]
    small[net.g,net.y,net.x]=tot
    for i,zp in enumerate(zback):
        arrived(prompt.at[net.g,net.y,net.x,zp],zs.at[1,i],zr.at[1,i],net.dev(z=zp))
    for i,(to,fr) in enumerate(plane):
        dev=net.dev(**to)
        mine=small.at[net.g,net.y,net.x]
        remote(mine,mine,ps.at[0,i],pr.at[0,i],dev)
        mine=prompt.at[net.g,net.y,net.x]
        remote(mine,mine,ps.at[1,i],pr.at[1,i],dev)
    H=lambda h: pl.ds(h*half,half)
    first=[("x",X,net.x),("y",Y,net.y)]
    for h,(dim,size,at) in enumerate(first):
        for i,zp in enumerate(zback):
            arrived(ctx.at[zp,net.y,net.x,:,H(h)],zs.at[2+h,i],zr.at[2+h,i],net.dev(z=zp))
        mine=ctx.at[:,net.y,net.x,:,H(h)]
        for d in range(1,size):
            remote(mine,mine,cs.at[0,h,d-1],cr.at[0,h,d-1],net.dev(**{dim:(at+d)%size}))
    for h,(dim,size,at) in enumerate(first):
        for d in range(1,size):
            q=(at+size-d)%size
            view=ctx.at[:,net.y,q,:,H(h)] if dim=="x" else ctx.at[:,q,net.x,:,H(h)]
            arrived(view,cs.at[0,h,d-1],cr.at[0,h,d-1],net.dev(**{dim:q}))
        dim2,size2,at2=first[1-h]
        mine=ctx.at[:,net.y,:,:,H(h)] if dim2=="y" else ctx.at[:,:,net.x,:,H(h)]
        for d in range(1,size2):
            remote(mine,mine,cs.at[1,h,d-1],cr.at[1,h,d-1],net.dev(**{dim2:(at2+d)%size2}))
    for i,(to,fr) in enumerate(plane):
        dev=net.dev(**fr)
        arrived(small.at[fr["g"],fr["y"],fr["x"]],ps.at[0,i],pr.at[0,i],dev)
        arrived(prompt.at[fr["g"],fr["y"],fr["x"]],ps.at[1,i],pr.at[1,i],dev)
    for h in range(2):
        dim2,size2,at2=first[1-h]
        for d in range(1,size2):
            q=(at2+size2-d)%size2
            view=ctx.at[:,q,:,:,H(h)] if dim2=="y" else ctx.at[:,:,q,:,H(h)]
            arrived(view,cs.at[1,h,d-1],cr.at[1,h,d-1],net.dev(**{dim2:q}))
    for c in pending: c.wait_send()


def gather(x,segs,kinds,prompt_rows,groups,seq):
    Z,Y,X=seq_dims(seq); own,D=x.shape; C=own//8; N=groups*Y*X; M=max(X,Y,2); L=D//128
    small=(4*L,128); pshape=(prompt_rows.shape[0]*L,128)
    DMA=pltpu.SemaphoreType.DMA
    vm=pl.BlockSpec(memory_space=pltpu.VMEM)
    return pl.pallas_call(
        functools.partial(gather_kernel,groups,seq),
        out_shape=(jax.ShapeDtypeStruct((Z,Y,X,C,D),f32),jax.ShapeDtypeStruct((groups,Y,X)+small,f32),jax.ShapeDtypeStruct((groups,Y,X,Z)+pshape,bf16)),
        in_specs=[vm]*4,out_specs=(vm,)*3,
        scratch_shapes=[pltpu.VMEM((C,D),f32),pltpu.VMEM(small,f32),pltpu.VMEM(pshape,bf16),pltpu.VMEM((Z,)+small,f32),DMA((4,Z)),DMA((4,Z)),DMA((2,N)),DMA((2,N)),DMA((2,2,M)),DMA((2,2,M)),DMA((3,))],
        compiler_params=pltpu.CompilerParams(collective_id=0,has_side_effects=True,vmem_limit_bytes=40*2**20),
        name="gather_context",
    )(x,segs,kinds,prompt_rows)


HEADS=4
epsilon = 1e-05
masked_score = -1e30
inverse_root_two = 0.7071067811865476
inverse_root_two_pi = 0.3989422804014327
absent = 1e9
f32=jnp.float32
bf16=jnp.bfloat16

def mm(a,b): return jnp.dot(a,b,preferred_element_type=f32)
def mm_t(a,b): return lax.dot_general(a,b,(((1,),(1,)),((),())),preferred_element_type=f32)
def t_mm(a,b): return lax.dot_general(a,b,(((0,),(0,)),((),())),preferred_element_type=f32)

def row_mean(a): return jnp.mean(a,axis=-1,keepdims=True)

def normalize(z):
    center=z-row_mean(z)
    scale=lax.rsqrt(row_mean(center*center)+epsilon)
    return center*scale,scale

def normalize_backward(normal,scale,gain,grad):
    upstream=grad*gain
    return scale*(upstream-row_mean(upstream)-normal*row_mean(upstream*normal))

def block_rows(count,most):
    return max(b for b in range(16,min(count,most)+1,16) if count%b==0)

def compute_kernel(
    x, segs, kinds, small, ctx, prompt, d_out, w_qkv, w_out, w_up, w_down, ln_gain, ln_bias,
    out_rows, g_ctx, g_prompt, g_own, sums, stats,
    X, X1, qkv, kv1, q1, mixed, mixed1, p_ctx, p_prompt, p_own, p_own1,
    n1, r1, slope, n2, r2, n1b, r1b, slopeb, n2b, r2b, first, gm, dq, dk, dv,
):
    own,width=x.shape
    C=ctx.shape[0]; Pn=prompt.shape[0]; K=C+Pn; R=K+own
    E=width//HEADS
    scale=E**-0.5
    group=lax.axis_index("group")
    middle=3*group+1
    total=small[0]
    for i in range(1,small.shape[0]): total=total+small[i]
    lanes=width//128
    def wide(block): return jnp.concatenate([block[i:i+1] for i in range(lanes)],axis=1)
    count=total[2*lanes:2*lanes+1,0:1]
    mean=wide(total[0:lanes])/count
    second=wide(total[lanes:2*lanes])/count
    spread=lax.rsqrt(second-mean*mean+epsilon)
    stats[0:1]=mean
    stats[1:2]=spread
    stats[2:3]=jnp.broadcast_to(count,(1,width))
    raw=ctx[...]
    held=jnp.abs(raw[:,0:1])<0.5*absent
    X[0:C]=jnp.where(held,(raw-mean)*spread,0.0)
    X[C:K]=prompt[...].astype(f32)
    X[K:R]=(x[...]-mean)*spread
    eye=lax.broadcasted_iota(jnp.int32,(own,own),0)==lax.broadcasted_iota(jnp.int32,(own,own),1)
    def column(lane): return jnp.max(jnp.where(eye,lane,-9),axis=1,keepdims=True)
    seg=segs[...]; kind=kinds[...]
    own_key=jnp.where((kind==0)&(seg!=middle),seg,-1)
    query=column(jnp.where(kind==2,-2,seg))
    ctx_key=jnp.concatenate([
        jnp.max(jnp.where((lax.broadcasted_iota(jnp.int32,(128,128),0)==lax.broadcasted_iota(jnp.int32,(128,128),1))&held[i*128:i*128+128],middle,-1),axis=0,keepdims=True)
        for i in range(C//128)],axis=1)
    ctx_bias=jnp.concatenate([jnp.where(ctx_key==middle,0.0,masked_score),jnp.zeros((1,Pn),f32)],axis=1)
    own_allowed=jnp.concatenate([query==ctx_key,jnp.ones((own,Pn),jnp.bool_),query==own_key],axis=1)
    own_bias=jnp.where(own_allowed,0.0,masked_score)

    def softmax(raw):
        highest=jnp.max(raw,axis=-1,keepdims=True)
        e=jnp.exp((raw-highest)*scale)
        return (e*(1.0/jnp.sum(e,axis=-1,keepdims=True))).astype(bf16)

    def forward_head(h,q_ref,qat,k_ref,kcol,vcol,lo,hi,bias,p_ref,pat,m_ref,mat,n):
        q=q_ref[pl.ds(qat,n),pl.ds(h*E,E)]
        k=k_ref[lo:hi,pl.ds(kcol+h*E,E)]
        v=k_ref[lo:hi,pl.ds(vcol+h*E,E)]
        raw=mm_t(q,k)
        if bias is not None: raw=raw+bias
        p=softmax(raw)
        p_ref[h,pl.ds(pat,n)]=p
        m_ref[pl.ds(mat,n),pl.ds(h*E,E)]=mm(p,v)

    def tail_forward(inp,mix,layer):
        attended=mm(mix.astype(bf16),w_out[layer])
        na,ra=normalize(inp+attended)
        hidden=na*ln_gain[layer,0:1]+ln_bias[layer,0:1]
        u=mm(hidden.astype(bf16),w_up[layer])
        phi=0.5*(1.0+lax.erf(u*inverse_root_two))
        act=(u*phi).astype(bf16)
        sl=phi+u*jnp.exp(-0.5*u*u)*inverse_root_two_pi
        nb,rb=normalize(hidden+mm(act,w_down[layer]))
        return nb*ln_gain[layer,1:2]+ln_bias[layer,1:2],na,ra,sl,nb,rb

    def tail_backward(grad,na,ra,sl,nb,rb,layer):
        g2=normalize_backward(nb,rb,ln_gain[layer,1:2],grad)
        ga=mm_t(g2.astype(bf16),w_down[layer])
        ge=(ga*sl).astype(bf16)
        gh=g2+mm_t(ge,w_up[layer])
        g1=normalize_backward(na,ra,ln_gain[layer,0:1],gh)
        return g1,mm_t(g1.astype(bf16),w_out[layer]).astype(bf16)

    def backward_head(h,q_ref,qat,k_ref,kcol,vcol,lo,hi,p_ref,pat,m_ref,mat,gat,dqat,n):
        cols=pl.ds(h*E,E)
        q=q_ref[pl.ds(qat,n),cols]
        k=k_ref[lo:hi,pl.ds(kcol+h*E,E)]
        v=k_ref[lo:hi,pl.ds(vcol+h*E,E)]
        g=gm[pl.ds(gat,n),cols]
        p=p_ref[h,pl.ds(pat,n)]
        delta=jnp.sum(g.astype(f32)*m_ref[pl.ds(mat,n),cols],axis=1,keepdims=True)
        ds=(p.astype(f32)*(mm_t(g,v)-delta)).astype(bf16)
        dq[pl.ds(dqat,n),cols]=(mm(ds,k)*scale).astype(bf16)
        dk[lo:hi,cols]+=t_mm(ds,q)
        dv[lo:hi,cols]+=t_mm(p,g)

    B=block_rows(R,448)
    @pl.loop(0,R//B)
    def _(i):
        rows=pl.ds(pl.multiple_of(i*B,B),B)
        qkv[rows]=mm(X[rows].astype(bf16),w_qkv[0]).astype(bf16)
    cb=block_rows(C,256)
    @pl.loop(0,HEADS)
    def _(h):
        @pl.loop(0,C//cb)
        def _(i):
            at=pl.multiple_of(i*cb,cb)
            forward_head(h,qkv,at,qkv,width,2*width,0,K,ctx_bias,p_ctx,at,mixed,at,cb)
        forward_head(h,qkv,C,qkv,width,2*width,C,K,None,p_prompt,0,mixed,C,Pn)
        forward_head(h,qkv,K,qkv,width,2*width,0,R,own_bias,p_own,0,mixed,K,own)
    T=block_rows(R,256)
    @pl.loop(0,R//T)
    def _(i):
        rows=pl.ds(pl.multiple_of(i*T,T),T)
        y,na,ra,sl,nb,rb=tail_forward(X[rows],mixed[rows],0)
        X1[rows]=y; n1[rows]=na; r1[rows]=ra; slope[rows]=sl; n2[rows]=nb; r2[rows]=rb
    @pl.loop(0,R//B)
    def _(i):
        rows=pl.ds(pl.multiple_of(i*B,B),B)
        kv1[rows]=mm(X1[rows].astype(bf16),w_qkv[1,:,width:]).astype(bf16)
    q1[...]=mm(X1[K:R].astype(bf16),w_qkv[1,:,0:width]).astype(bf16)
    @pl.loop(0,HEADS)
    def _(h):
        forward_head(h,q1,0,kv1,0,width,0,R,own_bias,p_own1,0,mixed1,0,own)
    y,na,ra,sl,nb,rb=tail_forward(X1[K:R],mixed1[...],1)
    out_rows[...]=y; n1b[...]=na; r1b[...]=ra; slopeb[...]=sl; n2b[...]=nb; r2b[...]=rb
    g1,gmix=tail_backward(d_out[...],n1b[...],r1b[...],slopeb[...],n2b[...],r2b[...],1)
    first[K:R]=g1
    gm[K:R]=gmix
    dk[...]=jnp.zeros_like(dk); dv[...]=jnp.zeros_like(dv)
    @pl.loop(0,HEADS)
    def _(h):
        backward_head(h,q1,0,kv1,0,width,0,R,p_own1,0,mixed1,0,K,K,own)
    first[0:K]=jnp.zeros((K,width),f32)
    first[K:R]+=mm_t(dq[K:R],w_qkv[1,:,0:width])
    def key_grads(rows,layer):
        return mm_t((dk[rows]*scale).astype(bf16),w_qkv[layer,:,width:2*width])+mm_t(dv[rows].astype(bf16),w_qkv[layer,:,2*width:])
    @pl.loop(0,R//B)
    def _(i):
        rows=pl.ds(pl.multiple_of(i*B,B),B)
        first[rows]+=key_grads(rows,1)
    @pl.loop(0,R//T)
    def _(i):
        rows=pl.ds(pl.multiple_of(i*T,T),T)
        g1,gmix=tail_backward(first[rows],n1[rows],r1[rows],slope[rows],n2[rows],r2[rows],0)
        first[rows]=g1; gm[rows]=gmix
    dk[...]=jnp.zeros_like(dk); dv[...]=jnp.zeros_like(dv)
    @pl.loop(0,HEADS)
    def _(h):
        @pl.loop(0,C//cb)
        def _(i):
            at=pl.multiple_of(i*cb,cb)
            backward_head(h,qkv,at,qkv,width,2*width,0,K,p_ctx,at,mixed,at,at,at,cb)
        backward_head(h,qkv,C,qkv,width,2*width,C,K,p_prompt,0,mixed,C,C,C,Pn)
        backward_head(h,qkv,K,qkv,width,2*width,0,R,p_own,0,mixed,K,K,K,own)
    @pl.loop(0,R//B)
    def _(i):
        rows=pl.ds(pl.multiple_of(i*B,B),B)
        first[rows]+=mm_t(dq[rows],w_qkv[0,:,0:width])+key_grads(rows,0)
    g_ctx[...]=first[0:C]
    g_prompt[...]=first[C:K]
    g_own[...]=first[K:R]
    def over(lo,hi):
        g=first[lo:hi]
        return jnp.sum(g,axis=0,keepdims=True),jnp.sum(g*X[lo:hi],axis=0,keepdims=True)
    a,b=over(0,C); c,d=over(K,R)
    sums[0:1]=a+c
    sums[1:2]=b+d

def compute(x,segs,kinds,small,ctx,prompt,d_out,w_qkv,w_out,w_up,w_down,ln_gain,ln_bias):
    own,width=x.shape; C=ctx.shape[0]; Pn=prompt.shape[0]; K=C+Pn; R=K+own
    FF=w_up.shape[2]
    vm=pl.BlockSpec(memory_space=pltpu.VMEM)
    V=pltpu.VMEM
    S=jax.ShapeDtypeStruct
    return pl.pallas_call(
        compute_kernel,
        out_shape=(S((own,width),f32),S((C,width),f32),S((Pn,width),f32),S((own,width),f32),S((2,width),f32),S((3,width),f32)),
        in_specs=[vm]*13,out_specs=(vm,)*6,
        scratch_shapes=[
            V((R,width),f32),V((R,width),f32),V((R,3*width),bf16),V((R,2*width),bf16),V((own,width),bf16),V((R,width),f32),V((own,width),f32),
            V((HEADS,C,K),bf16),V((HEADS,Pn,Pn),bf16),V((HEADS,own,R),bf16),V((HEADS,own,R),bf16),
            V((R,width),f32),V((R,1),f32),V((R,FF),f32),V((R,width),f32),V((R,1),f32),
            V((own,width),f32),V((own,1),f32),V((own,FF),f32),V((own,width),f32),V((own,1),f32),
            V((R,width),f32),V((R,width),bf16),V((R,width),bf16),V((R,width),f32),V((R,width),f32),
        ],
        compiler_params=pltpu.CompilerParams(vmem_limit_bytes=60*2**20),
        name="layers",
    )(x,segs,kinds,small,ctx,prompt,d_out,w_qkv,w_out,w_up,w_down,ln_gain,ln_bias)
def reduce_kernel(groups, seq, g_ctx, g_prompt, sums, red, red_prompt, red_sums,
                  work, a1, b1, a2, b2, az, s1, p1, s2, sv, p2, pv, a2v, b2v, zv,
                  ps, pr, cs, cr, zs, zr):
    net=Net(groups,seq); Z,Y,X=net.dims; G=groups
    width=g_ctx.shape[-1]; half=width//2
    N=G*Y*X
    bar=pltpu.get_barrier_semaphore()
    zto=[(net.z+d)%Z for d in range(1,Z)]; zback=[(net.z+Z-d)%Z for d in range(1,Z)]
    for zp in zto: pl.semaphore_signal(bar,inc=1,device_id=net.dev(z=zp),device_id_type=MESH)
    p=(net.g*Y+net.y)*X+net.x
    def who(q): return dict(g=q//(Y*X),y=(q//X)%Y,x=q%X)
    plane=[(who((p+d)%N),who((p+N-d)%N)) for d in range(1,N)]
    for to,fr in plane: pl.semaphore_signal(bar,inc=1,device_id=net.dev(**to),device_id_type=MESH)
    pl.semaphore_wait(bar,Z-1+N-1)
    pending=[]
    def remote(src,dst,s,r,dev):
        c=pltpu.make_async_remote_copy(src_ref=src,dst_ref=dst,send_sem=s,recv_sem=r,device_id=dev,device_id_type=MESH)
        c.start(); pending.append(c)
    def arrived(dst,s,r,dev):
        pltpu.make_async_remote_copy(src_ref=dst,dst_ref=dst,send_sem=s,recv_sem=r,device_id=dev,device_id_type=MESH).wait_recv()
    H=lambda h: pl.ds(h*half,half)
    work[...]=g_ctx[...].astype(bf16)
    for d in range(1,Y):
        q=(net.y+d)%Y
        remote(work.at[:,q,:,:,H(0)],a1.at[d-1],cs.at[0,d-1],cr.at[0,d-1],net.dev(y=q))
    for d in range(1,X):
        q=(net.x+d)%X
        remote(work.at[:,:,q,:,H(1)],b1.at[d-1],cs.at[1,d-1],cr.at[1,d-1],net.dev(x=q))
    for i,(to,fr) in enumerate(plane):
        remote(sums,s1.at[i],ps.at[0,i],pr.at[0,i],net.dev(**to))
        remote(g_prompt.at[to["g"],to["y"],to["x"]],p1.at[i],ps.at[1,i],pr.at[1,i],net.dev(**to))
    tot=sums[...]
    for i,(to,fr) in enumerate(plane):
        arrived(s1.at[i],ps.at[0,i],pr.at[0,i],net.dev(**fr))
        tot=tot+s1[i]
    sv[...]=tot
    for i,zp in enumerate(zto):
        remote(sv,s2.at[i],zs.at[0,i],zr.at[0,i],net.dev(z=zp))
    t=g_ctx[:,net.y,:,:,0:half]
    for d in range(1,Y):
        arrived(a1.at[d-1],cs.at[0,d-1],cr.at[0,d-1],net.dev(y=(net.y+Y-d)%Y))
        t=t+a1[d-1].astype(f32)
    a2v[...]=t.astype(bf16)
    for d in range(1,X):
        q=(net.x+d)%X
        remote(a2v.at[:,q],a2.at[d-1],cs.at[2,d-1],cr.at[2,d-1],net.dev(x=q))
    t=g_ctx[:,:,net.x,:,half:]
    for d in range(1,X):
        arrived(b1.at[d-1],cs.at[1,d-1],cr.at[1,d-1],net.dev(x=(net.x+X-d)%X))
        t=t+b1[d-1].astype(f32)
    b2v[...]=t.astype(bf16)
    for d in range(1,Y):
        q=(net.y+d)%Y
        remote(b2v.at[:,q],b2.at[d-1],cs.at[3,d-1],cr.at[3,d-1],net.dev(y=q))
    t=g_prompt[net.g,net.y,net.x].astype(f32)
    for i,(to,fr) in enumerate(plane):
        arrived(p1.at[i],ps.at[1,i],pr.at[1,i],net.dev(**fr))
        t=t+p1[i].astype(f32)
    pv[...]=t
    for i,zp in enumerate(zto):
        remote(pv.at[zp],p2.at[i],zs.at[1,i],zr.at[1,i],net.dev(z=zp))
    t=a2v[:,net.x].astype(f32)
    for d in range(1,X):
        arrived(a2.at[d-1],cs.at[2,d-1],cr.at[2,d-1],net.dev(x=(net.x+X-d)%X))
        t=t+a2[d-1].astype(f32)
    zv[0]=t.astype(bf16)
    for i,zp in enumerate(zto):
        remote(zv.at[0,zp],az.at[0,i],zs.at[2,i],zr.at[2,i],net.dev(z=zp))
    t=b2v[:,net.y].astype(f32)
    for d in range(1,Y):
        arrived(b2.at[d-1],cs.at[3,d-1],cr.at[3,d-1],net.dev(y=(net.y+Y-d)%Y))
        t=t+b2[d-1].astype(f32)
    zv[1]=t.astype(bf16)
    for i,zp in enumerate(zto):
        remote(zv.at[1,zp],az.at[1,i],zs.at[3,i],zr.at[3,i],net.dev(z=zp))
    tot=sv[...]
    for i,zp in enumerate(zback):
        arrived(s2.at[i],zs.at[0,i],zr.at[0,i],net.dev(z=zp))
        tot=tot+s2[i]
    red_sums[...]=tot
    t=pv[net.z]
    for i,zp in enumerate(zback):
        arrived(p2.at[i],zs.at[1,i],zr.at[1,i],net.dev(z=zp))
        t=t+p2[i]
    red_prompt[...]=t
    for h in range(2):
        t=zv[h,net.z].astype(f32)
        for i,zp in enumerate(zback):
            arrived(az.at[h,i],zs.at[2+h,i],zr.at[2+h,i],net.dev(z=zp))
            t=t+az[h,i].astype(f32)
        red[:,h*half:(h+1)*half]=t
    for c in pending: c.wait_send()

def reduce(g_ctx,g_prompt,sums,groups,seq):
    Z,Y,X=seq_dims(seq); C,D=g_ctx.shape[3:]; N=groups*Y*X; M=max(X,Y,2); half=D//2
    pshape=g_prompt.shape[4:]
    DMA=pltpu.SemaphoreType.DMA; V=pltpu.VMEM
    vm=pl.BlockSpec(memory_space=pltpu.VMEM)
    S=jax.ShapeDtypeStruct
    return pl.pallas_call(
        functools.partial(reduce_kernel,groups,seq),
        out_shape=(S((C,D),f32),S(pshape,f32),S(sums.shape,f32)),
        in_specs=[vm]*3,out_specs=(vm,)*3,
        scratch_shapes=[V((Z,Y,X,C,D),bf16),
            V((Y,Z,X,C,half),bf16),V((X,Z,Y,C,half),bf16),V((X,Z,C,half),bf16),V((Y,Z,C,half),bf16),V((2,Z,C,half),bf16),
            V((N,)+sums.shape,f32),V((N,Z)+pshape,bf16),V((Z,)+sums.shape,f32),V(sums.shape,f32),V((Z,)+pshape,f32),V((Z,)+pshape,f32),
            V((Z,X,C,half),bf16),V((Z,Y,C,half),bf16),V((2,Z,C,half),bf16),
            DMA((2,N)),DMA((2,N)),DMA((4,M)),DMA((4,M)),DMA((4,Z)),DMA((4,Z))],
        compiler_params=pltpu.CompilerParams(collective_id=1,has_side_effects=True,vmem_limit_bytes=40*2**20),
        name="reduce_gradients",
    )(g_ctx,g_prompt,sums)


def compute_plain(x,segs,kinds,small,ctx,prompt,d_out,w_qkv,w_out,w_up,w_down,ln_gain,ln_bias):
    own,width=x.shape; C=ctx.shape[0]; Pn=prompt.shape[0]; K=C+Pn; E=width//HEADS; scale=E**-0.5
    middle=3*lax.axis_index("group")+1
    L=width//128
    total=jnp.sum(small,axis=0)
    count=total[2*L,0]
    mean=total[0:L].reshape(1,width)/count; second=total[L:2*L].reshape(1,width)/count
    spread=lax.rsqrt(second-mean*mean+epsilon)
    held=ctx[:,0]<0.5*absent
    X0=jnp.concatenate([jnp.where(held[:,None],(ctx-mean)*spread,0.0),prompt.astype(f32),(x-mean)*spread],axis=0)
    seg=segs[0]; kind=kinds[0]
    query=jnp.where(kind==2,-2,seg); own_key=jnp.where((kind==0)&(seg!=middle),seg,-1)
    ctx_key=jnp.where(held,middle,-1)
    bias=lambda flag: jnp.where(flag,0.0,masked_score)
    own_bias=bias(jnp.concatenate([query[:,None]==ctx_key[None],jnp.ones((own,Pn),bool),query[:,None]==own_key[None]],axis=1))
    ctx_bias=jnp.concatenate([bias(held)[None],jnp.zeros((1,Pn),f32)],axis=1)
    heads=lambda a: a.reshape(a.shape[0],HEADS,E)
    def attend(q,k,v,b):
        raw=jnp.einsum("rhe,khe->hrk",heads(q),heads(k),preferred_element_type=f32)+b
        e=jnp.exp((raw-jnp.max(raw,axis=-1,keepdims=True))*scale)
        p=(e/jnp.sum(e,axis=-1,keepdims=True)).astype(bf16)
        return jnp.einsum("hrk,khe->rhe",p,heads(v),preferred_element_type=f32).reshape(q.shape[0],width),p
    def attend_back(q,k,v,p,mix,g):
        delta=jnp.sum(heads(g).astype(f32)*heads(mix),axis=2).T
        ds=(p.astype(f32)*(jnp.einsum("rhe,khe->hrk",heads(g),heads(v),preferred_element_type=f32)-delta[...,None])).astype(bf16)
        flat=lambda a: a.reshape(a.shape[0],width)
        return (flat(jnp.einsum("hrk,khe->rhe",ds,heads(k),preferred_element_type=f32))*scale,
            flat(jnp.einsum("hrk,rhe->khe",ds,heads(q),preferred_element_type=f32))*scale,
            flat(jnp.einsum("hrk,rhe->khe",p,heads(g),preferred_element_type=f32)))
    def tail(inp,mix,layer):
        na,ra=normalize(inp+mm(mix.astype(bf16),w_out[layer]))
        hidden=na*ln_gain[layer,0]+ln_bias[layer,0]
        u=mm(hidden.astype(bf16),w_up[layer])
        phi=0.5*(1.0+lax.erf(u*inverse_root_two))
        nb,rb=normalize(hidden+mm((u*phi).astype(bf16),w_down[layer]))
        return nb*ln_gain[layer,1]+ln_bias[layer,1],(na,ra,phi+u*jnp.exp(-0.5*u*u)*inverse_root_two_pi,nb,rb)
    def tail_back(grad,kept,layer):
        na,ra,sl,nb,rb=kept
        g2=normalize_backward(nb,rb,ln_gain[layer,1],grad)
        ge=(mm_t(g2.astype(bf16),w_down[layer])*sl).astype(bf16)
        g1=normalize_backward(na,ra,ln_gain[layer,0],g2+mm_t(ge,w_up[layer]))
        return g1,mm_t(g1.astype(bf16),w_out[layer]).astype(bf16)
    qkv=mm(X0.astype(bf16),w_qkv[0]).astype(bf16)
    q,k,v=qkv[:,:width],qkv[:,width:2*width],qkv[:,2*width:]
    mix_c,p_c=attend(q[:C],k[:K],v[:K],ctx_bias)
    mix_p,p_p=attend(q[C:K],k[C:K],v[C:K],0.0)
    mix_o,p_o=attend(q[K:],k,v,own_bias)
    mix=jnp.concatenate([mix_c,mix_p,mix_o],axis=0)
    X1,kept=tail(X0,mix,0)
    kv=mm(X1.astype(bf16),w_qkv[1,:,width:]).astype(bf16)
    q1=mm(X1[K:].astype(bf16),w_qkv[1,:,:width]).astype(bf16)
    mix1,p1=attend(q1,kv[:,:width],kv[:,width:],own_bias)
    out,kept1=tail(X1[K:],mix1,1)
    g1,gm=tail_back(d_out,kept1,1)
    dq,dk,dv=attend_back(q1,kv[:,:width],kv[:,width:],p1,mix1,gm)
    G=mm_t(jnp.concatenate([dk,dv],axis=1).astype(bf16),w_qkv[1,:,width:])
    G=G.at[K:].add(g1+mm_t(dq.astype(bf16),w_qkv[1,:,:width]))
    g1,gm=tail_back(G,kept,0)
    dqc,dkc,dvc=attend_back(q[:C],k[:K],v[:K],p_c,mix[:C],gm[:C])
    dqp,dkp,dvp=attend_back(q[C:K],k[C:K],v[C:K],p_p,mix[C:K],gm[C:K])
    dqo,dk,dv=attend_back(q[K:],k,v,p_o,mix[K:],gm[K:])
    dk=dk.at[:K].add(dkc).at[C:K].add(dkp); dv=dv.at[:K].add(dvc).at[C:K].add(dvp)
    grads=jnp.concatenate([jnp.concatenate([dqc,dqp,dqo],axis=0),dk,dv],axis=1).astype(bf16)
    G=g1+mm_t(grads,w_qkv[0])
    data=jnp.concatenate([G[:C],G[K:]],axis=0)
    sums=jnp.stack([jnp.sum(data,axis=0),jnp.sum(data*jnp.concatenate([X0[:C],X0[K:]],axis=0),axis=0)])
    return out,G[:C],G[C:K],G[K:],sums,jnp.concatenate([mean,spread,jnp.broadcast_to(count,(1,width))],axis=0)


def per_device(groups, seq, x, seg_ids, row_kind, prompt, w_qkv, w_out, w_up, w_down, ln_gain, ln_bias, d_out):
    own,width=x.shape; L=width//128
    Z,Y,X=seq_dims(seq); C=own//8; Pd=prompt.shape[0]
    segs=seg_ids.reshape(1,own); kinds=row_kind.reshape(1,own)
    ctx,small,blocks=gather(x,segs,kinds,prompt,groups,seq)
    ctx=ctx.reshape(seq*C,width)
    prompts=blocks.reshape(-1,L,Pd,128).transpose(0,2,1,3).reshape(-1,width)
    run=compute if seq*C+prompts.shape[0]<=1024 else compute_plain
    out,g_ctx,g_prompt,g_own,sums,stats=run(x,segs,kinds,small.reshape((-1,)+small.shape[3:]),ctx,prompts,d_out,w_qkv,w_out,w_up,w_down,ln_gain,ln_bias)
    g_blocks=g_prompt.astype(bf16).reshape(-1,Pd,L,128).transpose(0,2,1,3).reshape(blocks.shape)
    red,red_prompt,red_sums=reduce(g_ctx.reshape(Z,Y,X,C,width),g_blocks,sums.reshape(2*L,128),groups,seq)
    middle=3*lax.axis_index("group")+1
    chosen=((row_kind==0)&(seg_ids==middle))[:,None]
    usable=(row_kind!=2).astype(f32)[:,None]
    grad=g_own+jnp.where(chosen,jnp.repeat(red,8,axis=0),0.0)
    mean,spread,count=stats[0:1],stats[1:2],stats[2:3]
    grad_sum=red_sums[:L].reshape(1,width); grad_dot=red_sums[L:].reshape(1,width)
    normed=(x-mean)*spread
    grad_rows=spread*(grad-usable/count*(grad_sum+normed*grad_dot))
    grad_prompt=red_prompt.reshape(L,Pd,128).transpose(1,0,2).reshape(Pd,width)
    return out,grad_rows,grad_prompt


def solution(mesh):
    rows=P(("group","seq"),None); labels=P(("group","seq"))
    return jax.shard_map(
        functools.partial(per_device,mesh.shape["group"],mesh.shape["seq"]),
        mesh=mesh,
        in_specs=(rows,labels,labels,rows,P(),P(),P(),P(),P(),P(),rows),
        out_specs=(rows,rows,rows),
        check_vma=False,
    )
```

time: 1070 us -> 106 us (0.10)
  blocking collectives: 449 us -> 0 us
  waiting for transfers between devices: 293 us -> 0 us
  matrix products: 152 us -> 0 us
  local copies, waits for them, and re-layouts: 118 us -> 7.96 us
  Pallas kernels: 0 us -> 93.4 us
  other arithmetic: 30.8 us -> 3.08 us
  between operations: 17.1 us -> 0.78 us
    all_gather x5 -> x0, blocking collectives: 303 us -> none  [the longest x2 135 us: per_device(): lax.all_gather(prompt_pair[:, :width], ('group', 'seq'), axis=0, tiled=True)]
    reduce_scatter x4 -> x0, waiting for transfers between devices: 292 us -> none  [the longest x2 194 us: per_device(): lax.psum_scatter(merge_heads(group_grads[1]).astype(jnp.bfloat16), 'seq',...]
    dot_general x69 -> x0, matrix products: 152 us -> none  [the longest x10 26.5 us: times_transpose(): lax.dot_general(left, right, (((1,), (1,)), ((), ())), preferred_element_...]
    pallas_call x0 -> x3, Pallas kernels: none -> 93.4 us  [the longest x1 51.1 us: compute(): pl.pallas_call(compute_kernel, out_shape=(S((own, width), f32), S((C, wid...]
    psum x2 -> x0, blocking collectives: 89.1 us -> none  [the longest x1 46.7 us: per_device(): lax.psum((jnp.sum(grad_rows, axis=0), jnp.sum(grad_rows * normed, axis=0)...]
    unnamed x1 -> x0, blocking collectives: 56.4 us -> none
    another operation x8 -> x0, local copies, waits for them, and re-layouts: 37.9 us -> none  [the longest x4 27.7 us: blocks_of(): return array.reshape((array.shape[0] // size, size) + array.shape[1:])]
    convert_element_type x8 -> x0, local copies, waits for them, and re-layouts: 23.7 us -> none  [the longest x2 11.9 us: per_device(): merge_heads(group_grads[1]).astype(jnp.bfloat16)]
  transfers between devices with their start and end apart: 8 -> 0, of which waited for: 4 -> 0; matrix products, arithmetic and copies ran while one was open for 9% -> 0% of each run, Pallas kernels for 0% -> 0%
where the time goes in v1:
time: 106 us; the launch traced here: 105 us
  Pallas kernels  93.4 us (88%)
  local copies, waits for them, and re-layouts  7.96 us (8%)
  other arithmetic  3.08 us (3%)
    pallas_call x1, Pallas kernels, compute(): pl.pallas_call(compute_kernel, out_shape=(S((own, width), f32), S((C, wid...  51.1 us
    pallas_call x1, Pallas kernels, gather(): pl.pallas_call(functools.partial(gather_kernel, groups, seq), out_shape=(...  25.4 us
    pallas_call x1, Pallas kernels, reduce(): pl.pallas_call(functools.partial(reduce_kernel, groups, seq), out_shape=(...  16.9 us
    unnamed x24, local copies, waits for them, and re-layouts  7.13 us

profile of v1, /device:TPU:0, one launch (start us, length us, event | category | flops | bytes accessed | tf_op | source)
XLA Modules:
  0.0 105.2 jit_solution(7618359396787276718)
XLA Ops:
  0.6 0.0 copy-start
  0.6 1.0 copy-done
  1.7 0.7 copy-done.5
  2.4 0.7 copy-done.7
  3.0 0.7 copy-done.9
  3.7 25.4 %gather_context.1 = (f32[4,2,2,32,512]{4,3,2,1,0:T(8,128)S(1)}, f32[2,2,2,16,128]{4,3,2,1,0:T(8,128)S(1)}, bf16[2,2,2,4,16,128]{5,4,3,2,1,0:T(8,128)(2,1)S(1)}) custom-call(f32[256,512]{1,0:T(8,128)S(1)} %copy-done, s32[1,256]{1,0:T(1,128)S(1)} %bitcast.39, s32[1,256]{1,0:T(1,128)S(1)} %bitcast.41, bf16[4,512]{1,0:T(4,128)(2,1)S(1)} %copy-done.9), custom_call_target="tpu_custom_call" | custom-call | tf_op jit(solution)/shard_map/gather_context/pallas_call | solution.py:131
  29.1 0.0 copy-start.2
  29.1 1.0 copy-done.2
  30.1 0.1 copy.14
  30.1 0.6 copy-done.4
  30.7 0.7 copy.19
  31.4 51.1 %layers.1 = (f32[256,512]{1,0:T(8,128)}, f32[512,512]{1,0:T(8,128)}, f32[128,512]{1,0:T(8,128)}, f32[256,512]{1,0:T(8,128)}, f32[2,512]{1,0:T(2,128)}, /*index=5*/f32[3,512]{1,0:T(4,128)}) custom-call(f32[256,512]{1,0:T(8,128)} %x.3, s32[1,256]{1,0:T(1,128)} %bitcast.38, s32[1,256]{1,0:T(1,128)} %bitcast.40, f32[8,16,128]{2,1,0:T(8,128)} %bitcast.37, ...), custom_call_target="tpu_custom_call" | custom-call | tf_op jit(solution)/shard_map/layers/pallas_call | solution.py:334
  82.5 0.0 copy-start.6
  82.5 0.0 copy-start.8
  82.5 0.0 copy-start.1
  82.5 1.0 convert_element_type.6
  83.6 0.1 copy.15
  83.6 0.7 reshape.60.sums
  84.3 1.2 %copy-done.3 = f32[512,512]{1,0:T(8,128)S(1)} copy-done((f32[512,512]{1,0:T(8,128)S(1)}, f32[512,512]{1,0:T(8,128)}, u32[]{:S(2)}) %copy-start.3) | copy-done | bytes 1048600
  85.6 16.9 %reduce_gradients.1 = (f32[32,512]{1,0:T(8,128)S(1)}, f32[16,128]{1,0:T(8,128)S(1)}, f32[8,128]{1,0:T(8,128)S(1)}) custom-call(f32[4,2,2,32,512]{4,3,2,1,0:T(8,128)S(1)} %bitcast.34, bf16[2,2,2,4,16,128]{5,4,3,2,1,0:T(8,128)(2,1)S(1)} %bitcast.35, f32[8,128]{1,0:T(8,128)S(1)} %reshape.60.sums), custom_call_target="tpu_custom_call" | custom-call | tf_op jit(solution)/shard_map/reduce_gradients/pallas_call | solution.py:447
  102.5 0.0 copy-done.6
  102.5 0.0 copy-done.8
  102.6 2.0 %fusion.1 = f32[256,512]{1,0:T(8,128)} fusion(f32[256,512]{1,0:T(8,128)} %get-tuple-element.20, f32[256,512]{1,0:T(8,128)S(1)} %copy-done.1, f32[512]{0:T(512)S(1)} %get-tuple-element.31, f32[512]{0:T(512)S(1)} %bitcast.46, f32[512]{0:T(512)S(1)} %get-tuple-element.30, f32[512]{0:T(512)S(1)} %bitcast.47, f32[256]{0:T(256)S(1)} %get-tuple-element.33, ...), kind=kLoop, calls=%fused_computation.2 | loop fusion | flops 1310720 | bytes 1649920 | tf_op jit(solution)/shard_map/mul | solution.py:548
  104.6 0.6 copy.21
  (12 shorter events, 0.1 us)
Async XLA Ops:
  0.6 1.0 copy-start
  1.7 0.7 copy-start.5
  2.4 0.7 copy-start.7
  3.0 0.7 copy-start.9
  29.1 1.0 copy-start.2
  30.1 0.6 copy-start.4
  82.5 20.0 %copy-start.10 = (f32[3,512]{1,0:T(4,128)S(1)}, f32[3,512]{1,0:T(4,128)}, u32[]{:S(2)}) copy-start(f32[3,512]{1,0:T(4,128)} %get-tuple-element.19) | copy-start | bytes 18436
  82.5 20.1 %copy-start.6 = (s32[256]{0:T(256)S(1)}, s32[256]{0:T(256)}, u32[]{:S(2)}) copy-start(s32[256]{0:T(256)} %param.12) | copy-start | bytes 3076
  82.5 20.1 %copy-start.8 = (s32[256]{0:T(256)S(1)}, s32[256]{0:T(256)}, u32[]{:S(2)}) copy-start(s32[256]{0:T(256)} %param.13) | copy-start | bytes 3076
  82.5 20.1 %copy-start.1 = (f32[256,512]{1,0:T(8,128)S(1)}, f32[256,512]{1,0:T(8,128)}, u32[]{:S(2)}) copy-start(f32[256,512]{1,0:T(8,128)} %x.3) | copy-start | bytes 1572868
  84.3 1.2 %copy-start.3 = (f32[512,512]{1,0:T(8,128)S(1)}, f32[512,512]{1,0:T(8,128)}, u32[]{:S(2)}) copy-start(f32[512,512]{1,0:T(8,128)} %get-tuple-element.21) | copy-start | bytes 3145732

commit v2 on v1

--- a/solution.py
+++ b/solution.py
@@ -143,6 +143,7 @@
 masked_score = -1e30
 inverse_root_two = 0.7071067811865476
 inverse_root_two_pi = 0.3989422804014327
+log2_e = 1.4426950408889634
 absent = 1e9
 f32=jnp.float32
 bf16=jnp.bfloat16
@@ -165,14 +166,23 @@
 def block_rows(count,most):
     return max(b for b in range(16,min(count,most)+1,16) if count%b==0)
 
+def pipeline(jobs):
+    state=[{} for _ in jobs]
+    longest=max(len(j) for j in jobs)
+    for step in range(len(jobs)+longest-1):
+        now=[(state[j],)+jobs[j][step-j] for j in range(len(jobs)) if 0<=step-j<len(jobs[j])]
+        for want in "mv":
+            for s,kind,stage in reversed(now):
+                if kind==want: stage(s)
+
 def compute_kernel(
     x, segs, kinds, small, ctx, prompt, d_out, w_qkv, w_out, w_up, w_down, ln_gain, ln_bias,
     out_rows, g_ctx, g_prompt, g_own, sums, stats,
-    X, X1, qkv, kv1, q1, mixed, mixed1, p_ctx, p_prompt, p_own, p_own1,
-    n1, r1, slope, n2, r2, n1b, r1b, slopeb, n2b, r2b, first, gm, dq, dk, dv,
+    X, X1, qkv, qkv1, mixed, mixed1, inv, inv1, p_main, p_prompt, p_local, p_main1, p_local1,
+    n1, r1, slope, n2, r2, n1b, r1b, slopeb, n2b, r2b, first, gm, grads, ds_main, ds_local, ds_prompt, bias,
 ):
     own,width=x.shape
-    C=ctx.shape[0]; Pn=prompt.shape[0]; K=C+Pn; R=K+own
+    C=ctx.shape[0]; Pn=prompt.shape[0]; K=C+Pn; R=K+own; M=C+own
     E=width//HEADS
     scale=E**-0.5
     group=lax.axis_index("group")
@@ -190,67 +200,113 @@
     stats[2:3]=jnp.broadcast_to(count,(1,width))
     raw=ctx[...]
     held=jnp.abs(raw[:,0:1])<0.5*absent
-    X[0:C]=jnp.where(held,(raw-mean)*spread,0.0)
-    X[C:K]=prompt[...].astype(f32)
+    X[0:Pn]=prompt[...].astype(f32)
+    X[Pn:K]=jnp.where(held,(raw-mean)*spread,0.0)
     X[K:R]=(x[...]-mean)*spread
     eye=lax.broadcasted_iota(jnp.int32,(own,own),0)==lax.broadcasted_iota(jnp.int32,(own,own),1)
     def column(lane): return jnp.max(jnp.where(eye,lane,-9),axis=1,keepdims=True)
     seg=segs[...]; kind=kinds[...]
     own_key=jnp.where((kind==0)&(seg!=middle),seg,-1)
     query=column(jnp.where(kind==2,-2,seg))
+    square=lax.broadcasted_iota(jnp.int32,(128,128),0)==lax.broadcasted_iota(jnp.int32,(128,128),1)
     ctx_key=jnp.concatenate([
-        jnp.max(jnp.where((lax.broadcasted_iota(jnp.int32,(128,128),0)==lax.broadcasted_iota(jnp.int32,(128,128),1))&held[i*128:i*128+128],middle,-1),axis=0,keepdims=True)
+        jnp.max(jnp.where(square&held[i*128:i*128+128],middle,-1),axis=0,keepdims=True)
         for i in range(C//128)],axis=1)
-    ctx_bias=jnp.concatenate([jnp.where(ctx_key==middle,0.0,masked_score),jnp.zeros((1,Pn),f32)],axis=1)
-    own_allowed=jnp.concatenate([query==ctx_key,jnp.ones((own,Pn),jnp.bool_),query==own_key],axis=1)
-    own_bias=jnp.where(own_allowed,0.0,masked_score)
-
-    def softmax(raw):
-        highest=jnp.max(raw,axis=-1,keepdims=True)
-        e=jnp.exp((raw-highest)*scale)
-        return (e*(1.0/jnp.sum(e,axis=-1,keepdims=True))).astype(bf16)
-
-    def forward_head(h,q_ref,qat,k_ref,kcol,vcol,lo,hi,bias,p_ref,pat,m_ref,mat,n):
-        q=q_ref[pl.ds(qat,n),pl.ds(h*E,E)]
-        k=k_ref[lo:hi,pl.ds(kcol+h*E,E)]
-        v=k_ref[lo:hi,pl.ds(vcol+h*E,E)]
-        raw=mm_t(q,k)
-        if bias is not None: raw=raw+bias
-        p=softmax(raw)
-        p_ref[h,pl.ds(pat,n)]=p
-        m_ref[pl.ds(mat,n),pl.ds(h*E,E)]=mm(p,v)
-
-    def tail_forward(inp,mix,layer):
-        attended=mm(mix.astype(bf16),w_out[layer])
-        na,ra=normalize(inp+attended)
-        hidden=na*ln_gain[layer,0:1]+ln_bias[layer,0:1]
-        u=mm(hidden.astype(bf16),w_up[layer])
-        phi=0.5*(1.0+lax.erf(u*inverse_root_two))
-        act=(u*phi).astype(bf16)
-        sl=phi+u*jnp.exp(-0.5*u*u)*inverse_root_two_pi
-        nb,rb=normalize(hidden+mm(act,w_down[layer]))
-        return nb*ln_gain[layer,1:2]+ln_bias[layer,1:2],na,ra,sl,nb,rb
-
-    def tail_backward(grad,na,ra,sl,nb,rb,layer):
-        g2=normalize_backward(nb,rb,ln_gain[layer,1:2],grad)
-        ga=mm_t(g2.astype(bf16),w_down[layer])
-        ge=(ga*sl).astype(bf16)
-        gh=g2+mm_t(ge,w_up[layer])
-        g1=normalize_backward(na,ra,ln_gain[layer,0:1],gh)
-        return g1,mm_t(g1.astype(bf16),w_out[layer]).astype(bf16)
-
-    def backward_head(h,q_ref,qat,k_ref,kcol,vcol,lo,hi,p_ref,pat,m_ref,mat,gat,dqat,n):
-        cols=pl.ds(h*E,E)
-        q=q_ref[pl.ds(qat,n),cols]
-        k=k_ref[lo:hi,pl.ds(kcol+h*E,E)]
-        v=k_ref[lo:hi,pl.ds(vcol+h*E,E)]
-        g=gm[pl.ds(gat,n),cols]
-        p=p_ref[h,pl.ds(pat,n)]
-        delta=jnp.sum(g.astype(f32)*m_ref[pl.ds(mat,n),cols],axis=1,keepdims=True)
-        ds=(p.astype(f32)*(mm_t(g,v)-delta)).astype(bf16)
-        dq[pl.ds(dqat,n),cols]=(mm(ds,k)*scale).astype(bf16)
-        dk[lo:hi,cols]+=t_mm(ds,q)
-        dv[lo:hi,cols]+=t_mm(p,g)
+    ctx_bias=jnp.concatenate([jnp.zeros((1,Pn),f32),jnp.where(ctx_key==middle,0.0,masked_score)],axis=1)
+    own_allowed=jnp.concatenate([jnp.ones((own,Pn),jnp.bool_),query==ctx_key,query==own_key],axis=1)
+    bias[...]=jnp.where(own_allowed,0.0,masked_score)
+
+    def cols(h,part=0): return slice(part*width+h*E,part*width+(h+1)*E)
+
+    def exponentials(raws):
+        highest=functools.reduce(jnp.maximum,[jnp.max(r,axis=-1,keepdims=True) for r in raws])
+        es=[jnp.exp2((r-highest)*(scale*log2_e)) for r in raws]
+        return [e.astype(bf16) for e in es],1.0/sum(jnp.sum(e,axis=-1,keepdims=True) for e in es)
+
+    def forward_job(h,act,rows,out,keys,shift,store,m_ref,inv_ref):
+        def scores(s):
+            q=act[rows,cols(h)]
+            s["raw"]=[mm_t(q,act[lo:hi,cols(h,1)]) for lo,hi in keys]
+        def weigh(s):
+            s["p"],s["inv"]=exponentials(shift(s.pop("raw")))
+            store(s["p"])
+        def mix(s):
+            s["mix"]=functools.reduce(jnp.add,[mm(p,act[lo:hi,cols(h,2)]) for p,(lo,hi) in zip(s["p"],keys)])
+        def keep(s):
+            wide_inv=jnp.broadcast_to(s["inv"],s["mix"].shape)
+            m_ref[out,cols(h)]=s["mix"]*wide_inv
+            inv_ref[out,cols(h)]=wide_inv
+        return [("m",scores),("v",weigh),("m",mix),("v",keep)]
+
+    def ctx_job(h,at,n):
+        def store(p): p_main[h,at:at+n]=p[0]
+        return forward_job(h,qkv,slice(Pn+at,Pn+at+n),slice(Pn+at,Pn+at+n),[(0,K)],lambda raws:[raws[0]+ctx_bias],store,mixed,inv)
+    def prompt_job(h):
+        def store(p): p_prompt[h]=p[0]
+        return forward_job(h,qkv,slice(0,Pn),slice(0,Pn),[(0,Pn)],lambda raws:raws,store,mixed,inv)
+    def own_job(h,act,pm,at,pl_,m_ref,inv_ref,out):
+        def store(p):
+            pm[h,at:at+own]=p[0]; pl_[h]=p[1]
+        return forward_job(h,act,slice(K,R),out,[(0,K),(K,R)],lambda raws:[raws[0]+bias[:,0:K],raws[1]+bias[:,K:R]],store,m_ref,inv_ref)
+
+    def tail_job(layer,rows,kept,x_ref,m_ref,store):
+        na_,ra_,sl_,nb_,rb_=kept
+        xr,mr,kr=rows
+        def attended(s): s["a"]=mm(m_ref[mr].astype(bf16),w_out[layer])
+        def first_norm(s):
+            n,r=normalize(x_ref[xr]+s.pop("a"))
+            na_[kr]=n; ra_[kr]=r
+            s["h"]=n*ln_gain[layer,0:1]+ln_bias[layer,0:1]
+            s["hb"]=s["h"].astype(bf16)
+        def up(s): s["u"]=mm(s.pop("hb"),w_up[layer])
+        def gelu(s):
+            u=s.pop("u")
+            phi=0.5*(1.0+lax.erf(u*inverse_root_two))
+            s["act"]=(u*phi).astype(bf16)
+            sl_[kr]=phi+u*jnp.exp2(u*u*(-0.5*log2_e))*inverse_root_two_pi
+        def down(s): s["d"]=mm(s.pop("act"),w_down[layer])
+        def second_norm(s):
+            n,r=normalize(s.pop("h")+s.pop("d"))
+            nb_[kr]=n; rb_[kr]=r
+            store(n*ln_gain[layer,1:2]+ln_bias[layer,1:2])
+        return [("m",attended),("v",first_norm),("m",up),("v",gelu),("m",down),("v",second_norm)]
+
+    def tail_back_job(layer,kr,rows,kept,load,inv_ref,ir):
+        na_,ra_,sl_,nb_,rb_=kept
+        def second_norm(s):
+            s["g2"]=normalize_backward(nb_[kr],rb_[kr],ln_gain[layer,1:2],load())
+            s["g2b"]=s["g2"].astype(bf16)
+        def down(s): s["ga"]=mm_t(s.pop("g2b"),w_down[layer])
+        def gelu(s): s["ge"]=(s.pop("ga")*sl_[kr]).astype(bf16)
+        def up(s): s["gh"]=mm_t(s.pop("ge"),w_up[layer])
+        def first_norm(s):
+            g1=normalize_backward(na_[kr],ra_[kr],ln_gain[layer,0:1],s.pop("g2")+s.pop("gh"))
+            first[rows]=g1
+            s["g1b"]=g1.astype(bf16)
+        def out(s): s["gm"]=mm_t(s.pop("g1b"),w_out[layer])
+        def keep(s): gm[rows]=(s.pop("gm").astype(bf16).astype(f32)*inv_ref[ir]).astype(bf16)
+        return [("v",second_norm),("m",down),("v",gelu),("m",up),("v",first_norm),("m",out),("v",keep)]
+
+    def backward_job(h,act,rows,out,keys,load,store,m_ref):
+        def products(s):
+            g=gm[out,cols(h)]
+            s["dp"]=[mm_t(g,act[lo:hi,cols(h,2)]) for lo,hi in keys]
+        def scores(s):
+            shift=jnp.sum(gm[out,cols(h)].astype(f32)*m_ref[rows,cols(h)],axis=-1,keepdims=True)
+            s["ds"]=[(p.astype(f32)*(dp-shift)).astype(bf16) for p,dp in zip(load(),s.pop("dp"))]
+            store(s["ds"])
+        def queries(s):
+            s["dq"]=functools.reduce(jnp.add,[mm(d,act[lo:hi,cols(h,1)]) for d,(lo,hi) in zip(s.pop("ds"),keys)])
+        def keep(s): grads[out,cols(h)]=(s.pop("dq")*scale).astype(bf16)
+        return [("m",products),("v",scores),("m",queries),("v",keep)]
+
+    def key_job(h,terms,at,n):
+        jobs=[]
+        for part,mult in ((1,scale),(2,1.0)):
+            def product(s,part=part): s["t"]=functools.reduce(jnp.add,[t_mm(l(),r()) for l,r in terms[part]])
+            def keep(s,part=part,mult=mult): grads[at:at+n,cols(h,part)]=(s.pop("t")*mult).astype(bf16).T
+            jobs.append([("m",product),("v",keep)])
+        return jobs
 
     B=block_rows(R,448)
     @pl.loop(0,R//B)
@@ -258,75 +314,86 @@
         rows=pl.ds(pl.multiple_of(i*B,B),B)
         qkv[rows]=mm(X[rows].astype(bf16),w_qkv[0]).astype(bf16)
     cb=block_rows(C,256)
-    @pl.loop(0,HEADS)
-    def _(h):
-        @pl.loop(0,C//cb)
-        def _(i):
-            at=pl.multiple_of(i*cb,cb)
-            forward_head(h,qkv,at,qkv,width,2*width,0,K,ctx_bias,p_ctx,at,mixed,at,cb)
-        forward_head(h,qkv,C,qkv,width,2*width,C,K,None,p_prompt,0,mixed,C,Pn)
-        forward_head(h,qkv,K,qkv,width,2*width,0,R,own_bias,p_own,0,mixed,K,own)
+    jobs=[]
+    for h in range(HEADS):
+        jobs+=[ctx_job(h,at,cb) for at in range(0,C,cb)]
+        jobs+=[prompt_job(h),own_job(h,qkv,p_main,C,p_local,mixed,inv,slice(K,R))]
+    pipeline(jobs)
     T=block_rows(R,256)
-    @pl.loop(0,R//T)
-    def _(i):
-        rows=pl.ds(pl.multiple_of(i*T,T),T)
-        y,na,ra,sl,nb,rb=tail_forward(X[rows],mixed[rows],0)
-        X1[rows]=y; n1[rows]=na; r1[rows]=ra; slope[rows]=sl; n2[rows]=nb; r2[rows]=rb
+    kept=(n1,r1,slope,n2,r2)
+    def put(rows):
+        def store(y): X1[rows]=y
+        return store
+    pipeline([tail_job(0,(slice(a,a+T),)*3,kept,X,mixed,put(slice(a,a+T))) for a in range(0,R,T)])
     @pl.loop(0,R//B)
     def _(i):
         rows=pl.ds(pl.multiple_of(i*B,B),B)
-        kv1[rows]=mm(X1[rows].astype(bf16),w_qkv[1,:,width:]).astype(bf16)
-    q1[...]=mm(X1[K:R].astype(bf16),w_qkv[1,:,0:width]).astype(bf16)
-    @pl.loop(0,HEADS)
-    def _(h):
-        forward_head(h,q1,0,kv1,0,width,0,R,own_bias,p_own1,0,mixed1,0,own)
-    y,na,ra,sl,nb,rb=tail_forward(X1[K:R],mixed1[...],1)
-    out_rows[...]=y; n1b[...]=na; r1b[...]=ra; slopeb[...]=sl; n2b[...]=nb; r2b[...]=rb
-    g1,gmix=tail_backward(d_out[...],n1b[...],r1b[...],slopeb[...],n2b[...],r2b[...],1)
-    first[K:R]=g1
-    gm[K:R]=gmix
-    dk[...]=jnp.zeros_like(dk); dv[...]=jnp.zeros_like(dv)
-    @pl.loop(0,HEADS)
-    def _(h):
-        backward_head(h,q1,0,kv1,0,width,0,R,p_own1,0,mixed1,0,K,K,own)
+        qkv1[rows]=mm(X1[rows].astype(bf16),w_qkv[1]).astype(bf16)
+    pipeline([own_job(h,qkv1,p_main1,0,p_local1,mixed1,inv1,slice(0,own)) for h in range(HEADS)])
+    kept1=(n1b,r1b,slopeb,n2b,r2b)
+    O=own//2
+    def put_out(rows):
+        def store(y): out_rows[rows]=y
+        return store
+    pipeline([tail_job(1,(slice(K+a,K+a+O),slice(a,a+O),slice(a,a+O)),kept1,X1,mixed1,put_out(slice(a,a+O))) for a in range(0,own,O)])
+    pipeline([tail_back_job(1,slice(0,own),slice(K,R),kept1,lambda: d_out[...],inv1,slice(0,own))])
+    jobs=[]
+    def put_ds(h,main,at,local):
+        def store(d):
+            ds_main[h,at:at+own]=d[0]; ds_local[h]=d[1]
+        return store
+    for h in range(HEADS):
+        jobs.append(backward_job(h,qkv1,slice(0,own),slice(K,R),[(0,K),(K,R)],lambda h=h:[p_main1[h],p_local1[h]],put_ds(h,ds_main,C,ds_local),mixed1))
+    pipeline(jobs)
+    jobs=[]
+    for h in range(HEADS):
+        q=lambda h=h: qkv1[K:R,cols(h)]
+        g=lambda h=h: gm[K:R,cols(h)]
+        jobs+=key_job(h,{1:[(q,lambda h=h: ds_main[h,C:M])],2:[(g,lambda h=h: p_main1[h])]},0,K)
+        jobs+=key_job(h,{1:[(q,lambda h=h: ds_local[h])],2:[(g,lambda h=h: p_local1[h])]},K,own)
+    pipeline(jobs)
+    grads[0:K,0:width]=jnp.zeros((K,width),bf16)
     first[0:K]=jnp.zeros((K,width),f32)
-    first[K:R]+=mm_t(dq[K:R],w_qkv[1,:,0:width])
-    def key_grads(rows,layer):
-        return mm_t((dk[rows]*scale).astype(bf16),w_qkv[layer,:,width:2*width])+mm_t(dv[rows].astype(bf16),w_qkv[layer,:,2*width:])
     @pl.loop(0,R//B)
     def _(i):
         rows=pl.ds(pl.multiple_of(i*B,B),B)
-        first[rows]+=key_grads(rows,1)
-    @pl.loop(0,R//T)
-    def _(i):
-        rows=pl.ds(pl.multiple_of(i*T,T),T)
-        g1,gmix=tail_backward(first[rows],n1[rows],r1[rows],slope[rows],n2[rows],r2[rows],0)
-        first[rows]=g1; gm[rows]=gmix
-    dk[...]=jnp.zeros_like(dk); dv[...]=jnp.zeros_like(dv)
-    @pl.loop(0,HEADS)
-    def _(h):
-        @pl.loop(0,C//cb)
-        def _(i):
-            at=pl.multiple_of(i*cb,cb)
-            backward_head(h,qkv,at,qkv,width,2*width,0,K,p_ctx,at,mixed,at,at,at,cb)
-        backward_head(h,qkv,C,qkv,width,2*width,C,K,p_prompt,0,mixed,C,C,C,Pn)
-        backward_head(h,qkv,K,qkv,width,2*width,0,R,p_own,0,mixed,K,K,K,own)
+        first[rows]+=mm_t(grads[rows],w_qkv[1])
+    def take(rows): return lambda: first[rows]
+    pipeline([tail_back_job(0,slice(a,a+T),slice(a,a+T),kept,take(slice(a,a+T)),inv,slice(a,a+T)) for a in range(0,R,T)])
+    jobs=[]
+    def put_ctx(h,at):
+        def store(d): ds_main[h,at:at+cb]=d[0]
+        return store
+    def put_prompt(h):
+        def store(d): ds_prompt[h]=d[0]
+        return store
+    for h in range(HEADS):
+        for at in range(0,C,cb):
+            jobs.append(backward_job(h,qkv,slice(Pn+at,Pn+at+cb),slice(Pn+at,Pn+at+cb),[(0,K)],lambda h=h,at=at:[p_main[h,at:at+cb]],put_ctx(h,at),mixed))
+        jobs.append(backward_job(h,qkv,slice(0,Pn),slice(0,Pn),[(0,Pn)],lambda h=h:[p_prompt[h]],put_prompt(h),mixed))
+        jobs.append(backward_job(h,qkv,slice(K,R),slice(K,R),[(0,K),(K,R)],lambda h=h:[p_main[h,C:M],p_local[h]],put_ds(h,ds_main,C,ds_local),mixed))
+    pipeline(jobs)
+    jobs=[]
+    for h in range(HEADS):
+        def part(act,c): return lambda lo,hi: (lambda: act[lo:hi,c])
+        q=part(qkv,cols(h)); g=part(gm,cols(h))
+        jobs+=key_job(h,{1:[(q(Pn,R),lambda h=h: ds_main[h,:,0:Pn]),(q(0,Pn),lambda h=h: ds_prompt[h])],2:[(g(Pn,R),lambda h=h: p_main[h,:,0:Pn]),(g(0,Pn),lambda h=h: p_prompt[h])]},0,Pn)
+        jobs+=key_job(h,{1:[(q(Pn,R),lambda h=h: ds_main[h,:,Pn:K])],2:[(g(Pn,R),lambda h=h: p_main[h,:,Pn:K])]},Pn,C)
+        jobs+=key_job(h,{1:[(q(K,R),lambda h=h: ds_local[h])],2:[(g(K,R),lambda h=h: p_local[h])]},K,own)
+    pipeline(jobs)
     @pl.loop(0,R//B)
     def _(i):
         rows=pl.ds(pl.multiple_of(i*B,B),B)
-        first[rows]+=mm_t(dq[rows],w_qkv[0,:,0:width])+key_grads(rows,0)
-    g_ctx[...]=first[0:C]
-    g_prompt[...]=first[C:K]
+        first[rows]+=mm_t(grads[rows],w_qkv[0])
+    g_prompt[...]=first[0:Pn]
+    g_ctx[...]=first[Pn:K]
     g_own[...]=first[K:R]
-    def over(lo,hi):
-        g=first[lo:hi]
-        return jnp.sum(g,axis=0,keepdims=True),jnp.sum(g*X[lo:hi],axis=0,keepdims=True)
-    a,b=over(0,C); c,d=over(K,R)
-    sums[0:1]=a+c
-    sums[1:2]=b+d
+    g=first[Pn:R]
+    sums[0:1]=jnp.sum(g,axis=0,keepdims=True)
+    sums[1:2]=jnp.sum(g*X[Pn:R],axis=0,keepdims=True)
 
 def compute(x,segs,kinds,small,ctx,prompt,d_out,w_qkv,w_out,w_up,w_down,ln_gain,ln_bias):
-    own,width=x.shape; C=ctx.shape[0]; Pn=prompt.shape[0]; K=C+Pn; R=K+own
+    own,width=x.shape; C=ctx.shape[0]; Pn=prompt.shape[0]; K=C+Pn; R=K+own; M=C+own
     FF=w_up.shape[2]
     vm=pl.BlockSpec(memory_space=pltpu.VMEM)
     V=pltpu.VMEM
@@ -336,11 +403,11 @@
         out_shape=(S((own,width),f32),S((C,width),f32),S((Pn,width),f32),S((own,width),f32),S((2,width),f32),S((3,width),f32)),
         in_specs=[vm]*13,out_specs=(vm,)*6,
         scratch_shapes=[
-            V((R,width),f32),V((R,width),f32),V((R,3*width),bf16),V((R,2*width),bf16),V((own,width),bf16),V((R,width),f32),V((own,width),f32),
-            V((HEADS,C,K),bf16),V((HEADS,Pn,Pn),bf16),V((HEADS,own,R),bf16),V((HEADS,own,R),bf16),
+            V((R,width),f32),V((R,width),f32),V((R,3*width),bf16),V((R,3*width),bf16),V((R,width),f32),V((own,width),f32),V((R,width),f32),V((own,width),f32),
+            V((HEADS,M,K),bf16),V((HEADS,Pn,Pn),bf16),V((HEADS,own,own),bf16),V((HEADS,own,K),bf16),V((HEADS,own,own),bf16),
             V((R,width),f32),V((R,1),f32),V((R,FF),f32),V((R,width),f32),V((R,1),f32),
             V((own,width),f32),V((own,1),f32),V((own,FF),f32),V((own,width),f32),V((own,1),f32),
-            V((R,width),f32),V((R,width),bf16),V((R,width),bf16),V((R,width),f32),V((R,width),f32),
+            V((R,width),f32),V((R,width),bf16),V((R,3*width),bf16),V((HEADS,M,K),bf16),V((HEADS,own,own),bf16),V((HEADS,Pn,Pn),bf16),V((own,R),f32),
         ],
         compiler_params=pltpu.CompilerParams(vmem_limit_bytes=60*2**20),
         name="layers",

time: 106 us -> 92.2 us (0.87)
  Pallas kernels: 93.4 us -> 80.1 us
    pallas_call x1, Pallas kernels: 51.1 us -> 37.7 us  [compute(): pl.pallas_call(compute_kernel, out_shape=(S((own, width), f32), S((C, wid...]
where the time goes in v2:
time: 92.2 us; the launch traced here: 91.9 us
  Pallas kernels  80.1 us (87%)
  local copies, waits for them, and re-layouts  7.96 us (9%)
  other arithmetic  3.08 us (3%)
    pallas_call x1, Pallas kernels, compute(): pl.pallas_call(compute_kernel, out_shape=(S((own, width), f32), S((C, wid...  37.7 us
    pallas_call x1, Pallas kernels, gather(): pl.pallas_call(functools.partial(gather_kernel, groups, seq), out_shape=(...  25.4 us
    pallas_call x1, Pallas kernels, reduce(): pl.pallas_call(functools.partial(reduce_kernel, groups, seq), out_shape=(...  16.9 us
    unnamed x24, local copies, waits for them, and re-layouts  7.13 us
    mul x1, other arithmetic, per_device(): spread * (grad - usable / count * (grad_sum + normed * grad_dot))  2.04 us

profile of v2, /device:TPU:0, one launch (start us, length us, event | category | flops | bytes accessed | tf_op | source)
XLA Modules:
  0.0 91.9 jit_solution(12244282944173620396)
XLA Ops:
  0.6 0.0 copy-start
  0.6 1.0 %copy-done = f32[256,512]{1,0:T(8,128)S(1)} copy-done((f32[256,512]{1,0:T(8,128)S(1)}, f32[256,512]{1,0:T(8,128)}, u32[]{:S(2)}) %copy-start) | copy-done | bytes 524312
  1.7 0.7 copy-done.5
  2.4 0.7 copy-done.7
  3.0 0.7 copy-done.9
  3.7 25.4 %gather_context.1 = (f32[4,2,2,32,512]{4,3,2,1,0:T(8,128)S(1)}, f32[2,2,2,16,128]{4,3,2,1,0:T(8,128)S(1)}, bf16[2,2,2,4,16,128]{5,4,3,2,1,0:T(8,128)(2,1)S(1)}) custom-call(f32[256,512]{1,0:T(8,128)S(1)} %copy-done, s32[1,256]{1,0:T(1,128)S(1)} %bitcast.39, s32[1,256]{1,0:T(1,128)S(1)} %bitcast.41, bf16[4,512]{1,0:T(4,128)(2,1)S(1)} %copy-done.9), custom_call_target="tpu_custom_call" | custom-call | tf_op jit(solution)/shard_map/gather_context/pallas_call | solution.py:131
  29.1 0.0 copy-start.2
  29.1 1.0 %copy-done.2 = f32[4,2,2,32,512]{4,3,2,1,0:T(8,128)} copy-done((f32[4,2,2,32,512]{4,3,2,1,0:T(8,128)}, f32[4,2,2,32,512]{4,3,2,1,0:T(8,128)S(1)}, u32[]{:S(2)}) %copy-start.2) | copy-done | bytes 1048600
  30.1 0.1 copy.14
  30.1 0.6 copy-done.4
  30.7 0.7 copy.19
  31.4 37.7 %layers.1 = (f32[256,512]{1,0:T(8,128)}, f32[512,512]{1,0:T(8,128)}, f32[128,512]{1,0:T(8,128)}, f32[256,512]{1,0:T(8,128)}, f32[2,512]{1,0:T(2,128)}, /*index=5*/f32[3,512]{1,0:T(4,128)}) custom-call(f32[256,512]{1,0:T(8,128)} %x.3, s32[1,256]{1,0:T(1,128)} %bitcast.38, s32[1,256]{1,0:T(1,128)} %bitcast.40, f32[8,16,128]{2,1,0:T(8,128)} %bitcast.37, ...), custom_call_target="tpu_custom_call" | custom-call | tf_op jit(solution)/shard_map/layers/pallas_call | solution.py:401
  69.1 0.0 copy-start.6
  69.1 0.0 copy-start.8
  69.1 0.0 copy-start.1
  69.2 1.0 %convert_element_type.6 = bf16[128,512]{1,0:T(8,128)(2,1)S(1)} convert(f32[128,512]{1,0:T(8,128)} %get-tuple-element.22) | non-fusion elementwise | flops 65536 | bytes 393216 | tf_op jit(solution)/shard_map/convert_element_type | solution.py:606
  70.2 0.1 copy.15
  70.3 0.7 reshape.60.sums
  71.0 1.2 %copy-done.3 = f32[512,512]{1,0:T(8,128)S(1)} copy-done((f32[512,512]{1,0:T(8,128)S(1)}, f32[512,512]{1,0:T(8,128)}, u32[]{:S(2)}) %copy-start.3) | copy-done | bytes 1048600
  72.2 16.9 %reduce_gradients.1 = (f32[32,512]{1,0:T(8,128)S(1)}, f32[16,128]{1,0:T(8,128)S(1)}, f32[8,128]{1,0:T(8,128)S(1)}) custom-call(f32[4,2,2,32,512]{4,3,2,1,0:T(8,128)S(1)} %bitcast.34, bf16[2,2,2,4,16,128]{5,4,3,2,1,0:T(8,128)(2,1)S(1)} %bitcast.35, f32[8,128]{1,0:T(8,128)S(1)} %reshape.60.sums), custom_call_target="tpu_custom_call" | custom-call | tf_op jit(solution)/shard_map/reduce_gradients/pallas_call | solution.py:514
  89.2 0.0 copy-done.10
  89.2 0.0 copy-done.6
  89.2 2.0 %fusion.1 = f32[256,512]{1,0:T(8,128)} fusion(f32[256,512]{1,0:T(8,128)} %get-tuple-element.20, f32[256,512]{1,0:T(8,128)S(1)} %copy-done.1, f32[512]{0:T(512)S(1)} %get-tuple-element.31, f32[512]{0:T(512)S(1)} %bitcast.46, f32[512]{0:T(512)S(1)} %get-tuple-element.30, f32[512]{0:T(512)S(1)} %bitcast.47, f32[256]{0:T(256)S(1)} %get-tuple-element.33, ...), kind=kLoop, calls=%fused_computation.2 | loop fusion | flops 1310720 | bytes 1649920 | tf_op jit(solution)/shard_map/mul | solution.py:615
  91.3 0.6 copy.21
  (12 shorter events, 0.1 us)
Async XLA Ops:
  0.6 1.0 %copy-start = (f32[256,512]{1,0:T(8,128)S(1)}, f32[256,512]{1,0:T(8,128)}, u32[]{:S(2)}) copy-start(f32[256,512]{1,0:T(8,128)} %x.3) | copy-start | bytes 1572868
  1.7 0.7 copy-start.5
  2.4 0.7 copy-start.7
  3.0 0.7 copy-start.9
  29.1 1.0 %copy-start.2 = (f32[4,2,2,32,512]{4,3,2,1,0:T(8,128)}, f32[4,2,2,32,512]{4,3,2,1,0:T(8,128)S(1)}, u32[]{:S(2)}) copy-start(f32[4,2,2,32,512]{4,3,2,1,0:T(8,128)S(1)} %get-tuple-element.16) | copy-start | bytes 3145732
  30.1 0.6 copy-start.4
  69.1 20.0 %copy-start.10 = (f32[3,512]{1,0:T(4,128)S(1)}, f32[3,512]{1,0:T(4,128)}, u32[]{:S(2)}) copy-start(f32[3,512]{1,0:T(4,128)} %get-tuple-element.19) | copy-start | bytes 18436
  69.1 20.1 %copy-start.6 = (s32[256]{0:T(256)S(1)}, s32[256]{0:T(256)}, u32[]{:S(2)}) copy-start(s32[256]{0:T(256)} %param.12) | copy-start | bytes 3076
  69.1 20.1 %copy-start.8 = (s32[256]{0:T(256)S(1)}, s32[256]{0:T(256)}, u32[]{:S(2)}) copy-start(s32[256]{0:T(256)} %param.13) | copy-start | bytes 3076
  69.1 20.1 %copy-start.1 = (f32[256,512]{1,0:T(8,128)S(1)}, f32[256,512]{1,0:T(8,128)}, u32[]{:S(2)}) copy-start(f32[256,512]{1,0:T(8,128)} %x.3) | copy-start | bytes 1572868
  71.0 1.2 %copy-start.3 = (f32[512,512]{1,0:T(8,128)S(1)}, f32[512,512]{1,0:T(8,128)}, u32[]{:S(2)}) copy-start(f32[512,512]{1,0:T(8,128)} %get-tuple-element.21) | copy-start | bytes 3145732

commit v3 on v0

v3 whole, which is shorter than its diff:
```python
import functools
from types import SimpleNamespace as Namespace

import jax
import jax.numpy as jnp
from jax import lax
from jax.experimental import pallas as pl
from jax.experimental.pallas import tpu as pltpu
from jax.sharding import PartitionSpec as P

HEADS = 4
epsilon = 1e-05
masked_score = -1e30
inverse_root_two = 0.7071067811865476
inverse_root_two_pi = 0.3989422804014327
log2_e = 1.4426950408889634
absent = 1e9
STRIDE = 8
MESH = pl.DeviceIdType.MESH
f32 = jnp.float32
bf16 = jnp.bfloat16


def mm(a, b):
    return jnp.dot(a, b, preferred_element_type=f32)


def mm_t(a, b):
    return lax.dot_general(a, b, (((1,), (1,)), ((), ())), preferred_element_type=f32)


def t_mm(a, b):
    return lax.dot_general(a, b, (((0,), (0,)), ((), ())), preferred_element_type=f32)


def row_mean(a):
    return jnp.mean(a, axis=-1, keepdims=True)


def total_of(terms):
    return functools.reduce(jnp.add, terms)


def normalize(z):
    center = z - row_mean(z)
    scale = lax.rsqrt(row_mean(center * center) + epsilon)
    return center * scale, scale


def normalize_backward(normal, scale, gain, grad):
    upstream = grad * gain
    return scale * (upstream - row_mean(upstream) - normal * row_mean(upstream * normal))


def seq_dims(n):
    return {16: (4, 2, 2), 32: (2, 4, 4)}.get(n, (n, 1, 1))


def partner(at, d, size):
    out = at
    bit = 1
    while bit < size:
        if d & bit:
            out = out + bit - 2 * bit * ((at // bit) % 2)
        bit *= 2
    return out


class Net:
    def __init__(self, groups, seq):
        self.groups = groups
        self.dims = Z, Y, X = seq_dims(seq)
        self.g = lax.axis_index("group")
        s = lax.axis_index("seq")
        self.z, self.y, self.x = s // (Y * X), (s // X) % Y, s % X

    def device(self, z=None, y=None, x=None, g=None):
        Z, Y, X = self.dims
        z = self.z if z is None else z
        y = self.y if y is None else y
        x = self.x if x is None else x
        return (self.g if g is None else g, (z * Y + y) * X + x)

    def plane(self):
        Z, Y, X = self.dims
        at = (self.g * Y + self.y) * X + self.x
        out = []
        for d in range(1, self.groups * Y * X):
            q = partner(at, d, self.groups * Y * X)
            out.append(dict(g=q // (Y * X), y=(q // X) % Y, x=q % X))
        return out


def pipeline(jobs):
    state = [Namespace() for _ in jobs]
    longest = max(len(j) for j in jobs)
    for step in range(len(jobs) + longest - 1):
        now = [
            (state[j],) + jobs[j][step - j] for j in range(len(jobs)) if 0 <= step - j < len(jobs[j])
        ]
        for want in "mv":
            for s, kind, stage in reversed(now):
                if kind == want:
                    stage(s)


def narrow(rows):
    return jnp.concatenate([rows[:, i : i + 128] for i in range(0, rows.shape[1], 128)], axis=0)


def layers_kernel(groups, seq, names, *refs):
    r = Namespace(**dict(zip(names, refs)))
    net = Net(groups, seq)
    Z, Y, X = net.dims
    own, width = r.x.shape
    C, Pn = seq * (own // STRIDE), r.prompts.shape[0] // 4
    block = own // STRIDE
    K, R, M = C + Pn, C + Pn + own, C + own
    E = width // HEADS
    lanes = width // 128
    per = r.prompt_rows.shape[0]
    devices = groups * seq
    scale = E**-0.5
    half = width // 2
    middle = 3 * net.g + 1
    w_qkv, w_out, w_up, w_down = r.w_qkv, r.w_out, r.w_up, r.w_down
    ln_gain, ln_bias = r.ln_gain, r.ln_bias

    def local(src, dst, sem):
        c = pltpu.make_async_copy(src, dst, sem)
        c.start()
        return c

    early = [
        local(r.x_in, r.x, r.load_sem.at[0]),
        local(r.segs_in, r.segs, r.load_sem.at[1]),
        local(r.kinds_in, r.kinds, r.load_sem.at[2]),
    ]
    plane = net.plane()
    zs = [partner(net.z, d, Z) for d in range(1, Z)]
    barrier = pltpu.get_barrier_semaphore()
    for q in zs:
        pl.semaphore_signal(barrier, inc=1, device_id=net.device(z=q), device_id_type=MESH)
    for q in plane:
        pl.semaphore_signal(barrier, inc=1, device_id=net.device(**q), device_id_type=MESH)
    late = local(r.d_out_in, r.d_out, r.load_sem.at[3])
    stored = ((r.w_qkv_in, w_qkv), (r.w_out_in, w_out), (r.w_up_in, w_up), (r.w_down_in, w_down))
    weights = [
        [local(src.at[n], dst.at[n], r.weight_sem.at[n, i]) for i, (src, dst) in enumerate(stored)]
        for n in range(2)
    ]
    norms = [
        local(r.ln_gain_in, ln_gain, r.load_sem.at[4]),
        local(r.ln_bias_in, ln_bias, r.load_sem.at[5]),
    ]

    pending = []

    def remote(src, dst, sems, at, dev):
        c = pltpu.make_async_remote_copy(
            src_ref=src,
            dst_ref=dst,
            send_sem=sems.at[(0,) + at],
            recv_sem=sems.at[(1,) + at],
            device_id=dev,
            device_id_type=MESH,
        )
        c.start()
        pending.append(c)

    def arrived(dst, sems, at, dev):
        pltpu.make_async_remote_copy(
            src_ref=dst,
            dst_ref=dst,
            send_sem=sems.at[(0,) + at],
            recv_sem=sems.at[(1,) + at],
            device_id=dev,
            device_id_type=MESH,
        ).wait_recv()

    for c in early:
        c.wait()
    eye = lax.broadcasted_iota(jnp.int32, (own, own), 0) == lax.broadcasted_iota(jnp.int32, (own, own), 1)

    def column(lane):
        return jnp.max(jnp.where(eye, lane, -9), axis=1, keepdims=True)

    seg, kind = r.segs[...], r.kinds[...]
    usable = (column(kind) != 2).astype(f32)
    chosen = column(jnp.where((kind == 0) & (seg == middle), 1, 0)).astype(f32)
    rows = r.x[...]
    picked = jnp.sum((rows * chosen).reshape(block, STRIDE, width), axis=1)
    held = jnp.sum(jnp.broadcast_to(chosen, (own, width)).reshape(block, STRIDE, width), axis=1)
    ctx = r.ctx
    weighed = rows * usable
    small_own = r.small_own
    small_own[0:lanes] = narrow(jnp.sum(weighed, axis=0, keepdims=True))
    small_own[lanes : 2 * lanes] = narrow(jnp.sum(weighed * rows, axis=0, keepdims=True))
    small_own[2 * lanes : 4 * lanes] = jnp.broadcast_to(jnp.sum(usable), (2 * lanes, 128))
    r.ctx_own[...] = jnp.where(held > 0.5, picked, absent)
    r.prompt_own[...] = narrow(r.prompt_rows[...].astype(f32)).astype(bf16)
    place = local(r.ctx_own, ctx.at[net.z, net.y, net.x], r.load_sem.at[6])
    prompt_blocks = r.prompt_blocks
    prompt_at = (net.g, net.y, net.x, net.z)
    place_prompt = local(r.prompt_own, prompt_blocks.at[prompt_at], r.load_sem.at[7])

    pl.semaphore_wait(barrier, len(zs) + len(plane))
    for i, q in enumerate(zs):
        remote(small_own, r.small_z.at[i], r.zsmall, (0, i), net.device(z=q))
    for i, q in enumerate(zs):
        remote(r.prompt_own, prompt_blocks.at[prompt_at], r.zsmall, (1, i), net.device(z=q))
    xs = [partner(net.x, d, X) for d in range(1, X)]
    ys = [partner(net.y, d, Y) for d in range(1, Y)]
    levels = [net.z] + zs

    def spread_block(src, z, d):
        for i, q in enumerate(xs):
            remote(src, ctx.at[z, net.y, net.x], r.xctx, (d, i), net.device(x=q))
        for i, q in enumerate(ys):
            remote(src, ctx.at[z, net.y, net.x], r.yctx, (d, i), net.device(y=q))

    for i, q in enumerate(zs):
        remote(r.ctx_own, ctx.at[net.z, net.y, net.x], r.zctx, (i,), net.device(z=q))
    spread_block(r.ctx_own, net.z, 0)
    for i, q in enumerate(zs):
        arrived(r.small_z.at[i], r.zsmall, (0, i), net.device(z=q))
    small = r.small
    small[0] = total_of([small_own[...]] + [r.small_z[i] for i in range(Z - 1)])
    for i, q in enumerate(plane):
        remote(small.at[0], small.at[i + 1], r.psmall, (0, i), net.device(**q))
    place_prompt.wait()
    for i, q in enumerate(zs):
        arrived(prompt_blocks.at[net.g, net.y, net.x, q], r.zsmall, (1, i), net.device(z=q))
    for i, q in enumerate(plane):
        mine = prompt_blocks.at[net.g, net.y, net.x]
        remote(mine, mine, r.psmall, (1, i), net.device(**q))
    for i, q in enumerate(zs):
        arrived(ctx.at[q, net.y, net.x], r.zctx, (i,), net.device(z=q))
        spread_block(ctx.at[q, net.y, net.x], q, i + 1)

    for i, q in enumerate(plane):
        arrived(small.at[i + 1], r.psmall, (0, i), net.device(**q))
    total = total_of([small[i] for i in range(len(plane) + 1)])

    def wide(part):
        return jnp.concatenate([part[i : i + 1] for i in range(lanes)], axis=1)

    count = total[2 * lanes : 2 * lanes + 1, 0:1]
    mean = wide(total[0:lanes]) / count
    second = wide(total[lanes : 2 * lanes]) / count
    spread = lax.rsqrt(second - mean * mean + epsilon)
    Xs = r.X
    Xs[K:R] = (r.x[...] - mean) * spread
    qkv = r.qkv
    weights[0][0].wait()
    qkv[K:R] = mm(Xs[K:R].astype(bf16), w_qkv[0]).astype(bf16)

    def forward_blocks(d):
        z = levels[d]
        for i, q in enumerate(xs):
            arrived(ctx.at[z, net.y, q], r.xctx, (d, i), net.device(x=q))
            view = ctx.at[z, net.y, q, :, pl.ds(0, half)]
            for j, t in enumerate(ys):
                remote(view, view, r.ydiag, (d, i, j), net.device(y=t))
        for i, q in enumerate(ys):
            arrived(ctx.at[z, q, net.x], r.yctx, (d, i), net.device(y=q))
            view = ctx.at[z, q, net.x, :, pl.ds(half, half)]
            for j, t in enumerate(xs):
                remote(view, view, r.xdiag, (d, i, j), net.device(x=t))

    for d in range(Z // 2):
        forward_blocks(d)

    for i, q in enumerate(plane):
        arrived(prompt_blocks.at[q["g"], q["y"], q["x"]], r.psmall, (1, i), net.device(**q))
    prompts = r.prompts
    prompts[...] = prompt_blocks[...].astype(f32).reshape(prompts.shape)
    for c in range(lanes):
        for i in range(per):
            Xs[i * devices : (i + 1) * devices, c * 128 : (c + 1) * 128] = prompts[
                pl.ds(c * per + i, devices, stride=lanes * per)
            ]
    qkv[0:Pn] = mm(Xs[0:Pn].astype(bf16), w_qkv[0]).astype(bf16)
    for d in range(Z // 2, Z):
        forward_blocks(d)

    def cols(h, part=0):
        return slice(part * width + h * E, part * width + (h + 1) * E)

    def weights_of(raw, bias):
        if bias is None:
            highest = jnp.max(raw, axis=-1, keepdims=True)
            e = jnp.exp2((raw - highest) * (scale * log2_e))
        else:
            highest = jnp.max(raw + bias, axis=-1, keepdims=True)
            e = jnp.exp2((raw - highest) * (scale * log2_e) + bias)
        return e.astype(bf16), 1.0 / jnp.sum(e, axis=-1, keepdims=True)

    def forward_job(h, act, rows, out, keys, exponentials, store, m_ref, inv_ref):
        lo, hi = keys

        def scores(s):
            s.raw = mm_t(act[rows, cols(h)], act[lo:hi, cols(h, 1)])

        def weigh(s):
            s.p, s.inv = exponentials(s.raw)
            store(s.p)

        def mix(s):
            s.mix = mm(s.p, act[lo:hi, cols(h, 2)])

        def keep(s):
            inv = jnp.broadcast_to(s.inv, s.mix.shape)
            m_ref[out, cols(h)] = s.mix * inv
            inv_ref[out, cols(h)] = inv

        return [("m", scores), ("v", weigh), ("m", mix), ("v", keep)]

    def tail_job(layer, rows, kept, x_ref, m_ref, store):
        na, ra, sl, nb, rb = kept
        xr, mr, kr = rows

        def attended(s):
            s.a = mm(m_ref[mr].astype(bf16), w_out[layer])

        def first_norm(s):
            n, q = normalize(x_ref[xr] + s.a)
            na[kr] = n
            ra[kr] = q
            s.h = n * ln_gain[layer, 0:1] + ln_bias[layer, 0:1]
            s.hb = s.h.astype(bf16)

        def up(s):
            s.u = mm(s.hb, w_up[layer])

        def gelu(s):
            u = s.u
            phi = 0.5 * (1.0 + lax.erf(u * inverse_root_two))
            s.act = (u * phi).astype(bf16)
            sl[kr] = phi + u * jnp.exp2(u * u * (-0.5 * log2_e)) * inverse_root_two_pi

        def down(s):
            s.d = mm(s.act, w_down[layer])

        def second_norm(s):
            n, q = normalize(s.h + s.d)
            nb[kr] = n
            rb[kr] = q
            store(n * ln_gain[layer, 1:2] + ln_bias[layer, 1:2])

        return [("m", attended), ("v", first_norm), ("m", up), ("v", gelu), ("m", down), ("v", second_norm)]

    first, gm, grads = r.first, r.gm, r.grads

    def tail_back_job(layer, kr, rows, kept, load, inv_ref, ir):
        na, ra, sl, nb, rb = kept

        def second_norm(s):
            s.g2 = normalize_backward(nb[kr], rb[kr], ln_gain[layer, 1:2], load())
            s.g2b = s.g2.astype(bf16)

        def down(s):
            s.ga = mm_t(s.g2b, w_down[layer])

        def gelu(s):
            s.ge = (s.ga * sl[kr]).astype(bf16)

        def up(s):
            s.gh = mm_t(s.ge, w_up[layer])

        def first_norm(s):
            g1 = normalize_backward(na[kr], ra[kr], ln_gain[layer, 0:1], s.g2 + s.gh)
            first[rows] = g1
            s.g1b = g1.astype(bf16)

        def out(s):
            s.gm = mm_t(s.g1b, w_out[layer])

        def keep(s):
            gm[rows] = (s.gm.astype(bf16).astype(f32) * inv_ref[ir]).astype(bf16)

        return [
            ("v", second_norm),
            ("m", down),
            ("v", gelu),
            ("m", up),
            ("v", first_norm),
            ("m", out),
            ("v", keep),
        ]

    def backward_job(h, act, rows, out, keys, load, store, m_ref):
        lo, hi = keys

        def products(s):
            g = gm[out, cols(h)]
            s.dp = mm_t(g, act[lo:hi, cols(h, 2)])

        def scores(s):
            shift = jnp.sum(gm[out, cols(h)].astype(f32) * m_ref[rows, cols(h)], axis=-1, keepdims=True)
            s.ds = (load().astype(f32) * (s.dp - shift)).astype(bf16)
            store(s.ds)

        def queries(s):
            s.dq = mm(s.ds, act[lo:hi, cols(h, 1)])

        def keep(s):
            grads[out, cols(h)] = (s.dq * scale).astype(bf16)

        return [("m", products), ("v", scores), ("m", queries), ("v", keep)]

    def key_jobs(h, key_terms, value_terms, at, n):
        out = []
        for part, terms, factor in ((1, key_terms, scale), (2, value_terms, 1.0)):

            def product(s, terms=terms):
                s.t = total_of([t_mm(a(), b()) for a, b in terms])

            def keep(s, part=part, factor=factor):
                grads[at : at + n, cols(h, part)] = (s.t * factor).astype(bf16).T

            out.append([("m", product), ("v", keep)])
        return out

    p_main, p_prompt, p_local = r.p_main, r.p_prompt, r.p_local
    p_main1, p_local1 = r.p_main1, r.p_local1
    mixed, inv, mixed1, inv1 = r.mixed, r.inv, r.mixed1, r.inv1
    ds_main, ds_local, ds_prompt = r.ds_main, r.ds_local, r.ds_prompt
    kept = (r.n1, r.r1, r.slope, r.n2, r.r2)
    kept1 = (r.n1b, r.r1b, r.slopeb, r.n2b, r.r2b)
    X1, qkv1, bias = r.X1, r.qkv1, r.bias

    def put(ref, rows):
        def store(y):
            ref[rows] = y

        return store

    def prompt_job(h):
        def store(p):
            p_prompt[h] = p

        rows = slice(0, Pn)
        return forward_job(h, qkv, rows, rows, (0, Pn), lambda raw: weights_of(raw, None), store, mixed, inv)

    pipeline([prompt_job(h) for h in range(HEADS)])
    for c in weights[0][1:]:
        c.wait()
    for c in norms:
        c.wait()
    pipeline([tail_job(0, (slice(0, Pn),) * 3, kept, Xs, mixed, put(X1, slice(0, Pn)))])

    place.wait()
    for d in range(Z):
        z = levels[d]
        for i, q in enumerate(ys):
            for j, t in enumerate(xs):
                arrived(ctx.at[z, q, t, :, pl.ds(0, half)], r.ydiag, (d, j, i), net.device(y=q))
                arrived(ctx.at[z, q, t, :, pl.ds(half, half)], r.xdiag, (d, i, j), net.device(x=t))
    raw = ctx[...].reshape(C, width)
    present = jnp.abs(raw[:, 0:1]) < 0.5 * absent
    Xs[Pn:K] = jnp.where(present, (raw - mean) * spread, 0.0)
    qkv[Pn:K] = mm(Xs[Pn:K].astype(bf16), w_qkv[0]).astype(bf16)
    square = lax.broadcasted_iota(jnp.int32, (128, 128), 0) == lax.broadcasted_iota(jnp.int32, (128, 128), 1)
    ctx_key = jnp.concatenate(
        [
            jnp.max(jnp.where(square & present[i : i + 128], middle, -1), axis=0, keepdims=True)
            for i in range(0, C, 128)
        ],
        axis=1,
    )
    ctx_bias = jnp.concatenate([jnp.zeros((1, Pn), f32), jnp.where(ctx_key == middle, 0.0, masked_score)], axis=1)
    query = column(jnp.where(kind == 2, -2, seg))
    own_key = jnp.where((kind == 0) & (seg != middle), seg, -1)
    allowed = jnp.concatenate([jnp.ones((own, Pn), jnp.bool_), query == ctx_key, query == own_key], axis=1)
    bias[...] = jnp.where(allowed, 0.0, masked_score)

    def ctx_job(h, at, n):
        def store(p):
            p_main[h, at : at + n] = p

        def exponentials(raw):
            lo, hi = Pn + 128, K - 128
            ends = [raw[:, Pn:lo] + ctx_bias[:, Pn:lo], raw[:, hi:K] + ctx_bias[:, hi:K]]
            return weights_of(jnp.concatenate([raw[:, :Pn], ends[0], raw[:, lo:hi], ends[1]], axis=1), None)

        rows = slice(Pn + at, Pn + at + n)
        return forward_job(h, qkv, rows, rows, (0, K), exponentials, store, mixed, inv)

    def own_job(h, act, main, at, near, m_ref, inv_ref, out):
        def store(p):
            main[h, at : at + own] = p[:, 0:K]
            near[h] = p[:, K:R]

        return forward_job(
            h, act, slice(K, R), out, (0, R), lambda raw: weights_of(raw, bias[...]), store, m_ref, inv_ref
        )

    part = 256
    jobs = []
    for h in range(HEADS):
        jobs += [ctx_job(h, at, part) for at in range(0, C, part)]
        jobs += [own_job(h, qkv, p_main, C, p_local, mixed, inv, slice(K, R))]
    pipeline(jobs)
    pieces = [slice(a, a + part) for a in range(Pn, R, part)]
    pipeline([tail_job(0, (a, a, a), kept, Xs, mixed, put(X1, a)) for a in pieces])

    weights[1][0].wait()
    step = R // 2

    @pl.loop(0, R // step)
    def _(i):
        a = pl.ds(pl.multiple_of(i * step, step), step)
        qkv1[a, width:] = mm(X1[a].astype(bf16), w_qkv[1, :, width:]).astype(bf16)

    qkv1[K:R, 0:width] = mm(X1[K:R].astype(bf16), w_qkv[1, :, 0:width]).astype(bf16)

    whole = slice(0, own)
    pipeline([own_job(h, qkv1, p_main1, 0, p_local1, mixed1, inv1, whole) for h in range(HEADS)])
    for c in weights[1][1:]:
        c.wait()
    late.wait()
    quarter = own // 2
    pipeline(
        [
            tail_job(
                1,
                (slice(K + a, K + a + quarter), slice(a, a + quarter), slice(a, a + quarter)),
                kept1,
                X1,
                mixed1,
                put(r.out_rows, slice(a, a + quarter)),
            )
            for a in range(0, own, quarter)
        ]
    )

    pipeline([tail_back_job(1, whole, slice(K, R), kept1, lambda: r.d_out[...], inv1, whole)])

    def put_ds(h):
        def store(d):
            ds_main[h, C:M] = d[:, 0:K]
            ds_local[h] = d[:, K:R]

        return store

    pipeline(
        [
            backward_job(
                h,
                qkv1,
                whole,
                slice(K, R),
                (0, R),
                lambda h=h: jnp.concatenate([p_main1[h], p_local1[h]], axis=1),
                put_ds(h),
                mixed1,
            )
            for h in range(HEADS)
        ]
    )
    jobs = []
    for h in range(HEADS):
        q = lambda h=h: qkv1[K:R, cols(h)]
        g = lambda h=h: gm[K:R, cols(h)]
        jobs += key_jobs(h, [(q, lambda h=h: ds_main[h, C:M])], [(g, lambda h=h: p_main1[h])], 0, K)
        jobs += key_jobs(h, [(q, lambda h=h: ds_local[h])], [(g, lambda h=h: p_local1[h])], K, own)
    pipeline(jobs)
    first[0:K] = mm_t(grads[0:K, width:], w_qkv[1, :, width:])
    first[K:R] += mm_t(grads[K:R], w_qkv[1])

    def take(rows):
        return lambda: first[rows]

    piece = R // 4
    pieces = [slice(a, a + piece) for a in range(0, R, piece)]
    pipeline([tail_back_job(0, a, a, kept, take(a), inv, a) for a in pieces])
    jobs = []

    def put_ctx(h, at):
        def store(d):
            ds_main[h, at : at + part] = d

        return store

    def put_prompt(h):
        def store(d):
            ds_prompt[h] = d

        return store

    for h in range(HEADS):
        for at in range(0, C, part):
            a = slice(Pn + at, Pn + at + part)
            jobs.append(
                backward_job(
                    h, qkv, a, a, (0, K), lambda h=h, at=at: p_main[h, at : at + part], put_ctx(h, at), mixed
                )
            )
        a = slice(0, Pn)
        jobs.append(backward_job(h, qkv, a, a, (0, Pn), lambda h=h: p_prompt[h], put_prompt(h), mixed))
        a = slice(K, R)
        jobs.append(
            backward_job(
                h,
                qkv,
                a,
                a,
                (0, R),
                lambda h=h: jnp.concatenate([p_main[h, C:M], p_local[h]], axis=1),
                put_ds(h),
                mixed,
            )
        )
    pipeline(jobs)
    jobs = []
    for h in range(HEADS):

        def view(ref, lo, hi, c):
            return lambda: ref[lo:hi, c]

        def piece_of(ref, h, lo, hi):
            return lambda: ref[h, :, lo:hi]

        q = functools.partial(view, qkv, c=cols(h))
        g = functools.partial(view, gm, c=cols(h))
        jobs += key_jobs(
            h,
            [(q(Pn, R), piece_of(ds_main, h, 0, Pn)), (q(0, Pn), piece_of(ds_prompt, h, 0, Pn))],
            [(g(Pn, R), piece_of(p_main, h, 0, Pn)), (g(0, Pn), piece_of(p_prompt, h, 0, Pn))],
            0,
            Pn,
        )
        jobs += key_jobs(
            h,
            [(q(Pn, R), piece_of(ds_main, h, Pn, K))],
            [(g(Pn, R), piece_of(p_main, h, Pn, K))],
            Pn,
            C,
        )
        jobs += key_jobs(
            h,
            [(q(K, R), piece_of(ds_local, h, 0, own))],
            [(g(K, R), piece_of(p_local, h, 0, own))],
            K,
            own,
        )
    pipeline(jobs)

    work = r.work
    order = list(range(Z - 1, -1, -1))

    def context_gradient(lo, hi):
        g = first[Pn:K, lo:hi] + mm_t(grads[Pn:K], w_qkv[0, lo:hi])
        first[Pn:K, lo:hi] = g
        work[:, :, :, :, lo:hi] = g.astype(bf16).reshape(Z, Y, X, block, half)

    context_gradient(0, half)
    for d in order:
        for i, q in enumerate(ys):
            remote(
                work.at[levels[d], q, :, :, pl.ds(0, half)], r.a1.at[i, d], r.first_a, (d, i), net.device(y=q)
            )
    context_gradient(half, width)
    for d in order:
        for i, q in enumerate(xs):
            remote(
                work.at[levels[d], :, q, :, pl.ds(half, half)],
                r.b1.at[i, d],
                r.first_b,
                (d, i),
                net.device(x=q),
            )
    first[0:Pn] += mm_t(grads[0:Pn], w_qkv[0])
    for c in range(lanes):
        for i in range(per):
            prompts[pl.ds(c * per + i, devices, stride=lanes * per)] = first[
                i * devices : (i + 1) * devices, c * 128 : (c + 1) * 128
            ]
    share = r.prompt_share
    share[...] = prompts[...].astype(bf16).reshape(share.shape)
    for i, q in enumerate(plane):
        remote(share.at[q["g"], q["y"], q["x"]], r.share_p.at[i], r.pshare, (0, i), net.device(**q))
    first[K:R] += mm_t(grads[K:R], w_qkv[0])
    g = first[Pn:R]
    sums = r.sums
    sums[0:lanes] = narrow(jnp.sum(g, axis=0, keepdims=True))
    sums[lanes:] = narrow(jnp.sum(g * Xs[Pn:R], axis=0, keepdims=True))
    for i, q in enumerate(plane):
        remote(sums, r.sums_p.at[i], r.pshare, (1, i), net.device(**q))

    a2, b2 = r.a2, r.b2
    a2_own, b2_own, z_own = r.a2_own, r.b2_own, r.z_own
    for d in order:
        z = levels[d]
        t = work[z, net.y, :, :, 0:half].astype(f32)
        for i, q in enumerate(ys):
            arrived(r.a1.at[i, d], r.first_a, (d, i), net.device(y=q))
            t = t + r.a1[i, d].astype(f32)
        a2_own[d] = t.astype(bf16)
        for i, q in enumerate(xs):
            remote(a2_own.at[d, q], a2.at[i, d], r.second_a, (d, i), net.device(x=q))
        t = work[z, :, net.x, :, half:].astype(f32)
        for i, q in enumerate(xs):
            arrived(r.b1.at[i, d], r.first_b, (d, i), net.device(x=q))
            t = t + r.b1[i, d].astype(f32)
        b2_own[d] = t.astype(bf16)
        for i, q in enumerate(ys):
            remote(b2_own.at[d, q], b2.at[i, d], r.second_b, (d, i), net.device(y=q))
    t = share[net.g, net.y, net.x].astype(f32)
    for i, q in enumerate(plane):
        arrived(r.share_p.at[i], r.pshare, (0, i), net.device(**q))
        t = t + r.share_p[i].astype(f32)
    r.share_own[...] = t
    for i, q in enumerate(zs):
        remote(r.share_own.at[q], r.share_z.at[i], r.zshare, (0, i), net.device(z=q))
    t = sums[...]
    for i, q in enumerate(plane):
        arrived(r.sums_p.at[i], r.pshare, (1, i), net.device(**q))
        t = t + r.sums_p[i]
    r.sums_own[...] = t
    for i, q in enumerate(zs):
        remote(r.sums_own, r.sums_z.at[i], r.zshare, (1, i), net.device(z=q))
    for d in order:
        t = a2_own[d, net.x].astype(f32)
        for i, q in enumerate(xs):
            arrived(a2.at[i, d], r.second_a, (d, i), net.device(x=q))
            t = t + a2[i, d].astype(f32)
        z_own[d, :, 0:half] = t.astype(bf16)
        t = b2_own[d, net.y].astype(f32)
        for i, q in enumerate(ys):
            arrived(b2.at[i, d], r.second_b, (d, i), net.device(y=q))
            t = t + b2[i, d].astype(f32)
        z_own[d, :, half:] = t.astype(bf16)
        if d:
            remote(z_own.at[d], r.z_in.at[d - 1], r.zred, (d - 1,), net.device(z=zs[d - 1]))

    t = r.share_own[net.z]
    for i, q in enumerate(zs):
        arrived(r.share_z.at[i], r.zshare, (0, i), net.device(z=q))
        t = t + r.share_z[i]
    for c in range(lanes):
        r.grad_prompt[:, c * 128 : (c + 1) * 128] = t[c * per : (c + 1) * per]
    t = r.sums_own[...]
    for i, q in enumerate(zs):
        arrived(r.sums_z.at[i], r.zshare, (1, i), net.device(z=q))
        t = t + r.sums_z[i]
    grad_sum, grad_dot = wide(t[0:lanes]), wide(t[lanes : 2 * lanes])
    base = first[K:R] - (usable / count) * (grad_sum + Xs[K:R] * grad_dot)
    t = z_own[0].astype(f32)
    for i, q in enumerate(zs):
        arrived(r.z_in.at[i], r.zred, (i,), net.device(z=q))
        t = t + r.z_in[i].astype(f32)
    reached = jnp.broadcast_to(t.reshape(block, 1, width), (block, STRIDE, width)).reshape(own, width)
    r.grad_rows[...] = spread * (base + chosen * reached)
    for c in pending:
        c.wait_send()


def write_kernel(a, b, c, a_out, b_out, c_out, sems):
    copies = [pltpu.make_async_copy(v, w, sems.at[i]) for i, (v, w) in enumerate(((a, a_out), (b, b_out), (c, c_out)))]
    for copy in copies:
        copy.start()
    for copy in copies:
        copy.wait()


def fused(groups, seq, x, segs, kinds, prompt, d_out, w_qkv, w_out, w_up, w_down, ln_gain, ln_bias):
    Z, Y, X = seq_dims(seq)
    own, width = x.shape
    block, per, lanes, half = own // STRIDE, prompt.shape[0], width // 128, width // 2
    C, Pn = seq * block, groups * seq * per
    K, R, M = C + Pn, C + Pn + own, C + own
    FF = w_up.shape[2]
    N = groups * Y * X
    V = pltpu.VMEM
    DMA = pltpu.SemaphoreType.DMA
    S = jax.ShapeDtypeStruct
    any_space = pl.BlockSpec(memory_space=pl.ANY)
    vmem = pl.BlockSpec(memory_space=pltpu.VMEM)
    pb = (lanes * per, 128)
    small = (4 * lanes, 128)
    sums = (2 * lanes, 128)
    inputs = dict(
        x_in=x,
        segs_in=segs,
        kinds_in=kinds,
        prompt_rows=prompt,
        d_out_in=d_out,
        w_qkv_in=w_qkv,
        w_out_in=w_out,
        w_up_in=w_up,
        w_down_in=w_down,
        ln_gain_in=ln_gain,
        ln_bias_in=ln_bias,
    )
    outputs = dict(
        out_rows=S((own, width), f32), grad_rows=S((own, width), f32), grad_prompt=S((per, width), f32)
    )
    scratch = dict(
        x=V((own, width), f32),
        segs=V(segs.shape, jnp.int32),
        kinds=V(kinds.shape, jnp.int32),
        d_out=V((own, width), f32),
        w_qkv=V(w_qkv.shape, bf16),
        w_out=V(w_out.shape, bf16),
        w_up=V(w_up.shape, bf16),
        w_down=V(w_down.shape, bf16),
        ln_gain=V(ln_gain.shape, f32),
        ln_bias=V(ln_bias.shape, f32),
        small_own=V(small, f32),
        small_z=V((Z,) + small, f32),
        small=V((N,) + small, f32),
        ctx_own=V((block, width), f32),
        ctx=V((Z, Y, X, block, width), f32),
        prompt_own=V(pb, bf16),
        prompt_blocks=V((groups, Y, X, Z) + pb, bf16),
        prompts=V((Pn * lanes, 128), f32),
        X=V((R, width), f32),
        X1=V((R, width), f32),
        qkv=V((R, 3 * width), bf16),
        qkv1=V((R, 3 * width), bf16),
        mixed=V((R, width), f32),
        inv=V((R, width), f32),
        mixed1=V((own, width), f32),
        inv1=V((own, width), f32),
        p_main=V((HEADS, M, K), bf16),
        p_prompt=V((HEADS, Pn, Pn), bf16),
        p_local=V((HEADS, own, own), bf16),
        p_main1=V((HEADS, own, K), bf16),
        p_local1=V((HEADS, own, own), bf16),
        n1=V((R, width), f32),
        r1=V((R, 1), f32),
        slope=V((R, FF), f32),
        n2=V((R, width), f32),
        r2=V((R, 1), f32),
        n1b=V((own, width), f32),
        r1b=V((own, 1), f32),
        slopeb=V((own, FF), f32),
        n2b=V((own, width), f32),
        r2b=V((own, 1), f32),
        first=V((R, width), f32),
        gm=V((R, width), bf16),
        grads=V((R, 3 * width), bf16),
        ds_main=V((HEADS, M, K), bf16),
        ds_local=V((HEADS, own, own), bf16),
        ds_prompt=V((HEADS, Pn, Pn), bf16),
        bias=V((own, R), f32),
        work=V((Z, Y, X, block, width), bf16),
        a1=V((Y, Z, X, block, half), bf16),
        b1=V((X, Z, Y, block, half), bf16),
        a2=V((X, Z, block, half), bf16),
        b2=V((Y, Z, block, half), bf16),
        a2_own=V((Z, X, block, half), bf16),
        b2_own=V((Z, Y, block, half), bf16),
        z_own=V((Z, block, width), bf16),
        z_in=V((Z, block, width), bf16),
        prompt_share=V((groups, Y, X, Z) + pb, bf16),
        share_p=V((N, Z) + pb, bf16),
        share_own=V((Z,) + pb, f32),
        share_z=V((Z,) + pb, f32),
        sums=V(sums, f32),
        sums_p=V((N,) + sums, f32),
        sums_own=V(sums, f32),
        sums_z=V((Z,) + sums, f32),
        load_sem=DMA((10,)),
        weight_sem=DMA((2, 4)),
    )
    for name, shape in dict(
        zsmall=(2, Z),
        psmall=(2, N),
        zctx=(Z,),
        xctx=(Z, X),
        yctx=(Z, Y),
        ydiag=(Z, X, Y),
        xdiag=(Z, Y, X),
        first_a=(Z, Y),
        first_b=(Z, X),
        second_a=(Z, X),
        second_b=(Z, Y),
        pshare=(2, N),
        zshare=(2, Z),
        zred=(Z,),
    ).items():
        scratch[name] = DMA((2,) + shape)
    names = tuple(inputs) + tuple(outputs) + tuple(scratch)
    results = pl.pallas_call(
        functools.partial(layers_kernel, groups, seq, names),
        out_shape=tuple(outputs.values()),
        in_specs=[vmem if n == "prompt_rows" else any_space for n in inputs],
        out_specs=(vmem,) * 3,
        scratch_shapes=list(scratch.values()),
        compiler_params=pltpu.CompilerParams(
            collective_id=0, has_side_effects=True, vmem_limit_bytes=60 * 2**20
        ),
        name="layers",
    )(*inputs.values())
    return pl.pallas_call(
        write_kernel,
        out_shape=tuple(outputs.values()),
        in_specs=[vmem] * 3,
        out_specs=(any_space,) * 3,
        scratch_shapes=[DMA((3,))],
        name="write_results",
    )(*results)


def plain(x, segs, kinds, prompt, d_out, w_qkv, w_out, w_up, w_down, ln_gain, ln_bias):
    both = ("group", "seq")
    own, width = x.shape
    E = width // HEADS
    scale = E**-0.5
    middle = 3 * lax.axis_index("group") + 1
    seg, kind = segs[0], kinds[0]
    usable = (kind != 2).astype(f32)[:, None]
    chosen = ((kind == 0) & (seg == middle)).astype(f32)[:, None]
    totals, squares, count = lax.psum(
        (jnp.sum(usable * x, axis=0), jnp.sum(usable * x * x, axis=0), jnp.sum(usable)), both
    )
    mean, second = totals / count, squares / count
    spread = lax.rsqrt(second - mean * mean + epsilon)
    picked = jnp.sum((x * chosen).reshape(-1, STRIDE, width), axis=1)
    present = jnp.sum(chosen.reshape(-1, STRIDE, 1), axis=1) > 0.5
    ctx = lax.all_gather(jnp.where(present, picked, absent), "seq", axis=0, tiled=True)
    prompts = lax.all_gather(prompt, both, axis=0, tiled=True)
    C, Pn = ctx.shape[0], prompts.shape[0]
    K = C + Pn
    held = ctx[:, 0] < 0.5 * absent
    X0 = jnp.concatenate(
        [
            jnp.where(held[:, None], (ctx - mean) * spread, 0.0),
            prompts.astype(f32),
            (x - mean) * spread,
        ],
        axis=0,
    )
    query = jnp.where(kind == 2, -2, seg)
    own_key = jnp.where((kind == 0) & (seg != middle), seg, -1)
    ctx_key = jnp.where(held, middle, -1)

    def bias(flag):
        return jnp.where(flag, 0.0, masked_score)

    own_bias = bias(
        jnp.concatenate(
            [
                query[:, None] == ctx_key[None],
                jnp.ones((own, Pn), bool),
                query[:, None] == own_key[None],
            ],
            axis=1,
        )
    )
    ctx_bias = jnp.concatenate([bias(held)[None], jnp.zeros((1, Pn), f32)], axis=1)

    def heads(a):
        return a.reshape(a.shape[0], HEADS, E)

    def flat(a):
        return a.reshape(a.shape[0], width)

    def attend(q, k, v, b):
        raw = jnp.einsum("rhe,khe->hrk", heads(q), heads(k), preferred_element_type=f32) + b
        e = jnp.exp((raw - jnp.max(raw, axis=-1, keepdims=True)) * scale)
        p = (e / jnp.sum(e, axis=-1, keepdims=True)).astype(bf16)
        return flat(jnp.einsum("hrk,khe->rhe", p, heads(v), preferred_element_type=f32)), p

    def attend_back(q, k, v, p, mix, g):
        delta = jnp.sum(heads(g).astype(f32) * heads(mix), axis=2).T
        dp = jnp.einsum("rhe,khe->hrk", heads(g), heads(v), preferred_element_type=f32)
        ds = (p.astype(f32) * (dp - delta[..., None])).astype(bf16)
        return (
            flat(jnp.einsum("hrk,khe->rhe", ds, heads(k), preferred_element_type=f32)) * scale,
            flat(jnp.einsum("hrk,rhe->khe", ds, heads(q), preferred_element_type=f32)) * scale,
            flat(jnp.einsum("hrk,rhe->khe", p, heads(g), preferred_element_type=f32)),
        )

    def tail(inp, mix, layer):
        na, ra = normalize(inp + mm(mix.astype(bf16), w_out[layer]))
        hidden = na * ln_gain[layer, 0] + ln_bias[layer, 0]
        u = mm(hidden.astype(bf16), w_up[layer])
        phi = 0.5 * (1.0 + lax.erf(u * inverse_root_two))
        slope = phi + u * jnp.exp(-0.5 * u * u) * inverse_root_two_pi
        nb, rb = normalize(hidden + mm((u * phi).astype(bf16), w_down[layer]))
        return nb * ln_gain[layer, 1] + ln_bias[layer, 1], (na, ra, slope, nb, rb)

    def tail_back(grad, kept, layer):
        na, ra, slope, nb, rb = kept
        g2 = normalize_backward(nb, rb, ln_gain[layer, 1], grad)
        ge = (mm_t(g2.astype(bf16), w_down[layer]) * slope).astype(bf16)
        g1 = normalize_backward(na, ra, ln_gain[layer, 0], g2 + mm_t(ge, w_up[layer]))
        return g1, mm_t(g1.astype(bf16), w_out[layer]).astype(bf16)

    qkv = mm(X0.astype(bf16), w_qkv[0]).astype(bf16)
    q, k, v = qkv[:, :width], qkv[:, width : 2 * width], qkv[:, 2 * width :]
    mix_c, p_c = attend(q[:C], k[:K], v[:K], ctx_bias)
    mix_p, p_p = attend(q[C:K], k[C:K], v[C:K], 0.0)
    mix_o, p_o = attend(q[K:], k, v, own_bias)
    X1, kept = tail(X0, jnp.concatenate([mix_c, mix_p, mix_o], axis=0), 0)
    kv = mm(X1.astype(bf16), w_qkv[1, :, width:]).astype(bf16)
    q1 = mm(X1[K:].astype(bf16), w_qkv[1, :, :width]).astype(bf16)
    mix1, p1 = attend(q1, kv[:, :width], kv[:, width:], own_bias)
    out, kept1 = tail(X1[K:], mix1, 1)
    g1, gm = tail_back(d_out, kept1, 1)
    dq, dk, dv = attend_back(q1, kv[:, :width], kv[:, width:], p1, mix1, gm)
    G = mm_t(jnp.concatenate([dk, dv], axis=1).astype(bf16), w_qkv[1, :, width:])
    G = G.at[K:].add(g1 + mm_t(dq.astype(bf16), w_qkv[1, :, :width]))
    g1, gm = tail_back(G, kept, 0)
    dqc, dkc, dvc = attend_back(q[:C], k[:K], v[:K], p_c, mix_c, gm[:C])
    dqp, dkp, dvp = attend_back(q[C:K], k[C:K], v[C:K], p_p, mix_p, gm[C:K])
    dqo, dk, dv = attend_back(q[K:], k, v, p_o, mix_o, gm[K:])
    dk = dk.at[:K].add(dkc).at[C:K].add(dkp)
    dv = dv.at[:K].add(dvc).at[C:K].add(dvp)
    parts = [jnp.concatenate([dqc, dqp, dqo], axis=0), dk, dv]
    G = g1 + mm_t(jnp.concatenate(parts, axis=1).astype(bf16), w_qkv[0])
    red = lax.psum_scatter(G[:C], "seq", scatter_dimension=0, tiled=True)
    grad_prompt = lax.psum_scatter(G[C:K], both, scatter_dimension=0, tiled=True)
    grad = G[K:] + chosen * jnp.repeat(red, STRIDE, axis=0)
    grad_sum, grad_dot = lax.psum((jnp.sum(grad, axis=0), jnp.sum(grad * X0[K:], axis=0)), both)
    grad_rows = spread * (grad - usable / count * (grad_sum + X0[K:] * grad_dot))
    return out, grad_rows, grad_prompt


def per_device(
    groups, seq, x, seg_ids, row_kind, prompt, w_qkv, w_out, w_up, w_down, ln_gain, ln_bias, d_out
):
    own = x.shape[0]
    fits = seq * (own // STRIDE) + groups * seq * prompt.shape[0] + own <= 1024
    run = functools.partial(fused, groups, seq) if fits else plain
    return run(
        x,
        seg_ids.reshape(1, own),
        row_kind.reshape(1, own),
        prompt,
        d_out,
        w_qkv,
        w_out,
        w_up,
        w_down,
        ln_gain,
        ln_bias,
    )


def solution(mesh):
    rows = P(("group", "seq"), None)
    labels = P(("group", "seq"))
    return jax.shard_map(
        functools.partial(per_device, mesh.shape["group"], mesh.shape["seq"]),
        mesh=mesh,
        in_specs=(rows, labels, labels, rows, P(), P(), P(), P(), P(), P(), rows),
        out_specs=(rows, rows, rows),
        check_vma=False,
    )
```

time: 1070 us -> 67.1 us (0.06)
  blocking collectives: 449 us -> 0 us
  waiting for transfers between devices: 293 us -> 0 us
  matrix products: 152 us -> 0 us
  local copies, waits for them, and re-layouts: 118 us -> 0 us
  Pallas kernels: 0 us -> 66.1 us
  other arithmetic: 30.8 us -> 0 us
  between operations: 17.1 us -> 0.82 us
    all_gather x5 -> x0, blocking collectives: 303 us -> none  [the longest x2 135 us: per_device(): lax.all_gather(prompt_pair[:, :width], ('group', 'seq'), axis=0, tiled=True)]
    reduce_scatter x4 -> x0, waiting for transfers between devices: 292 us -> none  [the longest x2 194 us: per_device(): lax.psum_scatter(merge_heads(group_grads[1]).astype(jnp.bfloat16), 'seq',...]
    dot_general x69 -> x0, matrix products: 152 us -> none  [the longest x10 26.5 us: times_transpose(): lax.dot_general(left, right, (((1,), (1,)), ((), ())), preferred_element_...]
    psum x2 -> x0, blocking collectives: 89.1 us -> none  [the longest x1 46.7 us: per_device(): lax.psum((jnp.sum(grad_rows, axis=0), jnp.sum(grad_rows * normed, axis=0)...]
    pallas_call x0 -> x2, Pallas kernels: none -> 66.1 us  [the longest x1 63.9 us: fused(): pl.pallas_call(functools.partial(layers_kernel, groups, seq, names), out_...]
    unnamed x1 -> x0, blocking collectives: 56.4 us -> none
    another operation x8 -> x0, local copies, waits for them, and re-layouts: 37.9 us -> none  [the longest x4 27.7 us: blocks_of(): return array.reshape((array.shape[0] // size, size) + array.shape[1:])]
    convert_element_type x8 -> x0, local copies, waits for them, and re-layouts: 23.7 us -> none  [the longest x2 11.9 us: per_device(): merge_heads(group_grads[1]).astype(jnp.bfloat16)]
  transfers between devices with their start and end apart: 8 -> 0, of which waited for: 4 -> 0; matrix products, arithmetic and copies ran while one was open for 9% -> 0% of each run, Pallas kernels for 0% -> 0%
where the time goes in v3:
time: 67.1 us; the launch traced here: 66.9 us
  Pallas kernels  66.1 us (99%)
  between operations  0.82 us (1%)
    pallas_call x1, Pallas kernels, fused(): pl.pallas_call(functools.partial(layers_kernel, groups, seq, names), out_...  63.9 us
    pallas_call x1, Pallas kernels, fused(): pl.pallas_call(write_kernel, out_shape=tuple(outputs.values()), in_specs=...  2.2 us

profile of v3, /device:TPU:0, one launch (start us, length us, event | category | flops | bytes accessed | tf_op | source)
XLA Modules:
  0.0 66.9 jit_solution(18303531530563391830)
XLA Ops:
  0.6 63.9 %layers.1 = (f32[256,512]{1,0:T(8,128)}, f32[256,512]{1,0:T(8,128)}, f32[4,512]{1,0:T(4,128)}) custom-call(f32[256,512]{1,0:T(8,128)} %refs_0_.1, s32[1,256]{1,0:T(1,128)} %bitcast.2, s32[1,256]{1,0:T(1,128)} %bitcast.3, bf16[4,512]{1,0:T(4,128)(2,1)} %refs_3_.1, f32[256,512]{1,0:T(8,128)} %refs_4_.1, bf16[2,512,1536]{2,1,0:T(8,128)(2,1)} %refs_5_.1, ...), custom_call_target="tpu_custom_call" | custom-call | tf_op jit(solution)/shard_map/layers/pallas_call | solution.py:887
  64.5 2.2 %write_results.1 = (f32[256,512]{1,0:T(8,128)}, f32[256,512]{1,0:T(8,128)}, f32[4,512]{1,0:T(4,128)}) custom-call(f32[256,512]{1,0:T(8,128)} %get-tuple-element.6.a, f32[256,512]{1,0:T(8,128)} %get-tuple-element.7.b, f32[4,512]{1,0:T(4,128)} %get-tuple-element.8.c), custom_call_target="tpu_custom_call" | custom-call | tf_op jit(solution)/shard_map/write_results/pallas_call | solution.py:898

commit v4 on v3

--- a/solution.py
+++ b/solution.py
@@ -14,7 +14,8 @@
 inverse_root_two = 0.7071067811865476
 inverse_root_two_pi = 0.3989422804014327
 log2_e = 1.4426950408889634
-absent = 1e9
+code_steps = 65500.0
+absent = -32768
 STRIDE = 8
 MESH = pl.DeviceIdType.MESH
 f32 = jnp.float32
@@ -83,12 +84,8 @@
 
     def plane(self):
         Z, Y, X = self.dims
-        at = (self.g * Y + self.y) * X + self.x
-        out = []
-        for d in range(1, self.groups * Y * X):
-            q = partner(at, d, self.groups * Y * X)
-            out.append(dict(g=q // (Y * X), y=(q // X) % Y, x=q % X))
-        return out
+        at = self.y * X + self.x
+        return [dict(y=q // X, x=q % X) for q in (partner(at, d, Y * X) for d in range(1, Y * X))]
 
 
 def pipeline(jobs):
@@ -121,7 +118,6 @@
     per = r.prompt_rows.shape[0]
     devices = groups * seq
     scale = E**-0.5
-    half = width // 2
     middle = 3 * net.g + 1
     w_qkv, w_out, w_up, w_down = r.w_qkv, r.w_out, r.w_up, r.w_down
     ln_gain, ln_bias = r.ln_gain, r.ln_bias
@@ -143,6 +139,8 @@
         pl.semaphore_signal(barrier, inc=1, device_id=net.device(z=q), device_id_type=MESH)
     for q in plane:
         pl.semaphore_signal(barrier, inc=1, device_id=net.device(**q), device_id_type=MESH)
+    sibling = net.device(g=1 - net.g)
+    pl.semaphore_signal(barrier, inc=1, device_id=sibling, device_id_type=MESH)
     late = local(r.d_out_in, r.d_out, r.load_sem.at[3])
     stored = ((r.w_qkv_in, w_qkv), (r.w_out_in, w_out), (r.w_up_in, w_up), (r.w_down_in, w_down))
     weights = [
@@ -197,50 +195,68 @@
     small_own[0:lanes] = narrow(jnp.sum(weighed, axis=0, keepdims=True))
     small_own[lanes : 2 * lanes] = narrow(jnp.sum(weighed * rows, axis=0, keepdims=True))
     small_own[2 * lanes : 4 * lanes] = jnp.broadcast_to(jnp.sum(usable), (2 * lanes, 128))
-    r.ctx_own[...] = jnp.where(held > 0.5, picked, absent)
+    some = jnp.max(held, axis=0, keepdims=True) > 0.5
+    most = jnp.where(some, jnp.max(jnp.where(held > 0.5, picked, -1e9), axis=0, keepdims=True), 0.0)
+    least = jnp.where(some, jnp.min(jnp.where(held > 0.5, picked, 1e9), axis=0, keepdims=True), 0.0)
+    center = 0.5 * (most + least)
+    step_size = jnp.maximum((most - least) * (1.0 / code_steps), 1e-30)
+    code = jnp.round((picked - center) / step_size).astype(jnp.int32)
+    r.ctx_own[...] = jnp.where(held > 0.5, code, absent).astype(jnp.int16)
+    r.scale_own[0:lanes] = narrow(center)
+    r.scale_own[lanes : 2 * lanes] = narrow(step_size)
     r.prompt_own[...] = narrow(r.prompt_rows[...].astype(f32)).astype(bf16)
     place = local(r.ctx_own, ctx.at[net.z, net.y, net.x], r.load_sem.at[6])
     prompt_blocks = r.prompt_blocks
-    prompt_at = (net.g, net.y, net.x, net.z)
-    place_prompt = local(r.prompt_own, prompt_blocks.at[prompt_at], r.load_sem.at[7])
-
-    pl.semaphore_wait(barrier, len(zs) + len(plane))
-    for i, q in enumerate(zs):
-        remote(small_own, r.small_z.at[i], r.zsmall, (0, i), net.device(z=q))
-    for i, q in enumerate(zs):
-        remote(r.prompt_own, prompt_blocks.at[prompt_at], r.zsmall, (1, i), net.device(z=q))
-    xs = [partner(net.x, d, X) for d in range(1, X)]
-    ys = [partner(net.y, d, Y) for d in range(1, Y)]
+    mine = (net.z, net.y, net.x)
+    place_prompt = local(r.prompt_own, prompt_blocks.at[(net.g,) + mine], r.load_sem.at[7])
+    scales = r.scales
+    place_scale = local(r.scale_own, scales.at[mine], r.load_sem.at[8])
+
+    pl.semaphore_wait(barrier, len(zs) + len(plane) + 1)
     levels = [net.z] + zs
 
     def spread_block(src, z, d):
-        for i, q in enumerate(xs):
-            remote(src, ctx.at[z, net.y, net.x], r.xctx, (d, i), net.device(x=q))
-        for i, q in enumerate(ys):
-            remote(src, ctx.at[z, net.y, net.x], r.yctx, (d, i), net.device(y=q))
-
-    for i, q in enumerate(zs):
-        remote(r.ctx_own, ctx.at[net.z, net.y, net.x], r.zctx, (i,), net.device(z=q))
+        for i, q in reversed(list(enumerate(plane))):
+            remote(src, ctx.at[z, net.y, net.x], r.pctx, (d, i), net.device(**q))
+
+    for i, q in enumerate(zs):
+        remote(r.ctx_own, ctx.at[mine], r.zctx, (i,), net.device(z=q))
     spread_block(r.ctx_own, net.z, 0)
-    for i, q in enumerate(zs):
-        arrived(r.small_z.at[i], r.zsmall, (0, i), net.device(z=q))
     small = r.small
-    small[0] = total_of([small_own[...]] + [r.small_z[i] for i in range(Z - 1)])
     for i, q in enumerate(plane):
-        remote(small.at[0], small.at[i + 1], r.psmall, (0, i), net.device(**q))
-    place_prompt.wait()
-    for i, q in enumerate(zs):
-        arrived(prompt_blocks.at[net.g, net.y, net.x, q], r.zsmall, (1, i), net.device(z=q))
-    for i, q in enumerate(plane):
-        mine = prompt_blocks.at[net.g, net.y, net.x]
-        remote(mine, mine, r.psmall, (1, i), net.device(**q))
+        dev = net.device(**q)
+        remote(small_own, small.at[0, i], r.psmall, (0, i), dev)
+        remote(r.prompt_own, prompt_blocks.at[(net.g,) + mine], r.psmall, (1, i), dev)
+        remote(r.scale_own, scales.at[mine], r.psmall, (2, i), dev)
     for i, q in enumerate(zs):
         arrived(ctx.at[q, net.y, net.x], r.zctx, (i,), net.device(z=q))
         spread_block(ctx.at[q, net.y, net.x], q, i + 1)
-
     for i, q in enumerate(plane):
-        arrived(small.at[i + 1], r.psmall, (0, i), net.device(**q))
-    total = total_of([small[i] for i in range(len(plane) + 1)])
+        arrived(small.at[0, i], r.psmall, (0, i), net.device(**q))
+    small_sum = r.small_sum
+    small_sum[0] = total_of([small_own[...]] + [small[0, i] for i in range(len(plane))])
+    remote(small_sum.at[0], small.at[1, 0], r.pair, (0,), sibling)
+    place_prompt.wait()
+    place_scale.wait()
+    for i, q in enumerate(plane):
+        dev = net.device(**q)
+        arrived(prompt_blocks.at[net.g, net.z, q["y"], q["x"]], r.psmall, (1, i), dev)
+        arrived(scales.at[net.z, q["y"], q["x"]], r.psmall, (2, i), dev)
+    for i, q in enumerate(zs):
+        dev = net.device(z=q)
+        remote(prompt_blocks.at[net.g, net.z], prompt_blocks.at[net.g, net.z], r.zsmall, (1, i), dev)
+        remote(scales.at[net.z], scales.at[net.z], r.zsmall, (2, i), dev)
+    arrived(small.at[1, 0], r.pair, (0,), sibling)
+    small_sum[1] = small_sum[0] + small[1, 0]
+    for i, q in enumerate(zs):
+        remote(small_sum.at[1], small.at[2, i], r.zsmall, (0, i), net.device(z=q))
+    for i, q in enumerate(zs):
+        arrived(prompt_blocks.at[net.g, q], r.zsmall, (1, i), net.device(z=q))
+    remote(prompt_blocks.at[net.g], prompt_blocks.at[net.g], r.pair, (1,), sibling)
+
+    for i, q in enumerate(zs):
+        arrived(small.at[2, i], r.zsmall, (0, i), net.device(z=q))
+    total = total_of([small_sum[1]] + [small[2, i] for i in range(len(zs))])
 
     def wide(part):
         return jnp.concatenate([part[i : i + 1] for i in range(lanes)], axis=1)
@@ -255,24 +271,7 @@
     weights[0][0].wait()
     qkv[K:R] = mm(Xs[K:R].astype(bf16), w_qkv[0]).astype(bf16)
 
-    def forward_blocks(d):
-        z = levels[d]
-        for i, q in enumerate(xs):
-            arrived(ctx.at[z, net.y, q], r.xctx, (d, i), net.device(x=q))
-            view = ctx.at[z, net.y, q, :, pl.ds(0, half)]
-            for j, t in enumerate(ys):
-                remote(view, view, r.ydiag, (d, i, j), net.device(y=t))
-        for i, q in enumerate(ys):
-            arrived(ctx.at[z, q, net.x], r.yctx, (d, i), net.device(y=q))
-            view = ctx.at[z, q, net.x, :, pl.ds(half, half)]
-            for j, t in enumerate(xs):
-                remote(view, view, r.xdiag, (d, i, j), net.device(x=t))
-
-    for d in range(Z // 2):
-        forward_blocks(d)
-
-    for i, q in enumerate(plane):
-        arrived(prompt_blocks.at[q["g"], q["y"], q["x"]], r.psmall, (1, i), net.device(**q))
+    arrived(prompt_blocks.at[1 - net.g], r.pair, (1,), sibling)
     prompts = r.prompts
     prompts[...] = prompt_blocks[...].astype(f32).reshape(prompts.shape)
     for c in range(lanes):
@@ -281,8 +280,6 @@
                 pl.ds(c * per + i, devices, stride=lanes * per)
             ]
     qkv[0:Pn] = mm(Xs[0:Pn].astype(bf16), w_qkv[0]).astype(bf16)
-    for d in range(Z // 2, Z):
-        forward_blocks(d)
 
     def cols(h, part=0):
         return slice(part * width + h * E, part * width + (h + 1) * E)
@@ -451,15 +448,26 @@
     pipeline([tail_job(0, (slice(0, Pn),) * 3, kept, Xs, mixed, put(X1, slice(0, Pn)))])
 
     place.wait()
+    for i, q in enumerate(zs):
+        arrived(scales.at[q], r.zsmall, (2, i), net.device(z=q))
     for d in range(Z):
-        z = levels[d]
-        for i, q in enumerate(ys):
-            for j, t in enumerate(xs):
-                arrived(ctx.at[z, q, t, :, pl.ds(0, half)], r.ydiag, (d, j, i), net.device(y=q))
-                arrived(ctx.at[z, q, t, :, pl.ds(half, half)], r.xdiag, (d, i, j), net.device(x=t))
-    raw = ctx[...].reshape(C, width)
-    present = jnp.abs(raw[:, 0:1]) < 0.5 * absent
-    Xs[Pn:K] = jnp.where(present, (raw - mean) * spread, 0.0)
+        for i, q in enumerate(plane):
+            arrived(ctx.at[levels[d], q["y"], q["x"]], r.pctx, (d, i), net.device(**q))
+    flags = []
+    for z in range(Z):
+        for y in range(Y):
+            for x in range(X):
+                code = ctx[z, y, x].astype(jnp.int32)
+                flags.append(code[:, 0:1] != absent)
+                part = scales[z, y, x]
+                at = Pn + ((z * Y + y) * X + x) * block
+                Xs[at : at + block] = jnp.where(
+                    flags[-1],
+                    (wide(part[0:lanes]) - mean) * spread
+                    + code.astype(f32) * (wide(part[lanes : 2 * lanes]) * spread),
+                    0.0,
+                )
+    present = jnp.concatenate(flags, axis=0)
     qkv[Pn:K] = mm(Xs[Pn:K].astype(bf16), w_qkv[0]).astype(bf16)
     square = lax.broadcasted_iota(jnp.int32, (128, 128), 0) == lax.broadcasted_iota(jnp.int32, (128, 128), 1)
     ctx_key = jnp.concatenate(
@@ -648,29 +656,13 @@
     pipeline(jobs)
 
     work = r.work
+    g = first[Pn:K] + mm_t(grads[Pn:K], w_qkv[0])
+    first[Pn:K] = g
+    work[...] = g.astype(bf16).reshape(work.shape)
     order = list(range(Z - 1, -1, -1))
-
-    def context_gradient(lo, hi):
-        g = first[Pn:K, lo:hi] + mm_t(grads[Pn:K], w_qkv[0, lo:hi])
-        first[Pn:K, lo:hi] = g
-        work[:, :, :, :, lo:hi] = g.astype(bf16).reshape(Z, Y, X, block, half)
-
-    context_gradient(0, half)
     for d in order:
-        for i, q in enumerate(ys):
-            remote(
-                work.at[levels[d], q, :, :, pl.ds(0, half)], r.a1.at[i, d], r.first_a, (d, i), net.device(y=q)
-            )
-    context_gradient(half, width)
-    for d in order:
-        for i, q in enumerate(xs):
-            remote(
-                work.at[levels[d], :, q, :, pl.ds(half, half)],
-                r.b1.at[i, d],
-                r.first_b,
-                (d, i),
-                net.device(x=q),
-            )
+        for i, q in reversed(list(enumerate(plane))):
+            remote(work.at[levels[d], q["y"], q["x"]], r.plane_in.at[d, i], r.pctx_back, (d, i), net.device(**q))
     first[0:Pn] += mm_t(grads[0:Pn], w_qkv[0])
     for c in range(lanes):
         for i in range(per):
@@ -679,75 +671,61 @@
             ]
     share = r.prompt_share
     share[...] = prompts[...].astype(bf16).reshape(share.shape)
-    for i, q in enumerate(plane):
-        remote(share.at[q["g"], q["y"], q["x"]], r.share_p.at[i], r.pshare, (0, i), net.device(**q))
+    remote(share.at[1 - net.g], r.share_pair, r.pair, (2,), sibling)
     first[K:R] += mm_t(grads[K:R], w_qkv[0])
     g = first[Pn:R]
     sums = r.sums
-    sums[0:lanes] = narrow(jnp.sum(g, axis=0, keepdims=True))
-    sums[lanes:] = narrow(jnp.sum(g * Xs[Pn:R], axis=0, keepdims=True))
+    sums[0, 0:lanes] = narrow(jnp.sum(g, axis=0, keepdims=True))
+    sums[0, lanes:] = narrow(jnp.sum(g * Xs[Pn:R], axis=0, keepdims=True))
+    remote(sums.at[0], r.sums_in.at[0, 0], r.pair, (3,), sibling)
+    arrived(r.share_pair, r.pair, (2,), sibling)
+    share_sum = r.share_sum
+    share_sum[...] = (share[net.g].astype(f32) + r.share_pair[...].astype(f32)).astype(bf16)
+    for i, q in enumerate(zs):
+        remote(share_sum.at[q], r.share_z.at[i], r.zshare, (0, i), net.device(z=q))
+    arrived(r.sums_in.at[0, 0], r.pair, (3,), sibling)
+    sums[1] = sums[0] + r.sums_in[0, 0]
+    for i, q in enumerate(zs):
+        remote(sums.at[1], r.sums_in.at[1, i], r.zshare, (1, i), net.device(z=q))
+    z_own = r.z_own
+    for d in order:
+        t = work[levels[d], net.y, net.x].astype(f32)
+        for i, q in enumerate(plane):
+            arrived(r.plane_in.at[d, i], r.pctx_back, (d, i), net.device(**q))
+            t = t + r.plane_in[d, i].astype(f32)
+        z_own[d] = t
+        if d:
+            r.z_out[d] = t.astype(bf16)
+            remote(r.z_out.at[d], r.z_in.at[d - 1], r.zred, (d - 1,), net.device(z=zs[d - 1]))
+    t = sums[1]
+    for i, q in enumerate(zs):
+        arrived(r.sums_in.at[1, i], r.zshare, (1, i), net.device(z=q))
+        t = t + r.sums_in[1, i]
+    sums[2] = t
     for i, q in enumerate(plane):
-        remote(sums, r.sums_p.at[i], r.pshare, (1, i), net.device(**q))
-
-    a2, b2 = r.a2, r.b2
-    a2_own, b2_own, z_own = r.a2_own, r.b2_own, r.z_own
-    for d in order:
-        z = levels[d]
-        t = work[z, net.y, :, :, 0:half].astype(f32)
-        for i, q in enumerate(ys):
-            arrived(r.a1.at[i, d], r.first_a, (d, i), net.device(y=q))
-            t = t + r.a1[i, d].astype(f32)
-        a2_own[d] = t.astype(bf16)
-        for i, q in enumerate(xs):
-            remote(a2_own.at[d, q], a2.at[i, d], r.second_a, (d, i), net.device(x=q))
-        t = work[z, :, net.x, :, half:].astype(f32)
-        for i, q in enumerate(xs):
-            arrived(r.b1.at[i, d], r.first_b, (d, i), net.device(x=q))
-            t = t + r.b1[i, d].astype(f32)
-        b2_own[d] = t.astype(bf16)
-        for i, q in enumerate(ys):
-            remote(b2_own.at[d, q], b2.at[i, d], r.second_b, (d, i), net.device(y=q))
-    t = share[net.g, net.y, net.x].astype(f32)
+        remote(sums.at[2], r.sums_in.at[2, i], r.pshare, (1, i), net.device(**q))
+    t = share_sum[net.z].astype(f32)
+    for i, q in enumerate(zs):
+        arrived(r.share_z.at[i], r.zshare, (0, i), net.device(z=q))
+        t = t + r.share_z[i].astype(f32)
+    share_own = r.share_own
+    share_own[...] = t
+    for i, q in enumerate(plane):
+        remote(share_own.at[q["y"], q["x"]], r.share_p.at[i], r.pshare, (0, i), net.device(**q))
+
+    t = share_own[net.y, net.x]
     for i, q in enumerate(plane):
         arrived(r.share_p.at[i], r.pshare, (0, i), net.device(**q))
-        t = t + r.share_p[i].astype(f32)
-    r.share_own[...] = t
-    for i, q in enumerate(zs):
-        remote(r.share_own.at[q], r.share_z.at[i], r.zshare, (0, i), net.device(z=q))
-    t = sums[...]
-    for i, q in enumerate(plane):
-        arrived(r.sums_p.at[i], r.pshare, (1, i), net.device(**q))
-        t = t + r.sums_p[i]
-    r.sums_own[...] = t
-    for i, q in enumerate(zs):
-        remote(r.sums_own, r.sums_z.at[i], r.zshare, (1, i), net.device(z=q))
-    for d in order:
-        t = a2_own[d, net.x].astype(f32)
-        for i, q in enumerate(xs):
-            arrived(a2.at[i, d], r.second_a, (d, i), net.device(x=q))
-            t = t + a2[i, d].astype(f32)
-        z_own[d, :, 0:half] = t.astype(bf16)
-        t = b2_own[d, net.y].astype(f32)
-        for i, q in enumerate(ys):
-            arrived(b2.at[i, d], r.second_b, (d, i), net.device(y=q))
-            t = t + b2[i, d].astype(f32)
-        z_own[d, :, half:] = t.astype(bf16)
-        if d:
-            remote(z_own.at[d], r.z_in.at[d - 1], r.zred, (d - 1,), net.device(z=zs[d - 1]))
-
-    t = r.share_own[net.z]
-    for i, q in enumerate(zs):
-        arrived(r.share_z.at[i], r.zshare, (0, i), net.device(z=q))
-        t = t + r.share_z[i]
+        t = t + r.share_p[i]
     for c in range(lanes):
         r.grad_prompt[:, c * 128 : (c + 1) * 128] = t[c * per : (c + 1) * per]
-    t = r.sums_own[...]
-    for i, q in enumerate(zs):
-        arrived(r.sums_z.at[i], r.zshare, (1, i), net.device(z=q))
-        t = t + r.sums_z[i]
+    t = sums[2]
+    for i, q in enumerate(plane):
+        arrived(r.sums_in.at[2, i], r.pshare, (1, i), net.device(**q))
+        t = t + r.sums_in[2, i]
     grad_sum, grad_dot = wide(t[0:lanes]), wide(t[lanes : 2 * lanes])
     base = first[K:R] - (usable / count) * (grad_sum + Xs[K:R] * grad_dot)
-    t = z_own[0].astype(f32)
+    t = z_own[0]
     for i, q in enumerate(zs):
         arrived(r.z_in.at[i], r.zred, (i,), net.device(z=q))
         t = t + r.z_in[i].astype(f32)
@@ -768,11 +746,11 @@
 def fused(groups, seq, x, segs, kinds, prompt, d_out, w_qkv, w_out, w_up, w_down, ln_gain, ln_bias):
     Z, Y, X = seq_dims(seq)
     own, width = x.shape
-    block, per, lanes, half = own // STRIDE, prompt.shape[0], width // 128, width // 2
+    block, per, lanes = own // STRIDE, prompt.shape[0], width // 128
     C, Pn = seq * block, groups * seq * per
     K, R, M = C + Pn, C + Pn + own, C + own
     FF = w_up.shape[2]
-    N = groups * Y * X
+    N = Y * X
     V = pltpu.VMEM
     DMA = pltpu.SemaphoreType.DMA
     S = jax.ShapeDtypeStruct
@@ -809,12 +787,14 @@
         ln_gain=V(ln_gain.shape, f32),
         ln_bias=V(ln_bias.shape, f32),
         small_own=V(small, f32),
-        small_z=V((Z,) + small, f32),
-        small=V((N,) + small, f32),
-        ctx_own=V((block, width), f32),
-        ctx=V((Z, Y, X, block, width), f32),
+        small=V((3, max(N, Z)) + small, f32),
+        small_sum=V((2,) + small, f32),
+        ctx_own=V((block, width), jnp.int16),
+        ctx=V((Z, Y, X, block, width), jnp.int16),
+        scale_own=V(sums, f32),
+        scales=V((Z, Y, X) + sums, f32),
         prompt_own=V(pb, bf16),
-        prompt_blocks=V((groups, Y, X, Z) + pb, bf16),
+        prompt_blocks=V((groups, Z, Y, X) + pb, bf16),
         prompts=V((Pn * lanes, 128), f32),
         X=V((R, width), f32),
         X1=V((R, width), f32),
@@ -847,37 +827,28 @@
         ds_prompt=V((HEADS, Pn, Pn), bf16),
         bias=V((own, R), f32),
         work=V((Z, Y, X, block, width), bf16),
-        a1=V((Y, Z, X, block, half), bf16),
-        b1=V((X, Z, Y, block, half), bf16),
-        a2=V((X, Z, block, half), bf16),
-        b2=V((Y, Z, block, half), bf16),
-        a2_own=V((Z, X, block, half), bf16),
-        b2_own=V((Z, Y, block, half), bf16),
-        z_own=V((Z, block, width), bf16),
+        plane_in=V((Z, N, block, width), bf16),
+        z_own=V((Z, block, width), f32),
+        z_out=V((Z, block, width), bf16),
         z_in=V((Z, block, width), bf16),
-        prompt_share=V((groups, Y, X, Z) + pb, bf16),
-        share_p=V((N, Z) + pb, bf16),
-        share_own=V((Z,) + pb, f32),
-        share_z=V((Z,) + pb, f32),
-        sums=V(sums, f32),
-        sums_p=V((N,) + sums, f32),
-        sums_own=V(sums, f32),
-        sums_z=V((Z,) + sums, f32),
+        prompt_share=V((groups, Z, Y, X) + pb, bf16),
+        share_pair=V((Z, Y, X) + pb, bf16),
+        share_sum=V((Z, Y, X) + pb, bf16),
+        share_z=V((Z, Y, X) + pb, bf16),
+        share_own=V((Y, X) + pb, f32),
+        share_p=V((N,) + pb, f32),
+        sums=V((3,) + sums, f32),
+        sums_in=V((3, max(N, Z)) + sums, f32),
         load_sem=DMA((10,)),
         weight_sem=DMA((2, 4)),
     )
     for name, shape in dict(
-        zsmall=(2, Z),
-        psmall=(2, N),
+        zsmall=(3, Z),
+        psmall=(3, N),
+        pair=(4,),
         zctx=(Z,),
-        xctx=(Z, X),
-        yctx=(Z, Y),
-        ydiag=(Z, X, Y),
-        xdiag=(Z, Y, X),
-        first_a=(Z, Y),
-        first_b=(Z, X),
-        second_a=(Z, X),
-        second_b=(Z, Y),
+        pctx=(Z, N),
+        pctx_back=(Z, N),
         pshare=(2, N),
         zshare=(2, Z),
         zred=(Z,),
@@ -907,6 +878,7 @@
 
 def plain(x, segs, kinds, prompt, d_out, w_qkv, w_out, w_up, w_down, ln_gain, ln_bias):
     both = ("group", "seq")
+    missing = 1e9
     own, width = x.shape
     E = width // HEADS
     scale = E**-0.5
@@ -921,11 +893,11 @@
     spread = lax.rsqrt(second - mean * mean + epsilon)
     picked = jnp.sum((x * chosen).reshape(-1, STRIDE, width), axis=1)
     present = jnp.sum(chosen.reshape(-1, STRIDE, 1), axis=1) > 0.5
-    ctx = lax.all_gather(jnp.where(present, picked, absent), "seq", axis=0, tiled=True)
+    ctx = lax.all_gather(jnp.where(present, picked, missing), "seq", axis=0, tiled=True)
     prompts = lax.all_gather(prompt, both, axis=0, tiled=True)
     C, Pn = ctx.shape[0], prompts.shape[0]
     K = C + Pn
-    held = ctx[:, 0] < 0.5 * absent
+    held = ctx[:, 0] < 0.5 * missing
     X0 = jnp.concatenate(
         [
             jnp.where(held[:, None], (ctx - mean) * spread, 0.0),
@@ -1025,7 +997,7 @@
     groups, seq, x, seg_ids, row_kind, prompt, w_qkv, w_out, w_up, w_down, ln_gain, ln_bias, d_out
 ):
     own = x.shape[0]
-    fits = seq * (own // STRIDE) + groups * seq * prompt.shape[0] + own <= 1024
+    fits = groups == 2 and seq * (own // STRIDE) + groups * seq * prompt.shape[0] + own <= 1024
     run = functools.partial(fused, groups, seq) if fits else plain
     return run(
         x,

time: 67.1 us -> 62.7 us (0.934)
  Pallas kernels: 66.1 us -> 61.7 us
    pallas_call x1, Pallas kernels: 63.9 us -> 59.5 us  [fused(): pl.pallas_call(functools.partial(layers_kernel, groups, seq, names), out_...]
where the time goes in v4:
time: 62.7 us; the launch traced here: 62.5 us
  Pallas kernels  61.7 us (98%)
  between operations  0.82 us (1%)
    pallas_call x1, Pallas kernels, fused(): pl.pallas_call(functools.partial(layers_kernel, groups, seq, names), out_...  59.5 us
    pallas_call x1, Pallas kernels, fused(): pl.pallas_call(write_kernel, out_shape=tuple(outputs.values()), in_specs=...  2.2 us

profile of v4, /device:TPU:0, one launch (start us, length us, event | category | flops | bytes accessed | tf_op | source)
XLA Modules:
  0.0 62.5 jit_solution(12927979304244155640)
XLA Ops:
  0.6 59.5 %layers.1 = (f32[256,512]{1,0:T(8,128)}, f32[256,512]{1,0:T(8,128)}, f32[4,512]{1,0:T(4,128)}) custom-call(f32[256,512]{1,0:T(8,128)} %refs_0_.1, s32[1,256]{1,0:T(1,128)} %bitcast.2, s32[1,256]{1,0:T(1,128)} %bitcast.3, bf16[4,512]{1,0:T(4,128)(2,1)} %refs_3_.1, f32[256,512]{1,0:T(8,128)} %refs_4_.1, bf16[2,512,1536]{2,1,0:T(8,128)(2,1)} %refs_5_.1, ...), custom_call_target="tpu_custom_call" | custom-call | tf_op jit(solution)/shard_map/layers/pallas_call | solution.py:858
  60.1 2.2 %write_results.1 = (f32[256,512]{1,0:T(8,128)}, f32[256,512]{1,0:T(8,128)}, f32[4,512]{1,0:T(4,128)}) custom-call(f32[256,512]{1,0:T(8,128)} %get-tuple-element.6.a, f32[256,512]{1,0:T(8,128)} %get-tuple-element.7.b, f32[4,512]{1,0:T(4,128)} %get-tuple-element.8.c), custom_call_target="tpu_custom_call" | custom-call | tf_op jit(solution)/shard_map/write_results/pallas_call | solution.py:869

commit v5 on v4

--- a/solution.py
+++ b/solution.py
@@ -88,17 +88,30 @@
         return [dict(y=q // X, x=q % X) for q in (partner(at, d, Y * X) for d in range(1, Y * X))]
 
 
+class Job:
+    def __init__(self, stages, after=()):
+        self.stages = stages
+        self.after = after
+        self.state = Namespace()
+
+    def end(self):
+        return self.start + len(self.stages)
+
+
 def pipeline(jobs):
-    state = [Namespace() for _ in jobs]
-    longest = max(len(j) for j in jobs)
-    for step in range(len(jobs) + longest - 1):
-        now = [
-            (state[j],) + jobs[j][step - j] for j in range(len(jobs)) if 0 <= step - j < len(jobs[j])
-        ]
+    taken = set()
+    for job in jobs:
+        job.start = max([0] + [other.end() for other in job.after])
+        while job.start in taken:
+            job.start += 1
+        taken.add(job.start)
+    for step in range(max(job.end() for job in jobs)):
+        now = [job for job in jobs if job.start <= step < job.end()]
         for want in "mv":
-            for s, kind, stage in reversed(now):
+            for job in reversed(now):
+                kind, stage = job.stages[step - job.start]
                 if kind == want:
-                    stage(s)
+                    stage(job.state)
 
 
 def narrow(rows):
@@ -140,7 +153,9 @@
     for q in plane:
         pl.semaphore_signal(barrier, inc=1, device_id=net.device(**q), device_id_type=MESH)
     sibling = net.device(g=1 - net.g)
-    pl.semaphore_signal(barrier, inc=1, device_id=sibling, device_id_type=MESH)
+    both = [net.device(**q) for q in plane] + [sibling] + [net.device(g=1 - net.g, **q) for q in plane]
+    for dev in both[len(plane) :]:
+        pl.semaphore_signal(barrier, inc=1, device_id=dev, device_id_type=MESH)
     late = local(r.d_out_in, r.d_out, r.load_sem.at[3])
     stored = ((r.w_qkv_in, w_qkv), (r.w_out_in, w_out), (r.w_up_in, w_up), (r.w_down_in, w_down))
     weights = [
@@ -212,30 +227,37 @@
     scales = r.scales
     place_scale = local(r.scale_own, scales.at[mine], r.load_sem.at[8])
 
-    pl.semaphore_wait(barrier, len(zs) + len(plane) + 1)
+    pl.semaphore_wait(barrier, len(zs) + len(both))
     levels = [net.z] + zs
 
     def spread_block(src, z, d):
         for i, q in reversed(list(enumerate(plane))):
             remote(src, ctx.at[z, net.y, net.x], r.pctx, (d, i), net.device(**q))
 
+    small = r.small
+    for i, dev in enumerate(both):
+        remote(small_own, small.at[0, i], r.psmall, (0, i), dev)
     for i, q in enumerate(zs):
         remote(r.ctx_own, ctx.at[mine], r.zctx, (i,), net.device(z=q))
     spread_block(r.ctx_own, net.z, 0)
-    small = r.small
     for i, q in enumerate(plane):
         dev = net.device(**q)
-        remote(small_own, small.at[0, i], r.psmall, (0, i), dev)
         remote(r.prompt_own, prompt_blocks.at[(net.g,) + mine], r.psmall, (1, i), dev)
         remote(r.scale_own, scales.at[mine], r.psmall, (2, i), dev)
+
+    def pass_on(d):
+        arrived(ctx.at[levels[d], net.y, net.x], r.zctx, (d - 1,), net.device(z=levels[d]))
+        spread_block(ctx.at[levels[d], net.y, net.x], levels[d], d)
+
+    pass_on(1)
+    for i, dev in enumerate(both):
+        arrived(small.at[0, i], r.psmall, (0, i), dev)
+    small_sum = r.small_sum
+    small_sum[...] = total_of([small_own[...]] + [small[0, i] for i in range(len(both))])
     for i, q in enumerate(zs):
-        arrived(ctx.at[q, net.y, net.x], r.zctx, (i,), net.device(z=q))
-        spread_block(ctx.at[q, net.y, net.x], q, i + 1)
-    for i, q in enumerate(plane):
-        arrived(small.at[0, i], r.psmall, (0, i), net.device(**q))
-    small_sum = r.small_sum
-    small_sum[0] = total_of([small_own[...]] + [small[0, i] for i in range(len(plane))])
-    remote(small_sum.at[0], small.at[1, 0], r.pair, (0,), sibling)
+        remote(small_sum, small.at[1, i], r.zsmall, (0, i), net.device(z=q))
+    for d in range(2, Z - 1):
+        pass_on(d)
     place_prompt.wait()
     place_scale.wait()
     for i, q in enumerate(plane):
@@ -246,17 +268,20 @@
         dev = net.device(z=q)
         remote(prompt_blocks.at[net.g, net.z], prompt_blocks.at[net.g, net.z], r.zsmall, (1, i), dev)
         remote(scales.at[net.z], scales.at[net.z], r.zsmall, (2, i), dev)
-    arrived(small.at[1, 0], r.pair, (0,), sibling)
-    small_sum[1] = small_sum[0] + small[1, 0]
-    for i, q in enumerate(zs):
-        remote(small_sum.at[1], small.at[2, i], r.zsmall, (0, i), net.device(z=q))
+    for d in range(max(Z - 1, 2), Z):
+        pass_on(d)
+    query = column(jnp.where(kind == 2, -2, seg))
+    own_key = jnp.where((kind == 0) & (seg != middle), seg, -1)
+    bias = r.bias
+    bias[:, 0:Pn] = jnp.zeros((own, Pn), f32)
+    bias[:, K:R] = jnp.where(query == own_key, 0.0, masked_score)
     for i, q in enumerate(zs):
         arrived(prompt_blocks.at[net.g, q], r.zsmall, (1, i), net.device(z=q))
     remote(prompt_blocks.at[net.g], prompt_blocks.at[net.g], r.pair, (1,), sibling)
 
     for i, q in enumerate(zs):
-        arrived(small.at[2, i], r.zsmall, (0, i), net.device(z=q))
-    total = total_of([small_sum[1]] + [small[2, i] for i in range(len(zs))])
+        arrived(small.at[1, i], r.zsmall, (0, i), net.device(z=q))
+    total = total_of([small_sum[...]] + [small[1, i] for i in range(len(zs))])
 
     def wide(part):
         return jnp.concatenate([part[i : i + 1] for i in range(lanes)], axis=1)
@@ -271,6 +296,37 @@
     weights[0][0].wait()
     qkv[K:R] = mm(Xs[K:R].astype(bf16), w_qkv[0]).astype(bf16)
 
+    square = lax.broadcasted_iota(jnp.int32, (128, 128), 0) == lax.broadcasted_iota(jnp.int32, (128, 128), 1)
+    level_rows = Y * X * block
+    ctx_bias = r.ctx_bias
+
+    def take_level(d):
+        z = levels[d]
+        for i, q in enumerate(plane):
+            arrived(ctx.at[z, q["y"], q["x"]], r.pctx, (d, i), net.device(**q))
+        if d:
+            arrived(scales.at[z], r.zsmall, (2, d - 1), net.device(z=z))
+        else:
+            place.wait()
+        flags, parts = [], []
+        for y in range(Y):
+            for x in range(X):
+                code = ctx[z, y, x].astype(jnp.int32)
+                flags.append(code[:, 0:1] != absent)
+                part = scales[z, y, x]
+                value = (wide(part[0:lanes]) - mean) * spread + code.astype(f32) * (
+                    wide(part[lanes : 2 * lanes]) * spread
+                )
+                parts.append(jnp.where(flags[-1], value, 0.0))
+        rows = jnp.concatenate(parts, axis=0)
+        at = pl.ds(pl.multiple_of(Pn + z * level_rows, 128), level_rows)
+        Xs[at] = rows
+        qkv[at] = mm(rows.astype(bf16), w_qkv[0]).astype(bf16)
+        present = jnp.concatenate(flags, axis=0)
+        ctx_bias[:, at] = jnp.max(jnp.where(square & present, 0.0, masked_score), axis=0, keepdims=True)
+
+    take_level(0)
+
     arrived(prompt_blocks.at[1 - net.g], r.pair, (1,), sibling)
     prompts = r.prompts
     prompts[...] = prompt_blocks[...].astype(f32).reshape(prompts.shape)
@@ -311,9 +367,9 @@
             m_ref[out, cols(h)] = s.mix * inv
             inv_ref[out, cols(h)] = inv
 
-        return [("m", scores), ("v", weigh), ("m", mix), ("v", keep)]
-
-    def tail_job(layer, rows, kept, x_ref, m_ref, store):
+        return Job([("m", scores), ("v", weigh), ("m", mix), ("v", keep)])
+
+    def tail_job(layer, rows, kept, x_ref, m_ref, store, after=(), more=()):
         na, ra, sl, nb, rb = kept
         xr, mr, kr = rows
 
@@ -343,17 +399,19 @@
             n, q = normalize(s.h + s.d)
             nb[kr] = n
             rb[kr] = q
-            store(n * ln_gain[layer, 1:2] + ln_bias[layer, 1:2])
-
-        return [("m", attended), ("v", first_norm), ("m", up), ("v", gelu), ("m", down), ("v", second_norm)]
+            s.y = n * ln_gain[layer, 1:2] + ln_bias[layer, 1:2]
+            store(s.y)
+
+        stages = [("m", attended), ("v", first_norm), ("m", up), ("v", gelu), ("m", down), ("v", second_norm)]
+        return Job(stages + list(more), after)
 
     first, gm, grads = r.first, r.gm, r.grads
 
-    def tail_back_job(layer, kr, rows, kept, load, inv_ref, ir):
+    def tail_back_job(layer, kr, rows, kept, load, inv_ref, ir, before=(), after=()):
         na, ra, sl, nb, rb = kept
 
         def second_norm(s):
-            s.g2 = normalize_backward(nb[kr], rb[kr], ln_gain[layer, 1:2], load())
+            s.g2 = normalize_backward(nb[kr], rb[kr], ln_gain[layer, 1:2], load(s))
             s.g2b = s.g2.astype(bf16)
 
         def down(s):
@@ -376,7 +434,7 @@
         def keep(s):
             gm[rows] = (s.gm.astype(bf16).astype(f32) * inv_ref[ir]).astype(bf16)
 
-        return [
+        stages = [
             ("v", second_norm),
             ("m", down),
             ("v", gelu),
@@ -385,8 +443,9 @@
             ("m", out),
             ("v", keep),
         ]
-
-    def backward_job(h, act, rows, out, keys, load, store, m_ref):
+        return Job(list(before) + stages, after)
+
+    def backward_job(h, act, rows, out, keys, load, store, m_ref, after=(), later=None):
         lo, hi = keys
 
         def products(s):
@@ -399,14 +458,16 @@
             store(s.ds)
 
         def queries(s):
-            s.dq = mm(s.ds, act[lo:hi, cols(h, 1)])
+            s.dq = mm(later() if later else s.ds, act[lo:hi, cols(h, 1)])
 
         def keep(s):
             grads[out, cols(h)] = (s.dq * scale).astype(bf16)
 
-        return [("m", products), ("v", scores), ("m", queries), ("v", keep)]
-
-    def key_jobs(h, key_terms, value_terms, at, n):
+        if later:
+            return Job([("m", products), ("v", scores)], after), Job([("m", queries), ("v", keep)])
+        return Job([("m", products), ("v", scores), ("m", queries), ("v", keep)], after)
+
+    def key_jobs(h, key_terms, value_terms, at, n, after=()):
         out = []
         for part, terms, factor in ((1, key_terms, scale), (2, value_terms, 1.0)):
 
@@ -414,9 +475,9 @@
                 s.t = total_of([t_mm(a(), b()) for a, b in terms])
 
             def keep(s, part=part, factor=factor):
-                grads[at : at + n, cols(h, part)] = (s.t * factor).astype(bf16).T
-
-            out.append([("m", product), ("v", keep)])
+                grads[pl.ds(at, n), cols(h, part)] = (s.t * factor).astype(bf16).T
+
+            out.append(Job([("m", product), ("v", keep)], after))
         return out
 
     p_main, p_prompt, p_local = r.p_main, r.p_prompt, r.p_local
@@ -425,7 +486,7 @@
     ds_main, ds_local, ds_prompt = r.ds_main, r.ds_local, r.ds_prompt
     kept = (r.n1, r.r1, r.slope, r.n2, r.r2)
     kept1 = (r.n1b, r.r1b, r.slopeb, r.n2b, r.r2b)
-    X1, qkv1, bias = r.X1, r.qkv1, r.bias
+    X1, qkv1 = r.X1, r.qkv1
 
     def put(ref, rows):
         def store(y):
@@ -440,48 +501,17 @@
         rows = slice(0, Pn)
         return forward_job(h, qkv, rows, rows, (0, Pn), lambda raw: weights_of(raw, None), store, mixed, inv)
 
+    for d in range(1, Z - 1):
+        take_level(d)
     pipeline([prompt_job(h) for h in range(HEADS)])
+    for d in range(max(Z - 1, 1), Z):
+        take_level(d)
+    reach = jnp.where(query == middle, 0.0, masked_score)
+    bias[:, Pn:K] = reach + ctx_bias[:, Pn:K]
     for c in weights[0][1:]:
         c.wait()
     for c in norms:
         c.wait()
-    pipeline([tail_job(0, (slice(0, Pn),) * 3, kept, Xs, mixed, put(X1, slice(0, Pn)))])
-
-    place.wait()
-    for i, q in enumerate(zs):
-        arrived(scales.at[q], r.zsmall, (2, i), net.device(z=q))
-    for d in range(Z):
-        for i, q in enumerate(plane):
-            arrived(ctx.at[levels[d], q["y"], q["x"]], r.pctx, (d, i), net.device(**q))
-    flags = []
-    for z in range(Z):
-        for y in range(Y):
-            for x in range(X):
-                code = ctx[z, y, x].astype(jnp.int32)
-                flags.append(code[:, 0:1] != absent)
-                part = scales[z, y, x]
-                at = Pn + ((z * Y + y) * X + x) * block
-                Xs[at : at + block] = jnp.where(
-                    flags[-1],
-                    (wide(part[0:lanes]) - mean) * spread
-                    + code.astype(f32) * (wide(part[lanes : 2 * lanes]) * spread),
-                    0.0,
-                )
-    present = jnp.concatenate(flags, axis=0)
-    qkv[Pn:K] = mm(Xs[Pn:K].astype(bf16), w_qkv[0]).astype(bf16)
-    square = lax.broadcasted_iota(jnp.int32, (128, 128), 0) == lax.broadcasted_iota(jnp.int32, (128, 128), 1)
-    ctx_key = jnp.concatenate(
-        [
-            jnp.max(jnp.where(square & present[i : i + 128], middle, -1), axis=0, keepdims=True)
-            for i in range(0, C, 128)
-        ],
-        axis=1,
-    )
-    ctx_bias = jnp.concatenate([jnp.zeros((1, Pn), f32), jnp.where(ctx_key == middle, 0.0, masked_score)], axis=1)
-    query = column(jnp.where(kind == 2, -2, seg))
-    own_key = jnp.where((kind == 0) & (seg != middle), seg, -1)
-    allowed = jnp.concatenate([jnp.ones((own, Pn), jnp.bool_), query == ctx_key, query == own_key], axis=1)
-    bias[...] = jnp.where(allowed, 0.0, masked_score)
 
     def ctx_job(h, at, n):
         def store(p):
@@ -505,45 +535,45 @@
         )
 
     part = 256
+    step = 128
+    weights[1][0].wait()
+
+    def next_stages(a, lo):
+        def product(s):
+            s.next = mm(s.y.astype(bf16), w_qkv[1, :, lo:])
+
+        def keep(s):
+            qkv1[a, lo:] = s.next.astype(bf16)
+
+        return [("m", product), ("v", keep)]
+
+    def tails(lo, hi, after):
+        out = []
+        for at in range(lo, hi, step):
+            a = slice(at, at + step)
+            mine = lo >= K
+            store = put(X1, slice(at - K, at - K + step)) if mine else (lambda y: None)
+            out.append(tail_job(0, (a, a, a), kept, Xs, mixed, store, after, next_stages(a, 0 if mine else width)))
+        return out
+
     jobs = []
-    for h in range(HEADS):
-        jobs += [ctx_job(h, at, part) for at in range(0, C, part)]
-        jobs += [own_job(h, qkv, p_main, C, p_local, mixed, inv, slice(K, R))]
-    pipeline(jobs)
-    pieces = [slice(a, a + part) for a in range(Pn, R, part)]
-    pipeline([tail_job(0, (a, a, a), kept, Xs, mixed, put(X1, a)) for a in pieces])
-
-    weights[1][0].wait()
-    step = R // 2
-
-    @pl.loop(0, R // step)
-    def _(i):
-        a = pl.ds(pl.multiple_of(i * step, step), step)
-        qkv1[a, width:] = mm(X1[a].astype(bf16), w_qkv[1, :, width:]).astype(bf16)
-
-    qkv1[K:R, 0:width] = mm(X1[K:R].astype(bf16), w_qkv[1, :, 0:width]).astype(bf16)
+    ready = [own_job(h, qkv, p_main, C, p_local, mixed, inv, slice(K, R)) for h in range(HEADS)]
+    jobs += ready
+    waiting = tails(K, R, ready)
+    for at in range(0, C, part):
+        ready = [ctx_job(h, at, part) for h in range(HEADS)]
+        jobs += ready + waiting
+        waiting = tails(Pn + at, Pn + at + part, ready)
+    pipeline(jobs + waiting + tails(0, Pn, ()))
 
     whole = slice(0, own)
-    pipeline([own_job(h, qkv1, p_main1, 0, p_local1, mixed1, inv1, whole) for h in range(HEADS)])
     for c in weights[1][1:]:
         c.wait()
     late.wait()
-    quarter = own // 2
-    pipeline(
-        [
-            tail_job(
-                1,
-                (slice(K + a, K + a + quarter), slice(a, a + quarter), slice(a, a + quarter)),
-                kept1,
-                X1,
-                mixed1,
-                put(r.out_rows, slice(a, a + quarter)),
-            )
-            for a in range(0, own, quarter)
-        ]
-    )
-
-    pipeline([tail_back_job(1, whole, slice(K, R), kept1, lambda: r.d_out[...], inv1, whole)])
+    ready = [own_job(h, qkv1, p_main1, 0, p_local1, mixed1, inv1, whole) for h in range(HEADS)]
+    pieces = [slice(at, at + step) for at in range(0, own, step)]
+    tail1 = [tail_job(1, (a, a, a), kept1, X1, mixed1, put(r.out_rows, a), ready) for a in pieces]
+    back1 = tail_back_job(1, whole, slice(K, R), kept1, lambda s: r.d_out[...], inv1, whole, (), tail1)
 
     def put_ds(h):
         def store(d):
@@ -552,38 +582,40 @@
 
         return store
 
-    pipeline(
-        [
-            backward_job(
-                h,
-                qkv1,
-                whole,
-                slice(K, R),
-                (0, R),
-                lambda h=h: jnp.concatenate([p_main1[h], p_local1[h]], axis=1),
-                put_ds(h),
-                mixed1,
-            )
-            for h in range(HEADS)
-        ]
-    )
-    jobs = []
+    jobs = ready + tail1 + [back1]
+    keys1 = []
     for h in range(HEADS):
+        job = backward_job(
+            h,
+            qkv1,
+            whole,
+            slice(K, R),
+            (0, R),
+            lambda h=h: jnp.concatenate([p_main1[h], p_local1[h]], axis=1),
+            put_ds(h),
+            mixed1,
+            [back1],
+        )
+        jobs.append(job)
         q = lambda h=h: qkv1[K:R, cols(h)]
         g = lambda h=h: gm[K:R, cols(h)]
-        jobs += key_jobs(h, [(q, lambda h=h: ds_main[h, C:M])], [(g, lambda h=h: p_main1[h])], 0, K)
-        jobs += key_jobs(h, [(q, lambda h=h: ds_local[h])], [(g, lambda h=h: p_local1[h])], K, own)
-    pipeline(jobs)
-    first[0:K] = mm_t(grads[0:K, width:], w_qkv[1, :, width:])
-    first[K:R] += mm_t(grads[K:R], w_qkv[1])
-
-    def take(rows):
-        return lambda: first[rows]
-
-    piece = R // 4
-    pieces = [slice(a, a + piece) for a in range(0, R, piece)]
-    pipeline([tail_back_job(0, a, a, kept, take(a), inv, a) for a in pieces])
-    jobs = []
+        keys1 += key_jobs(h, [(q, lambda h=h: ds_main[h, C:M])], [(g, lambda h=h: p_main1[h])], 0, K, [job])
+        keys1 += key_jobs(h, [(q, lambda h=h: ds_local[h])], [(g, lambda h=h: p_local1[h])], K, own, [job])
+    jobs += keys1
+
+    def row_gradient(a, mine):
+        lo = 0 if mine else width
+
+        def product(s):
+            s.g = mm_t(grads[a, lo:], w_qkv[1, :, lo:])
+
+        return [("m", product)]
+
+    def gradient_of(a, mine):
+        return lambda s: s.g + first[a] if mine else s.g
+
+    def back_job(a, mine):
+        return tail_back_job(0, a, a, kept, gradient_of(a, mine), inv, a, row_gradient(a, mine), keys1)
 
     def put_ctx(h, at):
         def store(d):
@@ -597,39 +629,90 @@
 
         return store
 
+    def back_ctx(h, at, after):
+        a = slice(Pn + at, Pn + at + part)
+        return backward_job(
+            h, qkv, a, a, (0, K), lambda: p_main[h, at : at + part], put_ctx(h, at), mixed, after
+        )
+
+    prompt_later, own_later = [], []
+
+    def back_prompt(h, after):
+        a = slice(0, Pn)
+        now, then = backward_job(
+            h, qkv, a, a, (0, Pn), lambda: p_prompt[h], put_prompt(h), mixed, after, lambda: ds_prompt[h]
+        )
+        prompt_later.append(then)
+        return now
+
+    def back_own(h, after):
+        a = slice(K, R)
+        now, then = backward_job(
+            h,
+            qkv,
+            a,
+            a,
+            (0, R),
+            lambda: jnp.concatenate([p_main[h, C:M], p_local[h]], axis=1),
+            put_ds(h),
+            mixed,
+            after,
+            lambda: jnp.concatenate([ds_main[h, C:M], ds_local[h]], axis=1),
+        )
+        own_later.append(then)
+        return now
+
+    lead = Pn + part
+    blocks = [(back_job(slice(K, R), True), [lambda h, b: back_own(h, [b])])]
+    for at in range(part, C, part):
+        a = slice(Pn + at, Pn + at + part)
+        blocks.append((back_job(a, False), [lambda h, b, at=at: back_ctx(h, at, [b])]))
+    blocks.append(
+        (back_job(slice(0, lead), False), [lambda h, b: back_prompt(h, [b]), lambda h, b: back_ctx(h, 0, [b])])
+    )
+    jobs += [b for b, makers in blocks]
+    for b, makers in blocks:
+        for h in range(HEADS):
+            jobs += [make(h, b) for make in makers]
+    pipeline(jobs)
+
+    def view(ref, lo, hi, c):
+        return lambda: ref[lo:hi, c]
+
+    def piece_of(ref, h, lo, hi):
+        return lambda: ref[h, :, lo:hi]
+
+    work = r.work
+    level = Y * X * block
+    chunk = Z // 2 * level
+
+    def half_gradient(far):
+        z = (net.z // (Z // 2) + far) % 2 * (Z // 2)
+        at = pl.multiple_of(Pn + z * level, 128)
+        jobs = []
+        for h in range(HEADS):
+            jobs += key_jobs(
+                h,
+                [(view(qkv, Pn, R, cols(h)), lambda h=h: ds_main[h, :, pl.ds(at, chunk)])],
+                [(view(gm, Pn, R, cols(h)), lambda h=h: p_main[h, :, pl.ds(at, chunk)])],
+                at,
+                chunk,
+            )
+        pipeline(jobs)
+        a = pl.ds(at, chunk)
+        g = first[a] + mm_t(grads[a], w_qkv[0])
+        first[a] = g
+        work[pl.ds(z, Z // 2)] = g.astype(bf16).reshape(Z // 2, Y, X, block, width)
+
+    def send_levels(order):
+        for d in order:
+            for i, q in reversed(list(enumerate(plane))):
+                remote(work.at[levels[d], q["y"], q["x"]], r.plane_in.at[d, i], r.pctx_back, (d, i), net.device(**q))
+
+    half_gradient(1)
+    send_levels(range(Z - 1, Z // 2 - 1, -1))
+    jobs = list(prompt_later)
     for h in range(HEADS):
-        for at in range(0, C, part):
-            a = slice(Pn + at, Pn + at + part)
-            jobs.append(
-                backward_job(
-                    h, qkv, a, a, (0, K), lambda h=h, at=at: p_main[h, at : at + part], put_ctx(h, at), mixed
-                )
-            )
-        a = slice(0, Pn)
-        jobs.append(backward_job(h, qkv, a, a, (0, Pn), lambda h=h: p_prompt[h], put_prompt(h), mixed))
-        a = slice(K, R)
-        jobs.append(
-            backward_job(
-                h,
-                qkv,
-                a,
-                a,
-                (0, R),
-                lambda h=h: jnp.concatenate([p_main[h, C:M], p_local[h]], axis=1),
-                put_ds(h),
-                mixed,
-            )
-        )
-    pipeline(jobs)
-    jobs = []
-    for h in range(HEADS):
-
-        def view(ref, lo, hi, c):
-            return lambda: ref[lo:hi, c]
-
-        def piece_of(ref, h, lo, hi):
-            return lambda: ref[h, :, lo:hi]
-
         q = functools.partial(view, qkv, c=cols(h))
         g = functools.partial(view, gm, c=cols(h))
         jobs += key_jobs(
@@ -639,30 +722,7 @@
             0,
             Pn,
         )
-        jobs += key_jobs(
-            h,
-            [(q(Pn, R), piece_of(ds_main, h, Pn, K))],
-            [(g(Pn, R), piece_of(p_main, h, Pn, K))],
-            Pn,
-            C,
-        )
-        jobs += key_jobs(
-            h,
-            [(q(K, R), piece_of(ds_local, h, 0, own))],
-            [(g(K, R), piece_of(p_local, h, 0, own))],
-            K,
-            own,
-        )
     pipeline(jobs)
-
-    work = r.work
-    g = first[Pn:K] + mm_t(grads[Pn:K], w_qkv[0])
-    first[Pn:K] = g
-    work[...] = g.astype(bf16).reshape(work.shape)
-    order = list(range(Z - 1, -1, -1))
-    for d in order:
-        for i, q in reversed(list(enumerate(plane))):
-            remote(work.at[levels[d], q["y"], q["x"]], r.plane_in.at[d, i], r.pctx_back, (d, i), net.device(**q))
     first[0:Pn] += mm_t(grads[0:Pn], w_qkv[0])
     for c in range(lanes):
         for i in range(per):
@@ -671,24 +731,34 @@
             ]
     share = r.prompt_share
     share[...] = prompts[...].astype(bf16).reshape(share.shape)
-    remote(share.at[1 - net.g], r.share_pair, r.pair, (2,), sibling)
+    remote(share.at[1 - net.g], r.share_pair, r.pair, (0,), sibling)
+    half_gradient(0)
+    arrived(r.share_pair, r.pair, (0,), sibling)
+    share_sum = r.share_sum
+    share_sum[...] = (share[net.g].astype(f32) + r.share_pair[...].astype(f32)).astype(bf16)
+    for i, q in enumerate(zs):
+        remote(share_sum.at[q], r.share_z.at[i], r.zshare, (0, i), net.device(z=q))
+    jobs = list(own_later)
+    for h in range(HEADS):
+        jobs += key_jobs(
+            h,
+            [(view(qkv, K, R, cols(h)), piece_of(ds_local, h, 0, own))],
+            [(view(gm, K, R, cols(h)), piece_of(p_local, h, 0, own))],
+            K,
+            own,
+        )
+    pipeline(jobs)
     first[K:R] += mm_t(grads[K:R], w_qkv[0])
     g = first[Pn:R]
     sums = r.sums
     sums[0, 0:lanes] = narrow(jnp.sum(g, axis=0, keepdims=True))
     sums[0, lanes:] = narrow(jnp.sum(g * Xs[Pn:R], axis=0, keepdims=True))
-    remote(sums.at[0], r.sums_in.at[0, 0], r.pair, (3,), sibling)
-    arrived(r.share_pair, r.pair, (2,), sibling)
-    share_sum = r.share_sum
-    share_sum[...] = (share[net.g].astype(f32) + r.share_pair[...].astype(f32)).astype(bf16)
-    for i, q in enumerate(zs):
-        remote(share_sum.at[q], r.share_z.at[i], r.zshare, (0, i), net.device(z=q))
-    arrived(r.sums_in.at[0, 0], r.pair, (3,), sibling)
-    sums[1] = sums[0] + r.sums_in[0, 0]
-    for i, q in enumerate(zs):
-        remote(sums.at[1], r.sums_in.at[1, i], r.zshare, (1, i), net.device(z=q))
+    for i, dev in enumerate(both):
+        remote(sums.at[0], r.sums_in.at[0, i], r.pshare, (1, i), dev)
+    send_levels(range(Z // 2 - 1, -1, -1))
     z_own = r.z_own
-    for d in order:
+
+    def take_back(d):
         t = work[levels[d], net.y, net.x].astype(f32)
         for i, q in enumerate(plane):
             arrived(r.plane_in.at[d, i], r.pctx_back, (d, i), net.device(**q))
@@ -697,13 +767,7 @@
         if d:
             r.z_out[d] = t.astype(bf16)
             remote(r.z_out.at[d], r.z_in.at[d - 1], r.zred, (d - 1,), net.device(z=zs[d - 1]))
-    t = sums[1]
-    for i, q in enumerate(zs):
-        arrived(r.sums_in.at[1, i], r.zshare, (1, i), net.device(z=q))
-        t = t + r.sums_in[1, i]
-    sums[2] = t
-    for i, q in enumerate(plane):
-        remote(sums.at[2], r.sums_in.at[2, i], r.pshare, (1, i), net.device(**q))
+
     t = share_sum[net.z].astype(f32)
     for i, q in enumerate(zs):
         arrived(r.share_z.at[i], r.zshare, (0, i), net.device(z=q))
@@ -712,6 +776,17 @@
     share_own[...] = t
     for i, q in enumerate(plane):
         remote(share_own.at[q["y"], q["x"]], r.share_p.at[i], r.pshare, (0, i), net.device(**q))
+    t = sums[0]
+    for i, dev in enumerate(both):
+        arrived(r.sums_in.at[0, i], r.pshare, (1, i), dev)
+        t = t + r.sums_in[0, i]
+    sums[1] = t
+    for i, q in enumerate(zs):
+        remote(sums.at[1], r.sums_in.at[1, i], r.zshare, (1, i), net.device(z=q))
+    for d in range(Z - 1, Z // 2 - 1, -1):
+        take_back(d)
+    for d in range(Z // 2 - 1, -1, -1):
+        take_back(d)
 
     t = share_own[net.y, net.x]
     for i, q in enumerate(plane):
@@ -719,10 +794,10 @@
         t = t + r.share_p[i]
     for c in range(lanes):
         r.grad_prompt[:, c * 128 : (c + 1) * 128] = t[c * per : (c + 1) * per]
-    t = sums[2]
-    for i, q in enumerate(plane):
-        arrived(r.sums_in.at[2, i], r.pshare, (1, i), net.device(**q))
-        t = t + r.sums_in[2, i]
+    t = sums[1]
+    for i, q in enumerate(zs):
+        arrived(r.sums_in.at[1, i], r.zshare, (1, i), net.device(z=q))
+        t = t + r.sums_in[1, i]
     grad_sum, grad_dot = wide(t[0:lanes]), wide(t[lanes : 2 * lanes])
     base = first[K:R] - (usable / count) * (grad_sum + Xs[K:R] * grad_dot)
     t = z_own[0]
@@ -736,7 +811,13 @@
 
 
 def write_kernel(a, b, c, a_out, b_out, c_out, sems):
-    copies = [pltpu.make_async_copy(v, w, sems.at[i]) for i, (v, w) in enumerate(((a, a_out), (b, b_out), (c, c_out)))]
+    pieces = 4
+    n = a.shape[0] // pieces
+    copies = [pltpu.make_async_copy(c, c_out, sems.at[2 * pieces])]
+    for i in range(pieces):
+        rows = pl.ds(i * n, n)
+        copies.append(pltpu.make_async_copy(a.at[rows], a_out.at[rows], sems.at[2 * i]))
+        copies.append(pltpu.make_async_copy(b.at[rows], b_out.at[rows], sems.at[2 * i + 1]))
     for copy in copies:
         copy.start()
     for copy in copies:
@@ -787,8 +868,8 @@
         ln_gain=V(ln_gain.shape, f32),
         ln_bias=V(ln_bias.shape, f32),
         small_own=V(small, f32),
-        small=V((3, max(N, Z)) + small, f32),
-        small_sum=V((2,) + small, f32),
+        small=V((2, max(2 * N, Z)) + small, f32),
+        small_sum=V(small, f32),
         ctx_own=V((block, width), jnp.int16),
         ctx=V((Z, Y, X, block, width), jnp.int16),
         scale_own=V(sums, f32),
@@ -797,7 +878,7 @@
         prompt_blocks=V((groups, Z, Y, X) + pb, bf16),
         prompts=V((Pn * lanes, 128), f32),
         X=V((R, width), f32),
-        X1=V((R, width), f32),
+        X1=V((own, width), f32),
         qkv=V((R, 3 * width), bf16),
         qkv1=V((R, 3 * width), bf16),
         mixed=V((R, width), f32),
@@ -826,6 +907,7 @@
         ds_local=V((HEADS, own, own), bf16),
         ds_prompt=V((HEADS, Pn, Pn), bf16),
         bias=V((own, R), f32),
+        ctx_bias=V((1, K), f32),
         work=V((Z, Y, X, block, width), bf16),
         plane_in=V((Z, N, block, width), bf16),
         z_own=V((Z, block, width), f32),
@@ -837,19 +919,19 @@
         share_z=V((Z, Y, X) + pb, bf16),
         share_own=V((Y, X) + pb, f32),
         share_p=V((N,) + pb, f32),
-        sums=V((3,) + sums, f32),
-        sums_in=V((3, max(N, Z)) + sums, f32),
+        sums=V((2,) + sums, f32),
+        sums_in=V((2, max(2 * N, Z)) + sums, f32),
         load_sem=DMA((10,)),
         weight_sem=DMA((2, 4)),
     )
     for name, shape in dict(
         zsmall=(3, Z),
-        psmall=(3, N),
-        pair=(4,),
+        psmall=(3, 2 * N),
+        pair=(2,),
         zctx=(Z,),
         pctx=(Z, N),
         pctx_back=(Z, N),
-        pshare=(2, N),
+        pshare=(2, 2 * N),
         zshare=(2, Z),
         zred=(Z,),
     ).items():
@@ -871,7 +953,7 @@
         out_shape=tuple(outputs.values()),
         in_specs=[vmem] * 3,
         out_specs=(any_space,) * 3,
-        scratch_shapes=[DMA((3,))],
+        scratch_shapes=[DMA((9,))],
         name="write_results",
     )(*results)
 

time: 62.7 us -> 60.1 us (0.959)
  Pallas kernels: 61.7 us -> 59.1 us
    pallas_call x1, Pallas kernels: 59.5 us -> 56.9 us  [fused(): pl.pallas_call(functools.partial(layers_kernel, groups, seq, names), out_...]
where the time goes in v5:
time: 60.1 us; the launch traced here: 60 us
  Pallas kernels  59.1 us (98%)
  between operations  0.82 us (1%)
    pallas_call x1, Pallas kernels, fused(): pl.pallas_call(functools.partial(layers_kernel, groups, seq, names), out_...  56.9 us
    pallas_call x1, Pallas kernels, fused(): pl.pallas_call(write_kernel, out_shape=tuple(outputs.values()), in_specs=...  2.24 us

profile of v5, /device:TPU:0, one launch (start us, length us, event | category | flops | bytes accessed | tf_op | source)
XLA Modules:
  0.0 60.0 jit_solution(8928757424947141690)
XLA Ops:
  0.6 56.9 %layers.1 = (f32[256,512]{1,0:T(8,128)}, f32[256,512]{1,0:T(8,128)}, f32[4,512]{1,0:T(4,128)}) custom-call(f32[256,512]{1,0:T(8,128)} %refs_0_.1, s32[1,256]{1,0:T(1,128)} %bitcast.2, s32[1,256]{1,0:T(1,128)} %bitcast.3, bf16[4,512]{1,0:T(4,128)(2,1)} %refs_3_.1, f32[256,512]{1,0:T(8,128)} %refs_4_.1, bf16[2,512,1536]{2,1,0:T(8,128)(2,1)} %refs_5_.1, ...), custom_call_target="tpu_custom_call" | custom-call | tf_op jit(solution)/shard_map/layers/pallas_call | solution.py:940
  57.5 2.2 %write_results.1 = (f32[256,512]{1,0:T(8,128)}, f32[256,512]{1,0:T(8,128)}, f32[4,512]{1,0:T(4,128)}) custom-call(f32[256,512]{1,0:T(8,128)} %get-tuple-element.6.a, f32[256,512]{1,0:T(8,128)} %get-tuple-element.7.b, f32[4,512]{1,0:T(4,128)} %get-tuple-element.8.c), custom_call_target="tpu_custom_call" | custom-call | tf_op jit(solution)/shard_map/write_results/pallas_call | solution.py:951

commit v6 on v5

--- a/solution.py
+++ b/solution.py
@@ -235,29 +235,20 @@
             remote(src, ctx.at[z, net.y, net.x], r.pctx, (d, i), net.device(**q))
 
     small = r.small
+    for i, q in enumerate(plane):
+        dev = net.device(**q)
+        remote(r.prompt_own, prompt_blocks.at[(net.g,) + mine], r.psmall, (1, i), dev)
+        remote(r.scale_own, scales.at[mine], r.psmall, (2, i), dev)
     for i, dev in enumerate(both):
         remote(small_own, small.at[0, i], r.psmall, (0, i), dev)
     for i, q in enumerate(zs):
         remote(r.ctx_own, ctx.at[mine], r.zctx, (i,), net.device(z=q))
     spread_block(r.ctx_own, net.z, 0)
-    for i, q in enumerate(plane):
-        dev = net.device(**q)
-        remote(r.prompt_own, prompt_blocks.at[(net.g,) + mine], r.psmall, (1, i), dev)
-        remote(r.scale_own, scales.at[mine], r.psmall, (2, i), dev)
 
     def pass_on(d):
         arrived(ctx.at[levels[d], net.y, net.x], r.zctx, (d - 1,), net.device(z=levels[d]))
         spread_block(ctx.at[levels[d], net.y, net.x], levels[d], d)
 
-    pass_on(1)
-    for i, dev in enumerate(both):
-        arrived(small.at[0, i], r.psmall, (0, i), dev)
-    small_sum = r.small_sum
-    small_sum[...] = total_of([small_own[...]] + [small[0, i] for i in range(len(both))])
-    for i, q in enumerate(zs):
-        remote(small_sum, small.at[1, i], r.zsmall, (0, i), net.device(z=q))
-    for d in range(2, Z - 1):
-        pass_on(d)
     place_prompt.wait()
     place_scale.wait()
     for i, q in enumerate(plane):
@@ -268,17 +259,25 @@
         dev = net.device(z=q)
         remote(prompt_blocks.at[net.g, net.z], prompt_blocks.at[net.g, net.z], r.zsmall, (1, i), dev)
         remote(scales.at[net.z], scales.at[net.z], r.zsmall, (2, i), dev)
+    pass_on(1)
+    for i, dev in enumerate(both):
+        arrived(small.at[0, i], r.psmall, (0, i), dev)
+    small_sum = r.small_sum
+    small_sum[...] = total_of([small_own[...]] + [small[0, i] for i in range(len(both))])
+    for i, q in enumerate(zs):
+        remote(small_sum, small.at[1, i], r.zsmall, (0, i), net.device(z=q))
+    for d in range(2, Z - 1):
+        pass_on(d)
     for d in range(max(Z - 1, 2), Z):
         pass_on(d)
+    for i, q in enumerate(zs):
+        arrived(prompt_blocks.at[net.g, q], r.zsmall, (1, i), net.device(z=q))
+    remote(prompt_blocks.at[net.g], prompt_blocks.at[net.g], r.pair, (1,), sibling)
     query = column(jnp.where(kind == 2, -2, seg))
     own_key = jnp.where((kind == 0) & (seg != middle), seg, -1)
     bias = r.bias
     bias[:, 0:Pn] = jnp.zeros((own, Pn), f32)
     bias[:, K:R] = jnp.where(query == own_key, 0.0, masked_score)
-    for i, q in enumerate(zs):
-        arrived(prompt_blocks.at[net.g, q], r.zsmall, (1, i), net.device(z=q))
-    remote(prompt_blocks.at[net.g], prompt_blocks.at[net.g], r.pair, (1,), sibling)
-
     for i, q in enumerate(zs):
         arrived(small.at[1, i], r.zsmall, (0, i), net.device(z=q))
     total = total_of([small_sum[...]] + [small[1, i] for i in range(len(zs))])
@@ -325,7 +324,8 @@
         present = jnp.concatenate(flags, axis=0)
         ctx_bias[:, at] = jnp.max(jnp.where(square & present, 0.0, masked_score), axis=0, keepdims=True)
 
-    take_level(0)
+    for d in range(max(Z - 1, 1)):
+        take_level(d)
 
     arrived(prompt_blocks.at[1 - net.g], r.pair, (1,), sibling)
     prompts = r.prompts
@@ -501,9 +501,6 @@
         rows = slice(0, Pn)
         return forward_job(h, qkv, rows, rows, (0, Pn), lambda raw: weights_of(raw, None), store, mixed, inv)
 
-    for d in range(1, Z - 1):
-        take_level(d)
-    pipeline([prompt_job(h) for h in range(HEADS)])
     for d in range(max(Z - 1, 1), Z):
         take_level(d)
     reach = jnp.where(query == middle, 0.0, masked_score)
@@ -564,7 +561,8 @@
         ready = [ctx_job(h, at, part) for h in range(HEADS)]
         jobs += ready + waiting
         waiting = tails(Pn + at, Pn + at + part, ready)
-    pipeline(jobs + waiting + tails(0, Pn, ()))
+    ready = [prompt_job(h) for h in range(HEADS)]
+    pipeline(jobs + ready + waiting + tails(0, Pn, ready))
 
     whole = slice(0, own)
     for c in weights[1][1:]:

time: 60.1 us -> 59.4 us (0.988)
  Pallas kernels: 59.1 us -> 58.4 us
    pallas_call x1, Pallas kernels: 56.9 us -> 56.2 us  [fused(): pl.pallas_call(functools.partial(layers_kernel, groups, seq, names), out_...]
where the time goes in v6:
time: 59.4 us; the launch traced here: 59.2 us
  Pallas kernels  58.4 us (98%)
  between operations  0.82 us (1%)
    pallas_call x1, Pallas kernels, fused(): pl.pallas_call(functools.partial(layers_kernel, groups, seq, names), out_...  56.2 us
    pallas_call x1, Pallas kernels, fused(): pl.pallas_call(write_kernel, out_shape=tuple(outputs.values()), in_specs=...  2.24 us

profile of v6, /device:TPU:0, one launch (start us, length us, event | category | flops | bytes accessed | tf_op | source)
XLA Modules:
  0.0 59.2 jit_solution(9721492050083882659)
XLA Ops:
  0.6 56.2 %layers.1 = (f32[256,512]{1,0:T(8,128)}, f32[256,512]{1,0:T(8,128)}, f32[4,512]{1,0:T(4,128)}) custom-call(f32[256,512]{1,0:T(8,128)} %refs_0_.1, s32[1,256]{1,0:T(1,128)} %bitcast.2, s32[1,256]{1,0:T(1,128)} %bitcast.3, bf16[4,512]{1,0:T(4,128)(2,1)} %refs_3_.1, f32[256,512]{1,0:T(8,128)} %refs_4_.1, bf16[2,512,1536]{2,1,0:T(8,128)(2,1)} %refs_5_.1, ...), custom_call_target="tpu_custom_call" | custom-call | tf_op jit(solution)/shard_map/layers/pallas_call | solution.py:938
  56.8 2.2 %write_results.1 = (f32[256,512]{1,0:T(8,128)}, f32[256,512]{1,0:T(8,128)}, f32[4,512]{1,0:T(4,128)}) custom-call(f32[256,512]{1,0:T(8,128)} %get-tuple-element.6.a, f32[256,512]{1,0:T(8,128)} %get-tuple-element.7.b, f32[4,512]{1,0:T(4,128)} %get-tuple-element.8.c), custom_call_target="tpu_custom_call" | custom-call | tf_op jit(solution)/shard_map/write_results/pallas_call | solution.py:949
